TPU v7x, 32 devices: a whole 2x2x4 slice. The times are simulated.
32 devices in a mesh: row: 8 (over z, y), col: 4 (over x, core).
Axes of the slice: x: 2, y: 2, z: 4, core: 2. Of those that a mesh axis runs over, the one named last changes fastest.
Arguments:
- block_cols: int32 [32, 8], replicated, may hold values from -1 to 31, as said below
- step_dir: bfloat16 [32, 8, 128, 128], P('row', 'col')
- intersection: bfloat16 [32, 8, 128, 128], P('row', 'col')
- density: bfloat16 [32, 8, 128, 128], P('row', 'col')
- kohn_sham: bfloat16 [32, 8, 128, 128], P('row', 'col')
Outputs:
- commutator: bfloat16 [32, 8, 128, 128], P('row', 'col')
- trace_value: float32 [], replicated
Inputs may be any that keep to these rules, and one draw needn't show every extreme that they name: block_cols[i, s] is -1 or a block column of group s // 2, that is from (s // 2) * 8 to (s // 2 + 1) * 8 - 1; the live entries of one block row within one group are distinct; the pattern is symmetric (j is live in row i exactly when i is live in row j) and holds every diagonal block.
All inputs are finite; a program needn't handle non-finite values.
Results may differ from a plain program's by a relative error of at most 0.0057.
Values may be sent and summed in bfloat16 or wider, within the bound.
No kernel may reach another device: no remote copies, remote signals or barrier semaphores. Data moves between devices by JAX's collectives and lax.ppermute only.
A program may use at most 64 MiB of HBM per device.

v0:
```python
import functools

import jax
import jax.numpy as jnp
from jax import lax
from jax.experimental import pallas as pl
from jax.experimental.pallas import tpu as pltpu
from jax.sharding import PartitionSpec as P

CORES = 2


def row_major_perm(n_row, n_col, target):
    pairs = []
    for r in range(n_row):
        for c in range(n_col):
            to_r, to_c = target(r, c)
            pairs.append((r * n_col + c, to_r * n_col + to_c))
    return pairs


def start_copies(pairs, sems):
    copies = [pltpu.make_async_copy(*pair, sems.at[i]) for i, pair in enumerate(pairs)]
    for copy in copies:
        copy.start()
    return copies


def wait_for(copies):
    for copy in copies:
        copy.wait()


def into(pieces, scratch, count):
    scratch[len(pieces) * count] = jnp.zeros(scratch.shape[1:], scratch.dtype)
    return [
        (piece, scratch.at[pl.ds(index * count, count)]) for index, piece in enumerate(pieces)
    ]


def multiply(index_ref, index_at, left_of, right, results, outs, sems, rows, slots, contract):
    copies = []
    for d in range(len(outs) - 1, -1, -1):
        for i in range(rows):
            left = left_of(i)
            for s in range(slots):
                base = index_at + ((d * rows + i) * slots + s) * slots
                blocks = jnp.concatenate(
                    [right[index_ref[base + a]] for a in range(slots)], axis=1
                )
                value = lax.dot_general(
                    blocks,
                    left,
                    (((1,), (contract,)), ((), ())),
                    preferred_element_type=jnp.float32,
                ).astype(results[d].dtype)
                if len(results[d].shape) == 3:
                    results[d][i * slots + s] = value
                else:
                    side = value.shape[0]
                    results[d][pl.ds((i * slots + s) * side, side)] = value
        copy = pltpu.make_async_copy(results[d], outs[d], sems.at[d])
        copy.start()
        copies.append(copy)
    wait_for(copies)


def split_results(first, others):
    return [first] + [others.at[d] for d in range(others.shape[0])]


def first_kernel(rows, slots, n_pieces, n_early, index_at, index_ref, left_ref, *refs):
    pieces, outs = refs[:n_pieces], refs[n_pieces + n_early : -6]
    right, left, first, others, sems, out_sems = refs[-6:]
    wait_for(start_copies(into(pieces, right, rows * slots) + [(left_ref, left)], sems))

    def left_of(i):
        return jnp.concatenate([left[i * slots + a] for a in range(slots)], axis=1)

    results = split_results(first, others)
    multiply(index_ref, index_at, left_of, right, results, outs, out_sems, rows, slots, 1)


def second_kernel(rows, slots, n_pieces, n_out, n_early, index_at, index_ref, *refs):
    pieces, parts = refs[:n_pieces], refs[n_pieces : n_pieces + n_out]
    right, left, part_first, part_others, first, others, sems, out_sems = refs[-8:]
    outs = refs[n_pieces + n_out + n_early : -8]
    held = split_results(part_first, part_others)
    wait_for(start_copies(list(zip(parts, held)) + into(pieces, right, rows * slots), sems))
    for b in range(rows * slots):
        value = held[0][b]
        for part in held[1:]:
            value = value + part[b].astype(jnp.float32)
        left[b] = value.astype(jnp.bfloat16)

    def left_of(i):
        return jnp.concatenate([left[i * slots + a] for a in range(slots)], axis=0)

    results = split_results(first, others)
    multiply(index_ref, index_at, left_of, right, results, outs, out_sems, rows, slots, 0)


def two_parts(x):
    high = x.astype(jnp.bfloat16)
    low = (x - high.astype(jnp.float32)).astype(jnp.bfloat16)
    return jnp.concatenate([high, low], axis=0)


def one_part(x):
    x = x.astype(jnp.float32)
    half = x.shape[0] // 2
    return x[:half] + x[half:]


def tree_sum(values):
    while len(values) > 1:
        values = [values[i] + values[i + 1] for i in range(0, len(values), 2)]
    return values[0]


def third_kernel(rows, slots, n_pieces, n_mirror, index_at, mirror_at, index_ref, own_ref, *refs):
    pieces, mirrored = refs[:n_pieces], refs[n_pieces : n_pieces + n_mirror]
    *outs, trace = refs[n_pieces + n_mirror : -8]
    right, mirror, own, left, first, others, sems, out_sems = refs[-8:]
    pairs = into(pieces, right, rows * slots) + into(mirrored, mirror, rows * slots) + [(own_ref, own)]
    wait_for(start_copies(pairs, sems))
    blocks, side = rows * slots, right.shape[1]
    part_rows = trace.shape[0] // 2
    total_trace = jnp.zeros((part_rows, side), jnp.float32)
    for b in range(blocks):
        other = mirror[index_ref[mirror_at + b]].astype(jnp.float32).T
        value = (-(own[b].astype(jnp.float32) + other)).astype(jnp.bfloat16)
        left[b] = value
        product = value.astype(jnp.float32) * right[b].astype(jnp.float32).T
        total_trace = total_trace + product.reshape(-1, part_rows, side).sum(0)
    total_trace = two_parts(total_trace)
    trace[...] = total_trace
    results = split_results(first, others)
    for result in results[1:]:
        result[pl.ds(blocks * side, 2 * part_rows)] = total_trace

    def left_of(i):
        return jnp.concatenate([left[i * slots + a] for a in range(slots)], axis=0)

    multiply(index_ref, index_at, left_of, right, results, outs, out_sems, rows, slots, 0)


def sum_kernel(n_out, trace_ref, own_ref, *refs):
    parts, (out, own, others, result, sems, out_sems) = refs[: n_out - 1], refs[n_out - 1 :]
    pairs = [(part, others.at[d]) for d, part in enumerate(parts)]
    wait_for(start_copies([(own_ref, own)] + pairs, sems))
    blocks, side = own.shape[:2]
    for b in range(blocks):
        value = own[b]
        for d in range(n_out - 1):
            value = value + others[d, pl.ds(b * side, side)].astype(jnp.float32)
        result[pl.ds(b * side, side)] = value.astype(result.dtype)
    tail = pl.ds(blocks * side, trace_ref.shape[0])
    tiles = [trace_ref[...]] + [others[d, tail] for d in range(n_out - 1)]
    result[tail] = two_parts(tree_sum([one_part(tile) for tile in tiles]))
    wait_for(start_copies([(result, out)], out_sems))


def last_kernel(n_mirror, blocks, mirror_at, index_ref, own_ref, *refs):
    mirrored, (out, mirror, own, result, sems, out_sems) = refs[:n_mirror], refs[n_mirror:]
    side = own.shape[1]
    count = blocks * side
    body = pl.ds(0, count)
    pairs = [(own_ref.at[body], own)] + [
        (piece.at[body], mirror.at[pl.ds(t * count, count)]) for t, piece in enumerate(mirrored)
    ]
    copies = start_copies(pairs, sems)
    mirror[pl.ds(n_mirror * count, side)] = jnp.zeros((side, side), mirror.dtype)
    wait_for(copies)
    for b in range(blocks):
        start = pl.multiple_of(index_ref[mirror_at + b] * side, side)
        other = mirror[pl.ds(start, side)].astype(jnp.float32)
        value = other - own[pl.ds(b * side, side)].astype(jnp.float32).T
        result[b] = value.astype(result.dtype)
    wait_for(start_copies([(result, out)], out_sems))


def per_device(n_row, n_col, block_cols, step_dir, intersection, density, kohn_sham):
    rows, slots, side = step_dir.shape[:3]
    blocks = rows * slots
    blocks_total = block_cols.shape[0]
    inner = n_row // n_col
    outer = n_row // inner
    assert inner == CORES and outer == n_col and outer & (outer - 1) == 0
    row_index = lax.axis_index("row")
    col_index = lax.axis_index("col")
    bf16, f32 = jnp.bfloat16, jnp.float32

    def at(o, h, g):
        return o * inner + g % inner, (g // inner) * CORES + h

    def inside(r, c):
        return r // inner, c % CORES, (c // CORES) * inner + r % inner

    def spread(o, g):
        bits = (n_col - 1).bit_length()
        return g ^ sum(((o >> b) & 1) << (bits - 1 - b) for b in range(bits))

    def at_spread(o, h, g):
        return at(o, h, spread(o, g))

    def inside_spread(r, c):
        o, h, p = inside(r, c)
        return o, h, spread(o, p)

    o_in, h_in, g_in = inside(row_index, col_index)

    by_group = block_cols.reshape(blocks_total, n_col, slots)
    mirror_cols = lax.dynamic_slice_in_dim(by_group, o_in, 1, 1)[:, 0]

    def rows_of(o, h):
        return lax.dynamic_slice_in_dim(by_group, (o * inner + h) * rows, rows, 0)

    def group_cols_of(cols, g):
        return lax.dynamic_slice_in_dim(cols, g, 1, 1)[:, 0]

    own_rows = rows_of(o_in, h_in)

    def index_table(group, first_out):
        own_cols, group_cols = group_cols_of(own_rows, group), group_cols_of(by_group, group)
        wanted = own_rows[:, first_out ^ jnp.arange(n_col)].transpose(1, 0, 2)
        safe = jnp.clip(wanted, 0, blocks_total - 1)
        matched = (
            (group_cols[safe][..., None, :] == own_cols[None, :, None, :, None])
            & (wanted >= 0)[..., None, None]
            & (own_cols >= 0)[None, :, None, :, None]
        )
        piece = ((safe // rows % inner) ^ h_in) * outer + (safe // rows // inner ^ o_in)
        slot = ((piece * rows + safe % rows) * slots)[..., None] + jnp.argmax(matched, axis=-1)
        return jnp.where(matched.any(-1), slot, n_row * blocks).astype(jnp.int32).reshape(-1)

    spread_in = spread(o_in, g_in)
    all_tables = [index_table(g_in, g_in), index_table(g_in, spread_in)]

    def mirror_table(h, cols):
        own_ids = (o_in * inner + h) * rows + jnp.arange(rows)
        safe_own = jnp.clip(cols, 0, blocks_total - 1)
        found = mirror_cols[safe_own] == own_ids[:, None, None]
        source = (safe_own // rows % inner) ^ h
        return jnp.where(
            cols >= 0,
            (source * rows + safe_own % rows) * slots + jnp.argmax(found, axis=-1),
            inner * blocks,
        ).astype(jnp.int32).reshape(-1)

    all_tables += [mirror_table(h_in, group_cols_of(own_rows, g)) for g in (g_in, spread_in)]
    starts = [sum(table.size for table in all_tables[:t]) for t in range(len(all_tables))]
    first_at, later_at, mirror_at, last_mirror_at = starts
    tables = jnp.concatenate(all_tables)

    smem = pl.BlockSpec(memory_space=pltpu.SMEM)
    vmem = pl.BlockSpec(memory_space=pltpu.VMEM)
    anywhere = pl.BlockSpec(memory_space=pl.ANY)

    def permute(x, target):
        return lax.ppermute(x, ("row", "col"), row_major_perm(n_row, n_col, target))

    def relayout(x, m=0, target=at):
        return permute(x, lambda r, c: target((r // inner) ^ m, r % inner, c))

    def inside_permute(x, move, source=inside, target=at):
        return permute(x, lambda r, c: target(*move(*source(r, c))))

    def share(x):
        return inside_permute(x, lambda o, h, g: (o, h ^ 1, g))

    def after(x, done):
        return lax.optimization_barrier((x, done))[0]

    def to_plane(x, m):
        return inside_permute(x, lambda o, h, g: (o ^ m, h, g))

    def share_all(pieces):
        return {m: share(piece) for m, piece in pieces.items()}

    def listed(pieces, shared):
        return [pieces[m] for m in range(outer)] + [shared[m] for m in range(outer)]

    def mirror(x, target):
        moved = inside_permute(x, lambda o, h, g: (g, h, o), inside_spread, target)
        return [moved, share(moved)]

    def exchange(outs):
        return [outs[0]] + [
            inside_permute(out, lambda o, h, g, d=d: (o, h, g ^ d))
            for d, out in enumerate(outs)
            if d
        ]

    def total_of(parts):
        value = parts[0]
        for part in parts[1:]:
            value = value + part.astype(f32)
        return value.astype(bf16)

    block_shape = (blocks, side, side)
    out_shapes = tuple(
        jax.ShapeDtypeStruct(block_shape, bf16 if d else f32) for d in range(n_col)
    )
    params = pltpu.CompilerParams(vmem_limit_bytes=14 * 2**20)

    def held(count):
        return pltpu.VMEM((count, side, side), bf16)

    def dma(count):
        return pltpu.SemaphoreType.DMA((count,))

    tail_shape = jax.ShapeDtypeStruct((16, side), bf16)
    long_shape = jax.ShapeDtypeStruct((blocks * side + tail_shape.shape[0], side), bf16)
    long_sums = [
        pltpu.VMEM(block_shape, f32),
        pltpu.VMEM((n_col - 1,) + long_shape.shape, bf16),
    ]
    sums = [pltpu.VMEM(block_shape, f32), pltpu.VMEM((n_col - 1,) + block_shape, bf16)]
    cost = pl.CostEstimate(
        flops=2 * n_col * blocks * slots * side**3,
        bytes_accessed=4 * 2**20,
        transcendentals=0,
    )

    flat = lambda x: x.reshape(block_shape)
    inter, dens, kohn = flat(intersection), flat(density), flat(kohn_sham)

    far_from = range(2, outer, 2)
    near = [*far_from, 1]

    inter_near = {m: relayout(inter, m) for m in near}
    inter_early = {0: relayout(inter)} | inter_near
    step = relayout(flat(step_dir))
    dens_own = relayout(dens)
    inter_far = {m + 1: to_plane(inter_near[m], 1) for m in far_from}
    dens_behind = after(dens_own, inter_near)
    dens_near = {m: to_plane(dens_behind, m) for m in far_from}
    dens_behind, kohn = after((dens_own, kohn), (inter_near, inter_far))
    dens_near[1] = to_plane(dens_behind, 1)
    kohn_own = relayout(kohn)
    inter_all = listed(inter_early | inter_far, share_all(inter_early) | share_all(inter_far))
    outs = pl.pallas_call(
        functools.partial(first_kernel, rows, slots, n_row, 1, first_at),
        out_shape=out_shapes,
        in_specs=[smem] + [anywhere] * (1 + n_row + 1),
        out_specs=(anywhere,) * n_col,
        scratch_shapes=[held(n_row * blocks + 1), held(blocks), *sums, dma(n_row + 1), dma(n_col)],
        compiler_params=params,
        cost_estimate=cost,
        name="scaled_step_product",
    )(tables, step, *inter_all, kohn_own)
    parts = exchange(outs)

    dens_beside = {0: share(dens_own)}
    dens_far = {m + 1: to_plane(after(dens_near[m], outs), 1) for m in far_from}
    kohn_behind = after(kohn_own, (dens_near, outs))
    kohn_pieces = {m: to_plane(kohn_behind, m) for m in far_from}
    kohn_early = list(kohn_pieces.values())
    dens_near, dens_far = after((dens_near, dens_far), parts[1:])
    dens_beside |= share_all(dens_near) | share_all(dens_far)
    dens_all = listed({0: dens_own} | dens_near | dens_far, dens_beside)
    outs = pl.pallas_call(
        functools.partial(second_kernel, rows, slots, n_row, n_col, len(kohn_early), later_at),
        out_shape=out_shapes,
        in_specs=[smem] + [anywhere] * (n_row + n_col + len(kohn_early)),
        out_specs=(anywhere,) * n_col,
        scratch_shapes=[
            held(n_row * blocks + 1),
            held(blocks),
            *sums,
            *sums,
            dma(n_row + n_col),
            dma(n_col),
        ],
        compiler_params=params,
        cost_estimate=cost,
        name="change_product",
    )(tables, *dens_all, *parts, *kohn_early)
    second_outs = outs
    total = total_of(exchange(outs))

    mirrored = mirror(total, at)
    own = inside_permute(total, lambda o, h, g: (o, h, g), inside_spread)
    kohn_pieces = {0: kohn_own} | after(kohn_pieces, second_outs)
    kohn_beside = share_all(kohn_pieces)
    kohn_last = {m + 1: to_plane(kohn_pieces[m], 1) for m in range(0, outer, 2)}
    kohn_last = after(kohn_last, total)
    kohn_all = listed(kohn_pieces | kohn_last, kohn_beside | share_all(kohn_last))
    *outs, trace = pl.pallas_call(
        functools.partial(third_kernel, rows, slots, n_row, inner, later_at, mirror_at),
        out_shape=out_shapes[:1] + (long_shape,) * (n_col - 1) + (tail_shape,),
        in_specs=[smem] + [anywhere] * (1 + n_row + inner),
        out_specs=(anywhere,) * n_col + (vmem,),
        scratch_shapes=[
            held(n_row * blocks + 1),
            held(inner * blocks + 1),
            held(blocks),
            held(blocks),
            *long_sums,
            dma(n_row + inner + 1),
            dma(n_col),
        ],
        compiler_params=params,
        cost_estimate=cost,
        name="commutator_product",
    )(tables, own, *kohn_all, *mirrored)
    own, *parts = exchange(outs)
    total = pl.pallas_call(
        functools.partial(sum_kernel, n_col),
        out_shape=long_shape,
        in_specs=[vmem] + [anywhere] * n_col,
        out_specs=anywhere,
        scratch_shapes=[*long_sums, pltpu.VMEM(long_shape.shape, bf16), dma(n_col), dma(1)],
        compiler_params=params,
        name="plane_sum",
    )(trace, own, *parts)
    mirrored = mirror(total, at_spread)

    commutator = pl.pallas_call(
        functools.partial(last_kernel, inner, blocks, last_mirror_at),
        out_shape=jax.ShapeDtypeStruct(block_shape, bf16),
        in_specs=[smem] + [anywhere] * (1 + inner),
        out_specs=anywhere,
        scratch_shapes=[
            pltpu.VMEM(((inner * blocks + 1) * side, side), bf16),
            pltpu.VMEM((blocks * side, side), bf16),
            held(blocks),
            dma(inner + 1),
            dma(1),
        ],
        compiler_params=params,
        name="commutator_difference",
    )(tables, total, *mirrored)
    commutator = inside_permute(
        commutator, lambda o, h, g: (o, h, g), inside_spread, lambda o, h, g: (o * inner + h, g)
    )

    plane_trace = tree_sum([one_part(piece[blocks * side :]) for piece in mirrored])
    trace = tree_sum(
        [plane_trace]
        + [
            inside_permute(plane_trace, lambda o, h, g, d=d: (o, h, g ^ d))
            for d in range(1, n_col)
        ]
    )
    trace_value = trace.sum() / (blocks_total * side * side)
    return commutator.reshape(step_dir.shape), trace_value


def solution(mesh):
    in_specs = (P(),) + (P("row", "col", None, None),) * 4
    out_specs = (P("row", "col", None, None), P())
    return jax.shard_map(
        functools.partial(per_device, mesh.shape["row"], mesh.shape["col"]),
        mesh=mesh,
        in_specs=in_specs,
        out_specs=out_specs,
        check_vma=False,
    )
```

profile of v0, /device:TPU:26, one launch (start us, length us, event | category | flops | bytes accessed | tf_op | source)
XLA Modules:
  0.0 141.1 jit_solution(17401531418448613540)
XLA Ops:
  13.6 2.9 %collective-permute-done.2.refs_2_ = bf16[8,128,128]{2,1,0:T(8,128)(2,1)S(1)} collective-permute-done((bf16[8,128,128]{2,1,0:T(8,128)(2,1)}, bf16[8,128,128]{2,1,0:T(8,128)(2,1)S(1)}, u32[]{:S(2)}, u32[]{:S(2)}) %collective-permute-start.2) | collective-permute-done | bytes 262176 | tf_op jit(solution)/shard_map/ppermute | solution.py:261
  16.5 3.5 %collective-permute-start.10 = (bf16[8,128,128]{2,1,0:T(8,128)(2,1)S(1)}, bf16[8,128,128]{2,1,0:T(8,128)(2,1)S(1)}, u32[]{:S(2)}, u32[]{:S(2)}) collective-permute-start(bf16[8,128,128]{2,1,0:T(8,128)(2,1)S(1)} %collective-permute-done.2.refs_2_), channel_id=1, source_target_pairs={{0,1},{1,0},{2,3},{3,2},{4,5},{5,4},{6,7},{7,6},{8,9},{9,8},{10,11... | collective-permute-start | bytes 786440 | tf_op jit(solution)/shard_map/ppermute | solution.py:261
  21.9 2.6 %collective-permute-start.5 = (bf16[8,128,128]{2,1,0:T(8,128)(2,1)S(1)}, bf16[8,128,128]{2,1,0:T(8,128)(2,1)S(1)}, u32[]{:S(2)}, u32[]{:S(2)}) collective-permute-start(bf16[8,128,128]{2,1,0:T(8,128)(2,1)S(1)} %collective-permute-done.refs_0_), channel_id=1, source_target_pairs={{0,16},{1,17},{2,18},{3,19},{4,20},{5,21},{6,22},{7,23},{8,24},{9,... | collective-permute-start | bytes 786440 | tf_op jit(solution)/shard_map/ppermute | solution.py:261
  29.5 2.2 %scaled_step_product.1 = (f32[8,128,128]{2,1,0:T(8,128)S(1)}, bf16[8,128,128]{2,1,0:T(8,128)(2,1)S(1)}, bf16[8,128,128]{2,1,0:T(8,128)(2,1)S(1)}, bf16[8,128,128]{2,1,0:T(8,128)(2,1)S(1)}) custom-call(s32[144]{0:T(256)S(1)} %pad_add_fusion.index_ref, bf16[8,128,128]{2,1,0:T(8,128)(2,1)S(1)} %collective-permute-done.6.left_ref, ...), custom_call_target="tpu_custom_call" | custom-call | flops 268435456 | bytes 4194304 | tf_op jit(solution)/shard_map/scaled_step_product/pallas_call | solution.py:343
  31.6 5.1 %collective-permute-done.5.refs_2_ = bf16[8,128,128]{2,1,0:T(8,128)(2,1)S(1)} collective-permute-done((bf16[8,128,128]{2,1,0:T(8,128)(2,1)S(1)}, bf16[8,128,128]{2,1,0:T(8,128)(2,1)S(1)}, u32[]{:S(2)}, u32[]{:S(2)}) %collective-permute-start.5) | collective-permute-done | bytes 262176 | tf_op jit(solution)/shard_map/ppermute | solution.py:261
  42.4 5.1 %collective-permute-done.13.refs_3_ = bf16[8,128,128]{2,1,0:T(8,128)(2,1)S(1)} collective-permute-done((bf16[8,128,128]{2,1,0:T(8,128)(2,1)S(1)}, bf16[8,128,128]{2,1,0:T(8,128)(2,1)S(1)}, u32[]{:S(2)}, u32[]{:S(2)}) %collective-permute-start.13) | collective-permute-done | bytes 262176 | tf_op jit(solution)/shard_map/ppermute | solution.py:261
  47.6 3.9 %collective-permute-done.16.refs_11_ = bf16[8,128,128]{2,1,0:T(8,128)(2,1)S(1)} collective-permute-done((bf16[8,128,128]{2,1,0:T(8,128)(2,1)S(1)}, bf16[8,128,128]{2,1,0:T(8,128)(2,1)S(1)}, u32[]{:S(2)}, u32[]{:S(2)}) %collective-permute-start.16) | collective-permute-done | bytes 262176 | tf_op jit(solution)/shard_map/ppermute | solution.py:261
  52.1 9.1 %collective-permute-done.21.refs_12_.refs_2_ = bf16[8,128,128]{2,1,0:T(8,128)(2,1)S(1)} collective-permute-done((bf16[8,128,128]{2,1,0:T(8,128)(2,1)S(1)}, bf16[8,128,128]{2,1,0:T(8,128)(2,1)S(1)}, u32[]{:S(2)}, u32[]{:S(2)}) %collective-permute-start.21) | collective-permute-done | bytes 262176 | tf_op jit(solution)/shard_map/ppermute | solution.py:261
  61.2 2.3 %change_product.1 = (f32[8,128,128]{2,1,0:T(8,128)S(1)}, bf16[8,128,128]{2,1,0:T(8,128)(2,1)S(1)}, bf16[8,128,128]{2,1,0:T(8,128)(2,1)S(1)}, bf16[8,128,128]{2,1,0:T(8,128)(2,1)S(1)}) custom-call(s32[144]{0:T(256)S(1)} %pad_add_fusion.index_ref, bf16[8,128,128]{2,1,0:T(8,128)(2,1)S(1)} %collective-permute-done.refs_0_, ...), custom_call_target="tpu_custom_call" | custom-call | flops 268435456 | bytes 4194304 | tf_op jit(solution)/shard_map/change_product/pallas_call | solution.py:363
  67.0 4.8 %collective-permute-done.22 = bf16[8,128,128]{2,1,0:T(8,128)(2,1)S(1)} collective-permute-done((bf16[8,128,128]{2,1,0:T(8,128)(2,1)S(1)}, bf16[8,128,128]{2,1,0:T(8,128)(2,1)S(1)}, u32[]{:S(2)}, u32[]{:S(2)}) %collective-permute-start.22) | collective-permute-done | bytes 262176 | tf_op jit(solution)/shard_map/ppermute | solution.py:261
  71.8 2.4 %collective-permute-done.23 = bf16[8,128,128]{2,1,0:T(8,128)(2,1)S(1)} collective-permute-done((bf16[8,128,128]{2,1,0:T(8,128)(2,1)S(1)}, bf16[8,128,128]{2,1,0:T(8,128)(2,1)S(1)}, u32[]{:S(2)}, u32[]{:S(2)}) %collective-permute-start.23) | collective-permute-done | bytes 262176 | tf_op jit(solution)/shard_map/ppermute | solution.py:261
  74.2 4.3 %collective-permute-done.24 = bf16[8,128,128]{2,1,0:T(8,128)(2,1)S(1)} collective-permute-done((bf16[8,128,128]{2,1,0:T(8,128)(2,1)S(1)}, bf16[8,128,128]{2,1,0:T(8,128)(2,1)S(1)}, u32[]{:S(2)}, u32[]{:S(2)}) %collective-permute-start.24) | collective-permute-done | bytes 262176 | tf_op jit(solution)/shard_map/ppermute | solution.py:261
  78.6 2.4 %collective-permute-start.32 = (bf16[8,128,128]{2,1,0:T(8,128)(2,1)S(1)}, bf16[8,128,128]{2,1,0:T(8,128)(2,1)S(1)}, u32[]{:S(2)}, u32[]{:S(2)}) collective-permute-start(bf16[8,128,128]{2,1,0:T(8,128)(2,1)S(1)} %add_convert_fusion), channel_id=1, source_target_pairs={{0,0},{1,1},{2,16},{3,17},{4,8},{5,9},{6,24},{7,25},{8,20},{9,21},... | collective-permute-start | bytes 786440 | tf_op jit(solution)/shard_map/ppermute | solution.py:261
  81.1 3.2 %collective-permute-start.25 = (bf16[8,128,128]{2,1,0:T(8,128)(2,1)S(1)}, bf16[8,128,128]{2,1,0:T(8,128)(2,1)S(1)}, u32[]{:S(2)}, u32[]{:S(2)}) collective-permute-start(bf16[8,128,128]{2,1,0:T(8,128)(2,1)S(1)} %add_convert_fusion), channel_id=1, source_target_pairs={{0,0},{1,1},{2,2},{3,3},{4,4},{5,5},{6,6},{7,7},{8,10},{9,11},{10,... | collective-permute-start | bytes 786440 | tf_op jit(solution)/shard_map/ppermute | solution.py:261
  84.9 2.7 %collective-permute-done.32.refs_8_ = bf16[8,128,128]{2,1,0:T(8,128)(2,1)S(1)} collective-permute-done((bf16[8,128,128]{2,1,0:T(8,128)(2,1)S(1)}, bf16[8,128,128]{2,1,0:T(8,128)(2,1)S(1)}, u32[]{:S(2)}, u32[]{:S(2)}) %collective-permute-start.32) | collective-permute-done | bytes 262176 | tf_op jit(solution)/shard_map/ppermute | solution.py:261
  87.6 5.0 %collective-permute-done.25.own_ref = bf16[8,128,128]{2,1,0:T(8,128)(2,1)S(1)} collective-permute-done((bf16[8,128,128]{2,1,0:T(8,128)(2,1)S(1)}, bf16[8,128,128]{2,1,0:T(8,128)(2,1)S(1)}, u32[]{:S(2)}, u32[]{:S(2)}) %collective-permute-start.25) | collective-permute-done | bytes 262176 | tf_op jit(solution)/shard_map/ppermute | solution.py:261
  92.6 2.3 %commutator_product.1 = (f32[8,128,128]{2,1,0:T(8,128)S(1)}, bf16[1040,128]{1,0:T(8,128)(2,1)S(1)}, bf16[1040,128]{1,0:T(8,128)(2,1)S(1)}, bf16[1040,128]{1,0:T(8,128)(2,1)S(1)}, bf16[16,128]{1,0:T(8,128)(2,1)S(1)}) custom-call(s32[144]{0:T(256)S(1)} %pad_add_fusion.index_ref, bf16[8,128,128]{2,1,0:T(8,128)(2,1)S(1)} %collective-permute-done.25.own_ref, ...), custom_call_target="tpu_custom_call" | custom-call | flops 268435456 | bytes 4194304 | tf_op jit(solution)/shard_map/commutator_product/pallas_call | solution.py:390
  94.9 3.3 %collective-permute-start.34 = (bf16[1040,128]{1,0:T(8,128)(2,1)S(1)}, bf16[1040,128]{1,0:T(8,128)(2,1)S(1)}, u32[]{:S(2)}, u32[]{:S(2)}) collective-permute-start(bf16[1040,128]{1,0:T(8,128)(2,1)S(1)} %get-tuple-element.55), channel_id=1, source_target_pairs={{0,4},{1,5},{2,6},{3,7},{4,0},{5,1},{6,2},{7,3},{8,12},{9,13},{10,... | collective-permute-start | bytes 798728 | tf_op jit(solution)/shard_map/ppermute | solution.py:261
  101.2 3.2 %collective-permute-done.34.refs_0_ = bf16[1040,128]{1,0:T(8,128)(2,1)S(1)} collective-permute-done((bf16[1040,128]{1,0:T(8,128)(2,1)S(1)}, bf16[1040,128]{1,0:T(8,128)(2,1)S(1)}, u32[]{:S(2)}, u32[]{:S(2)}) %collective-permute-start.34) | collective-permute-done | bytes 266272 | tf_op jit(solution)/shard_map/ppermute | solution.py:261
  104.4 3.0 %collective-permute-done.35.refs_1_ = bf16[1040,128]{1,0:T(8,128)(2,1)S(1)} collective-permute-done((bf16[1040,128]{1,0:T(8,128)(2,1)S(1)}, bf16[1040,128]{1,0:T(8,128)(2,1)S(1)}, u32[]{:S(2)}, u32[]{:S(2)}) %collective-permute-start.35) | collective-permute-done | bytes 266272 | tf_op jit(solution)/shard_map/ppermute | solution.py:261
  107.4 5.8 %collective-permute-done.36.refs_2_ = bf16[1040,128]{1,0:T(8,128)(2,1)S(1)} collective-permute-done((bf16[1040,128]{1,0:T(8,128)(2,1)S(1)}, bf16[1040,128]{1,0:T(8,128)(2,1)S(1)}, u32[]{:S(2)}, u32[]{:S(2)}) %collective-permute-start.36) | collective-permute-done | bytes 266272 | tf_op jit(solution)/shard_map/ppermute | solution.py:261
  115.4 10.2 %collective-permute-done.37.refs_0_ = bf16[1040,128]{1,0:T(8,128)(2,1)S(1)} collective-permute-done((bf16[1040,128]{1,0:T(8,128)(2,1)S(1)}, bf16[1040,128]{1,0:T(8,128)(2,1)S(1)}, u32[]{:S(2)}, u32[]{:S(2)}) %collective-permute-start.37) | collective-permute-done | bytes 266272 | tf_op jit(solution)/shard_map/ppermute | solution.py:261
  130.0 3.5 %collective-permute-start.41 = (f32[8,128]{1,0:T(8,128)S(1)}, f32[8,128]{1,0:T(8,128)S(1)}, u32[]{:S(2)}, u32[]{:S(2)}) collective-permute-start(f32[8,128]{1,0:T(8,128)S(1)} %fusion.4), channel_id=1, source_target_pairs={{0,2},{1,3},{2,0},{3,1},{4,6},{5,7},{6,4},{7,5},{8,10},{9,11},{10,... | collective-permute-start | bytes 12296 | tf_op jit(solution)/shard_map/ppermute | solution.py:261
  133.6 3.5 %collective-permute-done.41 = f32[8,128]{1,0:T(8,128)S(1)} collective-permute-done((f32[8,128]{1,0:T(8,128)S(1)}, f32[8,128]{1,0:T(8,128)S(1)}, u32[]{:S(2)}, u32[]{:S(2)}) %collective-permute-start.41) | collective-permute-done | bytes 4128 | tf_op jit(solution)/shard_map/ppermute | solution.py:261
  (136 shorter events, 42.2 us)
Async XLA Ops:
  0.6 15.8 %collective-permute-start.2 = (bf16[8,128,128]{2,1,0:T(8,128)(2,1)}, bf16[8,128,128]{2,1,0:T(8,128)(2,1)S(1)}, u32[]{:S(2)}, u32[]{:S(2)}) collective-permute-start(bf16[8,128,128]{2,1,0:T(8,128)(2,1)} %bitcast.58), channel_id=1, source_target_pairs={{0,16},{1,20},{2,18},{3,22},{4,17},{5,21},{6,19},{7,23},{8,24},{9,... | collective-permute-start | bytes 786440 | tf_op jit(solution)/shard_map/ppermute | solution.py:261
  1.0 15.4 %collective-permute-start.1 = (bf16[8,128,128]{2,1,0:T(8,128)(2,1)}, bf16[8,128,128]{2,1,0:T(8,128)(2,1)S(1)}, u32[]{:S(2)}, u32[]{:S(2)}) collective-permute-start(bf16[8,128,128]{2,1,0:T(8,128)(2,1)} %bitcast.59), channel_id=1, source_target_pairs={{0,8},{1,12},{2,10},{3,14},{4,9},{5,13},{6,11},{7,15},{8,0},{9,4},... | collective-permute-start | bytes 786440 | tf_op jit(solution)/shard_map/ppermute | solution.py:261
  1.5 23.0 %collective-permute-start.7 = (bf16[8,128,128]{2,1,0:T(8,128)(2,1)}, bf16[8,128,128]{2,1,0:T(8,128)(2,1)S(1)}, u32[]{:S(2)}, u32[]{:S(2)}) collective-permute-start(bf16[8,128,128]{2,1,0:T(8,128)(2,1)} %bitcast.60), channel_id=1, source_target_pairs={{0,0},{1,4},{2,2},{3,6},{4,1},{5,5},{6,3},{7,7},{8,8},{9,12},{10,1... | collective-permute-start | bytes 786440 | tf_op jit(solution)/shard_map/ppermute | solution.py:261
  3.1 18.8 %collective-permute-start = (bf16[8,128,128]{2,1,0:T(8,128)(2,1)}, bf16[8,128,128]{2,1,0:T(8,128)(2,1)S(1)}, u32[]{:S(2)}, u32[]{:S(2)}) collective-permute-start(bf16[8,128,128]{2,1,0:T(8,128)(2,1)} %bitcast.57), channel_id=1, source_target_pairs={{0,0},{1,4},{2,2},{3,6},{4,1},{5,5},{6,3},{7,7},{8,8},{9,12},{10,1... | collective-permute-start | bytes 786440 | tf_op jit(solution)/shard_map/ppermute | solution.py:261
  4.7 21.6 %collective-permute-start.6 = (bf16[8,128,128]{2,1,0:T(8,128)(2,1)}, bf16[8,128,128]{2,1,0:T(8,128)(2,1)S(1)}, u32[]{:S(2)}, u32[]{:S(2)}) collective-permute-start(bf16[8,128,128]{2,1,0:T(8,128)(2,1)} %bitcast.61), channel_id=1, source_target_pairs={{0,0},{1,4},{2,2},{3,6},{4,1},{5,5},{6,3},{7,7},{8,8},{9,12},{10,1... | collective-permute-start | bytes 786440 | tf_op jit(solution)/shard_map/ppermute | solution.py:261
  16.5 10.4 %collective-permute-start.10 = (bf16[8,128,128]{2,1,0:T(8,128)(2,1)S(1)}, bf16[8,128,128]{2,1,0:T(8,128)(2,1)S(1)}, u32[]{:S(2)}, u32[]{:S(2)}) collective-permute-start(bf16[8,128,128]{2,1,0:T(8,128)(2,1)S(1)} %collective-permute-done.2.refs_2_), channel_id=1, source_target_pairs={{0,1},{1,0},{2,3},{3,2},{4,5},{5,4},{6,7},{7,6},{8,9},{9,8},{10,11... | collective-permute-start | bytes 786440 | tf_op jit(solution)/shard_map/ppermute | solution.py:261
  21.9 14.8 %collective-permute-start.5 = (bf16[8,128,128]{2,1,0:T(8,128)(2,1)S(1)}, bf16[8,128,128]{2,1,0:T(8,128)(2,1)S(1)}, u32[]{:S(2)}, u32[]{:S(2)}) collective-permute-start(bf16[8,128,128]{2,1,0:T(8,128)(2,1)S(1)} %collective-permute-done.refs_0_), channel_id=1, source_target_pairs={{0,16},{1,17},{2,18},{3,19},{4,20},{5,21},{6,22},{7,23},{8,24},{9,... | collective-permute-start | bytes 786440 | tf_op jit(solution)/shard_map/ppermute | solution.py:261
  28.8 13.6 %collective-permute-start.4 = (bf16[8,128,128]{2,1,0:T(8,128)(2,1)S(1)}, bf16[8,128,128]{2,1,0:T(8,128)(2,1)S(1)}, u32[]{:S(2)}, u32[]{:S(2)}) collective-permute-start(bf16[8,128,128]{2,1,0:T(8,128)(2,1)S(1)} %collective-permute-done.refs_0_), channel_id=1, source_target_pairs={{0,8},{1,9},{2,10},{3,11},{4,12},{5,13},{6,14},{7,15},{8,0},{9,1},... | collective-permute-start | bytes 786440 | tf_op jit(solution)/shard_map/ppermute | solution.py:261
  36.8 10.7 %collective-permute-start.13 = (bf16[8,128,128]{2,1,0:T(8,128)(2,1)S(1)}, bf16[8,128,128]{2,1,0:T(8,128)(2,1)S(1)}, u32[]{:S(2)}, u32[]{:S(2)}) collective-permute-start(bf16[8,128,128]{2,1,0:T(8,128)(2,1)S(1)} %collective-permute-done.5.refs_2_), channel_id=1, source_target_pairs={{0,8},{1,9},{2,10},{3,11},{4,12},{5,13},{6,14},{7,15},{8,0},{9,1},... | collective-permute-start | bytes 786440 | tf_op jit(solution)/shard_map/ppermute | solution.py:261
  36.8 10.9 %collective-permute-start.14 = (bf16[8,128,128]{2,1,0:T(8,128)(2,1)S(1)}, bf16[8,128,128]{2,1,0:T(8,128)(2,1)S(1)}, u32[]{:S(2)}, u32[]{:S(2)}) collective-permute-start(bf16[8,128,128]{2,1,0:T(8,128)(2,1)S(1)} %get-tuple-element.38), channel_id=1, source_target_pairs={{0,4},{1,5},{2,6},{3,7},{4,0},{5,1},{6,2},{7,3},{8,12},{9,13},{10,... | collective-permute-start | bytes 786440 | tf_op jit(solution)/shard_map/ppermute | solution.py:261
  37.7 9.9 %collective-permute-start.15 = (bf16[8,128,128]{2,1,0:T(8,128)(2,1)S(1)}, bf16[8,128,128]{2,1,0:T(8,128)(2,1)S(1)}, u32[]{:S(2)}, u32[]{:S(2)}) collective-permute-start(bf16[8,128,128]{2,1,0:T(8,128)(2,1)S(1)} %get-tuple-element.39), channel_id=1, source_target_pairs={{0,2},{1,3},{2,0},{3,1},{4,6},{5,7},{6,4},{7,5},{8,10},{9,11},{10,... | collective-permute-start | bytes 786440 | tf_op jit(solution)/shard_map/ppermute | solution.py:261
  38.2 13.3 %collective-permute-start.16 = (bf16[8,128,128]{2,1,0:T(8,128)(2,1)S(1)}, bf16[8,128,128]{2,1,0:T(8,128)(2,1)S(1)}, u32[]{:S(2)}, u32[]{:S(2)}) collective-permute-start(bf16[8,128,128]{2,1,0:T(8,128)(2,1)S(1)} %get-tuple-element.40), channel_id=1, source_target_pairs={{0,6},{1,7},{2,4},{3,5},{4,2},{5,3},{6,0},{7,1},{8,14},{9,15},{10,... | collective-permute-start | bytes 786440 | tf_op jit(solution)/shard_map/ppermute | solution.py:261
  42.3 9.7 %collective-permute-start.17 = (bf16[8,128,128]{2,1,0:T(8,128)(2,1)S(1)}, bf16[8,128,128]{2,1,0:T(8,128)(2,1)S(1)}, u32[]{:S(2)}, u32[]{:S(2)}) collective-permute-start(bf16[8,128,128]{2,1,0:T(8,128)(2,1)S(1)} %collective-permute-done.refs_0_), channel_id=1, source_target_pairs={{0,1},{1,0},{2,3},{3,2},{4,5},{5,4},{6,7},{7,6},{8,9},{9,8},{10,11... | collective-permute-start | bytes 786440 | tf_op jit(solution)/shard_map/ppermute | solution.py:261
  47.5 13.7 %collective-permute-start.21 = (bf16[8,128,128]{2,1,0:T(8,128)(2,1)S(1)}, bf16[8,128,128]{2,1,0:T(8,128)(2,1)S(1)}, u32[]{:S(2)}, u32[]{:S(2)}) collective-permute-start(bf16[8,128,128]{2,1,0:T(8,128)(2,1)S(1)} %collective-permute-done.12.refs_8_.refs_0_), channel_id=1, source_target_pairs={{0,16},{1,17},{2,18},{3,19},{4,20},{5,21},{6,22},{7,23},{8,24},{9,... | collective-permute-start | bytes 786440 | tf_op jit(solution)/shard_map/ppermute | solution.py:261
  51.6 9.6 %collective-permute-start.18 = (bf16[8,128,128]{2,1,0:T(8,128)(2,1)S(1)}, bf16[8,128,128]{2,1,0:T(8,128)(2,1)S(1)}, u32[]{:S(2)}, u32[]{:S(2)}) collective-permute-start(bf16[8,128,128]{2,1,0:T(8,128)(2,1)S(1)} %collective-permute-done.4.refs_1_), channel_id=1, source_target_pairs={{0,1},{1,0},{2,3},{3,2},{4,5},{5,4},{6,7},{7,6},{8,9},{9,8},{10,11... | collective-permute-start | bytes 786440 | tf_op jit(solution)/shard_map/ppermute | solution.py:261
  51.6 9.6 %collective-permute-start.19 = (bf16[8,128,128]{2,1,0:T(8,128)(2,1)S(1)}, bf16[8,128,128]{2,1,0:T(8,128)(2,1)S(1)}, u32[]{:S(2)}, u32[]{:S(2)}) collective-permute-start(bf16[8,128,128]{2,1,0:T(8,128)(2,1)S(1)} %collective-permute-done.5.refs_2_), channel_id=1, source_target_pairs={{0,1},{1,0},{2,3},{3,2},{4,5},{5,4},{6,7},{7,6},{8,9},{9,8},{10,11... | collective-permute-start | bytes 786440 | tf_op jit(solution)/shard_map/ppermute | solution.py:261
  65.5 13.0 %collective-permute-start.24 = (bf16[8,128,128]{2,1,0:T(8,128)(2,1)S(1)}, bf16[8,128,128]{2,1,0:T(8,128)(2,1)S(1)}, u32[]{:S(2)}, u32[]{:S(2)}) collective-permute-start(bf16[8,128,128]{2,1,0:T(8,128)(2,1)S(1)} %get-tuple-element.49), channel_id=1, source_target_pairs={{0,6},{1,7},{2,4},{3,5},{4,2},{5,3},{6,0},{7,1},{8,14},{9,15},{10,... | collective-permute-start | bytes 786440 | tf_op jit(solution)/shard_map/ppermute | solution.py:261
  67.0 14.1 %collective-permute-start.26 = (bf16[8,128,128]{2,1,0:T(8,128)(2,1)S(1)}, bf16[8,128,128]{2,1,0:T(8,128)(2,1)S(1)}, u32[]{:S(2)}, u32[]{:S(2)}) collective-permute-start(bf16[8,128,128]{2,1,0:T(8,128)(2,1)S(1)} %collective-permute-done.12.refs_8_.refs_0_), channel_id=1, source_target_pairs={{0,8},{1,9},{2,10},{3,11},{4,12},{5,13},{6,14},{7,15},{8,0},{9,1},... | collective-permute-start | bytes 786440 | tf_op jit(solution)/shard_map/ppermute | solution.py:261
  67.0 17.6 %collective-permute-start.28 = (bf16[8,128,128]{2,1,0:T(8,128)(2,1)S(1)}, bf16[8,128,128]{2,1,0:T(8,128)(2,1)S(1)}, u32[]{:S(2)}, u32[]{:S(2)}) collective-permute-start(bf16[8,128,128]{2,1,0:T(8,128)(2,1)S(1)} %collective-permute-done.12.refs_8_.refs_0_), channel_id=1, source_target_pairs={{0,1},{1,0},{2,3},{3,2},{4,5},{5,4},{6,7},{7,6},{8,9},{9,8},{10,11... | collective-permute-start | bytes 786440 | tf_op jit(solution)/shard_map/ppermute | solution.py:261
  71.8 12.5 %collective-permute-start.27 = (bf16[8,128,128]{2,1,0:T(8,128)(2,1)S(1)}, bf16[8,128,128]{2,1,0:T(8,128)(2,1)S(1)}, u32[]{:S(2)}, u32[]{:S(2)}) collective-permute-start(bf16[8,128,128]{2,1,0:T(8,128)(2,1)S(1)} %collective-permute-done.21.refs_12_.refs_2_), channel_id=1, source_target_pairs={{0,8},{1,9},{2,10},{3,11},{4,12},{5,13},{6,14},{7,15},{8,0},{9,1},... | collective-permute-start | bytes 786440 | tf_op jit(solution)/shard_map/ppermute | solution.py:261
  81.1 11.5 %collective-permute-start.25 = (bf16[8,128,128]{2,1,0:T(8,128)(2,1)S(1)}, bf16[8,128,128]{2,1,0:T(8,128)(2,1)S(1)}, u32[]{:S(2)}, u32[]{:S(2)}) collective-permute-start(bf16[8,128,128]{2,1,0:T(8,128)(2,1)S(1)} %add_convert_fusion), channel_id=1, source_target_pairs={{0,0},{1,1},{2,2},{3,3},{4,4},{5,5},{6,6},{7,7},{8,10},{9,11},{10,... | collective-permute-start | bytes 786440 | tf_op jit(solution)/shard_map/ppermute | solution.py:261
  99.8 13.4 %collective-permute-start.36 = (bf16[1040,128]{1,0:T(8,128)(2,1)S(1)}, bf16[1040,128]{1,0:T(8,128)(2,1)S(1)}, u32[]{:S(2)}, u32[]{:S(2)}) collective-permute-start(bf16[1040,128]{1,0:T(8,128)(2,1)S(1)} %get-tuple-element.57), channel_id=1, source_target_pairs={{0,6},{1,7},{2,4},{3,5},{4,2},{5,3},{6,0},{7,1},{8,14},{9,15},{10,... | collective-permute-start | bytes 798728 | tf_op jit(solution)/shard_map/ppermute | solution.py:261
  113.5 12.1 %collective-permute-start.37 = (bf16[1040,128]{1,0:T(8,128)(2,1)S(1)}, bf16[1040,128]{1,0:T(8,128)(2,1)S(1)}, u32[]{:S(2)}, u32[]{:S(2)}) collective-permute-start(bf16[1040,128]{1,0:T(8,128)(2,1)S(1)} %plane_sum.1.own_ref), channel_id=1, source_target_pairs={{0,0},{1,1},{2,20},{3,21},{4,10},{5,11},{6,30},{7,31},{8,16},{9,17... | collective-permute-start | bytes 798728 | tf_op jit(solution)/shard_map/ppermute | solution.py:261
  128.0 11.3 %collective-permute-start.39 = (bf16[8,128,128]{2,1,0:T(8,128)(2,1)S(1)}, bf16[8,128,128]{2,1,0:T(8,128)(2,1)S(1)}, u32[]{:S(2)}, u32[]{:S(2)}) collective-permute-start(bf16[8,128,128]{2,1,0:T(8,128)(2,1)S(1)} %commutator_difference.1), channel_id=1, source_target_pairs={{0,0},{1,4},{2,2},{3,6},{4,1},{5,5},{6,3},{7,7},{8,10},{9,14},{10,... | collective-permute-start | bytes 786440 | tf_op jit(solution)/shard_map/ppermute | solution.py:261
  (21 other events, 129.4 us)
where the time goes:
time: 142 us; the launch traced here: 141 us
  waiting for transfers between devices  75.8 us (53%)
  starting transfers between devices  43.7 us (31%)
  Pallas kernels  7.8 us (5%)
  local copies, waits for them, and re-layouts  7.35 us (5%)
  other arithmetic  3.73 us (3%)
  between operations  2.77 us (2%)
    ppermute x43, waiting for transfers between devices, permute(): return lax.ppermute(x, ('row', 'col'), row_major_perm(n_row, n_col, target))  75.8 us
    ppermute x43, starting transfers between devices, permute(): return lax.ppermute(x, ('row', 'col'), row_major_perm(n_row, n_col, target))  43.7 us
  transfers between devices with their start and end apart: 43, of which 19 were waited for; matrix products, arithmetic and copies ran while one was open for 7% of the time, Pallas kernels for 2%

commit v1 on v0

--- a/solution.py
+++ b/solution.py
@@ -81,10 +81,10 @@
     multiply(index_ref, index_at, left_of, right, results, outs, out_sems, rows, slots, 1)
 
 
-def second_kernel(rows, slots, n_pieces, n_out, n_early, index_at, index_ref, *refs):
+def second_kernel(rows, slots, n_pieces, n_out, index_at, index_ref, *refs):
     pieces, parts = refs[:n_pieces], refs[n_pieces : n_pieces + n_out]
     right, left, part_first, part_others, first, others, sems, out_sems = refs[-8:]
-    outs = refs[n_pieces + n_out + n_early : -8]
+    outs = refs[n_pieces + n_out : -8]
     held = split_results(part_first, part_others)
     wait_for(start_copies(list(zip(parts, held)) + into(pieces, right, rows * slots), sems))
     for b in range(rows * slots):
@@ -356,14 +356,13 @@
     dens_far = {m + 1: to_plane(after(dens_near[m], outs), 1) for m in far_from}
     kohn_behind = after(kohn_own, (dens_near, outs))
     kohn_pieces = {m: to_plane(kohn_behind, m) for m in far_from}
-    kohn_early = list(kohn_pieces.values())
     dens_near, dens_far = after((dens_near, dens_far), parts[1:])
     dens_beside |= share_all(dens_near) | share_all(dens_far)
     dens_all = listed({0: dens_own} | dens_near | dens_far, dens_beside)
     outs = pl.pallas_call(
-        functools.partial(second_kernel, rows, slots, n_row, n_col, len(kohn_early), later_at),
+        functools.partial(second_kernel, rows, slots, n_row, n_col, later_at),
         out_shape=out_shapes,
-        in_specs=[smem] + [anywhere] * (n_row + n_col + len(kohn_early)),
+        in_specs=[smem] + [anywhere] * (n_row + n_col),
         out_specs=(anywhere,) * n_col,
         scratch_shapes=[
             held(n_row * blocks + 1),
@@ -376,7 +375,7 @@
         compiler_params=params,
         cost_estimate=cost,
         name="change_product",
-    )(tables, *dens_all, *parts, *kohn_early)
+    )(tables, *dens_all, *parts)
     second_outs = outs
     total = total_of(exchange(outs))
 

time: 142 us -> 136 us (0.958)
  waiting for transfers between devices: 75.8 us -> 66.2 us
  starting transfers between devices: 43.7 us -> 46.8 us
    ppermute x43, waiting for transfers between devices: 75.8 us -> 66.2 us  [permute(): return lax.ppermute(x, ('row', 'col'), row_major_perm(n_row, n_col, target))]
    ppermute x43, starting transfers between devices: 43.7 us -> 46.8 us  [permute(): return lax.ppermute(x, ('row', 'col'), row_major_perm(n_row, n_col, target))]
  transfers between devices with their start and end apart: 43 -> 43, of which waited for: 19 -> 17; matrix products, arithmetic and copies ran while one was open for 7% -> 7% of each run, Pallas kernels for 2% -> 3%
where the time goes in v1:
time: 136 us; the launch traced here: 135 us
  waiting for transfers between devices  66.2 us (49%)
  starting transfers between devices  46.8 us (34%)
  Pallas kernels  7.81 us (6%)
  local copies, waits for them, and re-layouts  7.35 us (5%)
  other arithmetic  3.75 us (3%)
  between operations  2.79 us (2%)
    ppermute x43, waiting for transfers between devices, permute(): return lax.ppermute(x, ('row', 'col'), row_major_perm(n_row, n_col, target))  66.2 us
    ppermute x43, starting transfers between devices, permute(): return lax.ppermute(x, ('row', 'col'), row_major_perm(n_row, n_col, target))  46.8 us
  transfers between devices with their start and end apart: 43, of which 17 were waited for; matrix products, arithmetic and copies ran while one was open for 7% of the time, Pallas kernels for 3%

profile of v1, /device:TPU:26, one launch (start us, length us, event | category | flops | bytes accessed | tf_op | source)
XLA Modules:
  0.0 134.7 jit_solution(1537781123951691171)
XLA Ops:
  13.6 2.9 %collective-permute-done.2.refs_2_ = bf16[8,128,128]{2,1,0:T(8,128)(2,1)S(1)} collective-permute-done((bf16[8,128,128]{2,1,0:T(8,128)(2,1)}, bf16[8,128,128]{2,1,0:T(8,128)(2,1)S(1)}, u32[]{:S(2)}, u32[]{:S(2)}) %collective-permute-start.2) | collective-permute-done | bytes 262176 | tf_op jit(solution)/shard_map/ppermute | solution.py:261
  16.5 3.5 %collective-permute-start.10 = (bf16[8,128,128]{2,1,0:T(8,128)(2,1)S(1)}, bf16[8,128,128]{2,1,0:T(8,128)(2,1)S(1)}, u32[]{:S(2)}, u32[]{:S(2)}) collective-permute-start(bf16[8,128,128]{2,1,0:T(8,128)(2,1)S(1)} %collective-permute-done.2.refs_2_), channel_id=1, source_target_pairs={{0,1},{1,0},{2,3},{3,2},{4,5},{5,4},{6,7},{7,6},{8,9},{9,8},{10,11... | collective-permute-start | bytes 786440 | tf_op jit(solution)/shard_map/ppermute | solution.py:261
  21.9 2.6 %collective-permute-start.5 = (bf16[8,128,128]{2,1,0:T(8,128)(2,1)S(1)}, bf16[8,128,128]{2,1,0:T(8,128)(2,1)S(1)}, u32[]{:S(2)}, u32[]{:S(2)}) collective-permute-start(bf16[8,128,128]{2,1,0:T(8,128)(2,1)S(1)} %collective-permute-done.refs_0_), channel_id=1, source_target_pairs={{0,16},{1,17},{2,18},{3,19},{4,20},{5,21},{6,22},{7,23},{8,24},{9,... | collective-permute-start | bytes 786440 | tf_op jit(solution)/shard_map/ppermute | solution.py:261
  29.5 2.2 %scaled_step_product.1 = (f32[8,128,128]{2,1,0:T(8,128)S(1)}, bf16[8,128,128]{2,1,0:T(8,128)(2,1)S(1)}, bf16[8,128,128]{2,1,0:T(8,128)(2,1)S(1)}, bf16[8,128,128]{2,1,0:T(8,128)(2,1)S(1)}) custom-call(s32[144]{0:T(256)S(1)} %pad_add_fusion.index_ref, bf16[8,128,128]{2,1,0:T(8,128)(2,1)S(1)} %collective-permute-done.6.left_ref, ...), custom_call_target="tpu_custom_call" | custom-call | flops 268435456 | bytes 4194304 | tf_op jit(solution)/shard_map/scaled_step_product/pallas_call | solution.py:343
  31.6 5.1 %collective-permute-done.5.refs_2_ = bf16[8,128,128]{2,1,0:T(8,128)(2,1)S(1)} collective-permute-done((bf16[8,128,128]{2,1,0:T(8,128)(2,1)S(1)}, bf16[8,128,128]{2,1,0:T(8,128)(2,1)S(1)}, u32[]{:S(2)}, u32[]{:S(2)}) %collective-permute-start.5) | collective-permute-done | bytes 262176 | tf_op jit(solution)/shard_map/ppermute | solution.py:261
  38.2 2.0 %collective-permute-start.16 = (bf16[8,128,128]{2,1,0:T(8,128)(2,1)S(1)}, bf16[8,128,128]{2,1,0:T(8,128)(2,1)S(1)}, u32[]{:S(2)}, u32[]{:S(2)}) collective-permute-start(bf16[8,128,128]{2,1,0:T(8,128)(2,1)S(1)} %get-tuple-element.40), channel_id=1, source_target_pairs={{0,6},{1,7},{2,4},{3,5},{4,2},{5,3},{6,0},{7,1},{8,14},{9,15},{10,... | collective-permute-start | bytes 786440 | tf_op jit(solution)/shard_map/ppermute | solution.py:261
  40.2 2.1 %collective-permute-done.4.refs_1_ = bf16[8,128,128]{2,1,0:T(8,128)(2,1)S(1)} collective-permute-done((bf16[8,128,128]{2,1,0:T(8,128)(2,1)S(1)}, bf16[8,128,128]{2,1,0:T(8,128)(2,1)S(1)}, u32[]{:S(2)}, u32[]{:S(2)}) %collective-permute-start.4) | collective-permute-done | bytes 262176 | tf_op jit(solution)/shard_map/ppermute | solution.py:261
  42.4 5.1 %collective-permute-done.13.refs_3_ = bf16[8,128,128]{2,1,0:T(8,128)(2,1)S(1)} collective-permute-done((bf16[8,128,128]{2,1,0:T(8,128)(2,1)S(1)}, bf16[8,128,128]{2,1,0:T(8,128)(2,1)S(1)}, u32[]{:S(2)}, u32[]{:S(2)}) %collective-permute-start.13) | collective-permute-done | bytes 262176 | tf_op jit(solution)/shard_map/ppermute | solution.py:261
  47.5 4.1 %collective-permute-done.16.refs_11_ = bf16[8,128,128]{2,1,0:T(8,128)(2,1)S(1)} collective-permute-done((bf16[8,128,128]{2,1,0:T(8,128)(2,1)S(1)}, bf16[8,128,128]{2,1,0:T(8,128)(2,1)S(1)}, u32[]{:S(2)}, u32[]{:S(2)}) %collective-permute-start.16) | collective-permute-done | bytes 262176 | tf_op jit(solution)/shard_map/ppermute | solution.py:261
  52.1 2.0 %collective-permute-start.26 = (bf16[8,128,128]{2,1,0:T(8,128)(2,1)S(1)}, bf16[8,128,128]{2,1,0:T(8,128)(2,1)S(1)}, u32[]{:S(2)}, u32[]{:S(2)}) collective-permute-start(bf16[8,128,128]{2,1,0:T(8,128)(2,1)S(1)} %collective-permute-done.12.refs_8_.refs_0_), channel_id=1, source_target_pairs={{0,16},{1,17},{2,18},{3,19},{4,20},{5,21},{6,22},{7,23},{8,24},{9,... | collective-permute-start | bytes 786440 | tf_op jit(solution)/shard_map/ppermute | solution.py:261
  54.2 2.3 %change_product.1 = (f32[8,128,128]{2,1,0:T(8,128)S(1)}, bf16[8,128,128]{2,1,0:T(8,128)(2,1)S(1)}, bf16[8,128,128]{2,1,0:T(8,128)(2,1)S(1)}, bf16[8,128,128]{2,1,0:T(8,128)(2,1)S(1)}) custom-call(s32[144]{0:T(256)S(1)} %pad_add_fusion.index_ref, bf16[8,128,128]{2,1,0:T(8,128)(2,1)S(1)} %collective-permute-done.refs_0_, ...), custom_call_target="tpu_custom_call" | custom-call | flops 268435456 | bytes 4194304 | tf_op jit(solution)/shard_map/change_product/pallas_call | solution.py:362
  61.3 6.1 %collective-permute-done.26.refs_2_ = bf16[8,128,128]{2,1,0:T(8,128)(2,1)S(1)} collective-permute-done((bf16[8,128,128]{2,1,0:T(8,128)(2,1)S(1)}, bf16[8,128,128]{2,1,0:T(8,128)(2,1)S(1)}, u32[]{:S(2)}, u32[]{:S(2)}) %collective-permute-start.26) | collective-permute-done | bytes 262176 | tf_op jit(solution)/shard_map/ppermute | solution.py:261
  67.5 4.3 %collective-permute-done.23 = bf16[8,128,128]{2,1,0:T(8,128)(2,1)S(1)} collective-permute-done((bf16[8,128,128]{2,1,0:T(8,128)(2,1)S(1)}, bf16[8,128,128]{2,1,0:T(8,128)(2,1)S(1)}, u32[]{:S(2)}, u32[]{:S(2)}) %collective-permute-start.23) | collective-permute-done | bytes 262176 | tf_op jit(solution)/shard_map/ppermute | solution.py:261
  71.9 4.3 %collective-permute-start.32 = (bf16[8,128,128]{2,1,0:T(8,128)(2,1)S(1)}, bf16[8,128,128]{2,1,0:T(8,128)(2,1)S(1)}, u32[]{:S(2)}, u32[]{:S(2)}) collective-permute-start(bf16[8,128,128]{2,1,0:T(8,128)(2,1)S(1)} %add_convert_fusion), channel_id=1, source_target_pairs={{0,0},{1,1},{2,16},{3,17},{4,8},{5,9},{6,24},{7,25},{8,20},{9,21},... | collective-permute-start | bytes 786440 | tf_op jit(solution)/shard_map/ppermute | solution.py:261
  76.3 2.7 %collective-permute-start.24 = (bf16[8,128,128]{2,1,0:T(8,128)(2,1)S(1)}, bf16[8,128,128]{2,1,0:T(8,128)(2,1)S(1)}, u32[]{:S(2)}, u32[]{:S(2)}) collective-permute-start(bf16[8,128,128]{2,1,0:T(8,128)(2,1)S(1)} %add_convert_fusion), channel_id=1, source_target_pairs={{0,0},{1,1},{2,2},{3,3},{4,4},{5,5},{6,6},{7,7},{8,10},{9,11},{10,... | collective-permute-start | bytes 786440 | tf_op jit(solution)/shard_map/ppermute | solution.py:261
  79.6 3.6 %collective-permute-done.32.refs_8_ = bf16[8,128,128]{2,1,0:T(8,128)(2,1)S(1)} collective-permute-done((bf16[8,128,128]{2,1,0:T(8,128)(2,1)S(1)}, bf16[8,128,128]{2,1,0:T(8,128)(2,1)S(1)}, u32[]{:S(2)}, u32[]{:S(2)}) %collective-permute-start.32) | collective-permute-done | bytes 262176 | tf_op jit(solution)/shard_map/ppermute | solution.py:261
  83.2 4.5 %collective-permute-done.24.own_ref = bf16[8,128,128]{2,1,0:T(8,128)(2,1)S(1)} collective-permute-done((bf16[8,128,128]{2,1,0:T(8,128)(2,1)S(1)}, bf16[8,128,128]{2,1,0:T(8,128)(2,1)S(1)}, u32[]{:S(2)}, u32[]{:S(2)}) %collective-permute-start.24) | collective-permute-done | bytes 262176 | tf_op jit(solution)/shard_map/ppermute | solution.py:261
  87.8 2.3 %commutator_product.1 = (f32[8,128,128]{2,1,0:T(8,128)S(1)}, bf16[1040,128]{1,0:T(8,128)(2,1)S(1)}, bf16[1040,128]{1,0:T(8,128)(2,1)S(1)}, bf16[1040,128]{1,0:T(8,128)(2,1)S(1)}, bf16[16,128]{1,0:T(8,128)(2,1)S(1)}) custom-call(s32[144]{0:T(256)S(1)} %pad_add_fusion.index_ref, bf16[8,128,128]{2,1,0:T(8,128)(2,1)S(1)} %collective-permute-done.24.own_ref, ...), custom_call_target="tpu_custom_call" | custom-call | flops 268435456 | bytes 4194304 | tf_op jit(solution)/shard_map/commutator_product/pallas_call | solution.py:389
  94.7 3.4 %collective-permute-done.34.refs_0_ = bf16[1040,128]{1,0:T(8,128)(2,1)S(1)} collective-permute-done((bf16[1040,128]{1,0:T(8,128)(2,1)S(1)}, bf16[1040,128]{1,0:T(8,128)(2,1)S(1)}, u32[]{:S(2)}, u32[]{:S(2)}) %collective-permute-start.34) | collective-permute-done | bytes 266272 | tf_op jit(solution)/shard_map/ppermute | solution.py:261
  98.1 2.5 %collective-permute-done.35.refs_1_ = bf16[1040,128]{1,0:T(8,128)(2,1)S(1)} collective-permute-done((bf16[1040,128]{1,0:T(8,128)(2,1)S(1)}, bf16[1040,128]{1,0:T(8,128)(2,1)S(1)}, u32[]{:S(2)}, u32[]{:S(2)}) %collective-permute-start.35) | collective-permute-done | bytes 266272 | tf_op jit(solution)/shard_map/ppermute | solution.py:261
  100.6 6.2 %collective-permute-done.36.refs_2_ = bf16[1040,128]{1,0:T(8,128)(2,1)S(1)} collective-permute-done((bf16[1040,128]{1,0:T(8,128)(2,1)S(1)}, bf16[1040,128]{1,0:T(8,128)(2,1)S(1)}, u32[]{:S(2)}, u32[]{:S(2)}) %collective-permute-start.36) | collective-permute-done | bytes 266272 | tf_op jit(solution)/shard_map/ppermute | solution.py:261
  109.0 10.2 %collective-permute-done.37.refs_0_ = bf16[1040,128]{1,0:T(8,128)(2,1)S(1)} collective-permute-done((bf16[1040,128]{1,0:T(8,128)(2,1)S(1)}, bf16[1040,128]{1,0:T(8,128)(2,1)S(1)}, u32[]{:S(2)}, u32[]{:S(2)}) %collective-permute-start.37) | collective-permute-done | bytes 266272 | tf_op jit(solution)/shard_map/ppermute | solution.py:261
  123.6 3.5 %collective-permute-start.41 = (f32[8,128]{1,0:T(8,128)S(1)}, f32[8,128]{1,0:T(8,128)S(1)}, u32[]{:S(2)}, u32[]{:S(2)}) collective-permute-start(f32[8,128]{1,0:T(8,128)S(1)} %fusion.4), channel_id=1, source_target_pairs={{0,2},{1,3},{2,0},{3,1},{4,6},{5,7},{6,4},{7,5},{8,10},{9,11},{10,... | collective-permute-start | bytes 12296 | tf_op jit(solution)/shard_map/ppermute | solution.py:261
  127.2 3.9 %collective-permute-done.41 = f32[8,128]{1,0:T(8,128)S(1)} collective-permute-done((f32[8,128]{1,0:T(8,128)S(1)}, f32[8,128]{1,0:T(8,128)S(1)}, u32[]{:S(2)}, u32[]{:S(2)}) %collective-permute-start.41) | collective-permute-done | bytes 4128 | tf_op jit(solution)/shard_map/ppermute | solution.py:261
  (136 shorter events, 40.6 us)
Async XLA Ops:
  0.6 15.8 %collective-permute-start.2 = (bf16[8,128,128]{2,1,0:T(8,128)(2,1)}, bf16[8,128,128]{2,1,0:T(8,128)(2,1)S(1)}, u32[]{:S(2)}, u32[]{:S(2)}) collective-permute-start(bf16[8,128,128]{2,1,0:T(8,128)(2,1)} %bitcast.58), channel_id=1, source_target_pairs={{0,16},{1,20},{2,18},{3,22},{4,17},{5,21},{6,19},{7,23},{8,24},{9,... | collective-permute-start | bytes 786440 | tf_op jit(solution)/shard_map/ppermute | solution.py:261
  1.0 15.4 %collective-permute-start.1 = (bf16[8,128,128]{2,1,0:T(8,128)(2,1)}, bf16[8,128,128]{2,1,0:T(8,128)(2,1)S(1)}, u32[]{:S(2)}, u32[]{:S(2)}) collective-permute-start(bf16[8,128,128]{2,1,0:T(8,128)(2,1)} %bitcast.59), channel_id=1, source_target_pairs={{0,8},{1,12},{2,10},{3,14},{4,9},{5,13},{6,11},{7,15},{8,0},{9,4},... | collective-permute-start | bytes 786440 | tf_op jit(solution)/shard_map/ppermute | solution.py:261
  1.5 23.0 %collective-permute-start.7 = (bf16[8,128,128]{2,1,0:T(8,128)(2,1)}, bf16[8,128,128]{2,1,0:T(8,128)(2,1)S(1)}, u32[]{:S(2)}, u32[]{:S(2)}) collective-permute-start(bf16[8,128,128]{2,1,0:T(8,128)(2,1)} %bitcast.60), channel_id=1, source_target_pairs={{0,0},{1,4},{2,2},{3,6},{4,1},{5,5},{6,3},{7,7},{8,8},{9,12},{10,1... | collective-permute-start | bytes 786440 | tf_op jit(solution)/shard_map/ppermute | solution.py:261
  3.1 18.8 %collective-permute-start = (bf16[8,128,128]{2,1,0:T(8,128)(2,1)}, bf16[8,128,128]{2,1,0:T(8,128)(2,1)S(1)}, u32[]{:S(2)}, u32[]{:S(2)}) collective-permute-start(bf16[8,128,128]{2,1,0:T(8,128)(2,1)} %bitcast.57), channel_id=1, source_target_pairs={{0,0},{1,4},{2,2},{3,6},{4,1},{5,5},{6,3},{7,7},{8,8},{9,12},{10,1... | collective-permute-start | bytes 786440 | tf_op jit(solution)/shard_map/ppermute | solution.py:261
  4.7 21.6 %collective-permute-start.6 = (bf16[8,128,128]{2,1,0:T(8,128)(2,1)}, bf16[8,128,128]{2,1,0:T(8,128)(2,1)S(1)}, u32[]{:S(2)}, u32[]{:S(2)}) collective-permute-start(bf16[8,128,128]{2,1,0:T(8,128)(2,1)} %bitcast.61), channel_id=1, source_target_pairs={{0,0},{1,4},{2,2},{3,6},{4,1},{5,5},{6,3},{7,7},{8,8},{9,12},{10,1... | collective-permute-start | bytes 786440 | tf_op jit(solution)/shard_map/ppermute | solution.py:261
  16.5 10.4 %collective-permute-start.10 = (bf16[8,128,128]{2,1,0:T(8,128)(2,1)S(1)}, bf16[8,128,128]{2,1,0:T(8,128)(2,1)S(1)}, u32[]{:S(2)}, u32[]{:S(2)}) collective-permute-start(bf16[8,128,128]{2,1,0:T(8,128)(2,1)S(1)} %collective-permute-done.2.refs_2_), channel_id=1, source_target_pairs={{0,1},{1,0},{2,3},{3,2},{4,5},{5,4},{6,7},{7,6},{8,9},{9,8},{10,11... | collective-permute-start | bytes 786440 | tf_op jit(solution)/shard_map/ppermute | solution.py:261
  21.9 14.8 %collective-permute-start.5 = (bf16[8,128,128]{2,1,0:T(8,128)(2,1)S(1)}, bf16[8,128,128]{2,1,0:T(8,128)(2,1)S(1)}, u32[]{:S(2)}, u32[]{:S(2)}) collective-permute-start(bf16[8,128,128]{2,1,0:T(8,128)(2,1)S(1)} %collective-permute-done.refs_0_), channel_id=1, source_target_pairs={{0,16},{1,17},{2,18},{3,19},{4,20},{5,21},{6,22},{7,23},{8,24},{9,... | collective-permute-start | bytes 786440 | tf_op jit(solution)/shard_map/ppermute | solution.py:261
  28.8 13.6 %collective-permute-start.4 = (bf16[8,128,128]{2,1,0:T(8,128)(2,1)S(1)}, bf16[8,128,128]{2,1,0:T(8,128)(2,1)S(1)}, u32[]{:S(2)}, u32[]{:S(2)}) collective-permute-start(bf16[8,128,128]{2,1,0:T(8,128)(2,1)S(1)} %collective-permute-done.refs_0_), channel_id=1, source_target_pairs={{0,8},{1,9},{2,10},{3,11},{4,12},{5,13},{6,14},{7,15},{8,0},{9,1},... | collective-permute-start | bytes 786440 | tf_op jit(solution)/shard_map/ppermute | solution.py:261
  36.8 10.7 %collective-permute-start.13 = (bf16[8,128,128]{2,1,0:T(8,128)(2,1)S(1)}, bf16[8,128,128]{2,1,0:T(8,128)(2,1)S(1)}, u32[]{:S(2)}, u32[]{:S(2)}) collective-permute-start(bf16[8,128,128]{2,1,0:T(8,128)(2,1)S(1)} %collective-permute-done.5.refs_2_), channel_id=1, source_target_pairs={{0,8},{1,9},{2,10},{3,11},{4,12},{5,13},{6,14},{7,15},{8,0},{9,1},... | collective-permute-start | bytes 786440 | tf_op jit(solution)/shard_map/ppermute | solution.py:261
  36.8 10.7 %collective-permute-start.14 = (bf16[8,128,128]{2,1,0:T(8,128)(2,1)S(1)}, bf16[8,128,128]{2,1,0:T(8,128)(2,1)S(1)}, u32[]{:S(2)}, u32[]{:S(2)}) collective-permute-start(bf16[8,128,128]{2,1,0:T(8,128)(2,1)S(1)} %get-tuple-element.38), channel_id=1, source_target_pairs={{0,4},{1,5},{2,6},{3,7},{4,0},{5,1},{6,2},{7,3},{8,12},{9,13},{10,... | collective-permute-start | bytes 786440 | tf_op jit(solution)/shard_map/ppermute | solution.py:261
  37.7 9.8 %collective-permute-start.15 = (bf16[8,128,128]{2,1,0:T(8,128)(2,1)S(1)}, bf16[8,128,128]{2,1,0:T(8,128)(2,1)S(1)}, u32[]{:S(2)}, u32[]{:S(2)}) collective-permute-start(bf16[8,128,128]{2,1,0:T(8,128)(2,1)S(1)} %get-tuple-element.39), channel_id=1, source_target_pairs={{0,2},{1,3},{2,0},{3,1},{4,6},{5,7},{6,4},{7,5},{8,10},{9,11},{10,... | collective-permute-start | bytes 786440 | tf_op jit(solution)/shard_map/ppermute | solution.py:261
  38.2 13.3 %collective-permute-start.16 = (bf16[8,128,128]{2,1,0:T(8,128)(2,1)S(1)}, bf16[8,128,128]{2,1,0:T(8,128)(2,1)S(1)}, u32[]{:S(2)}, u32[]{:S(2)}) collective-permute-start(bf16[8,128,128]{2,1,0:T(8,128)(2,1)S(1)} %get-tuple-element.40), channel_id=1, source_target_pairs={{0,6},{1,7},{2,4},{3,5},{4,2},{5,3},{6,0},{7,1},{8,14},{9,15},{10,... | collective-permute-start | bytes 786440 | tf_op jit(solution)/shard_map/ppermute | solution.py:261
  42.3 11.8 %collective-permute-start.17 = (bf16[8,128,128]{2,1,0:T(8,128)(2,1)S(1)}, bf16[8,128,128]{2,1,0:T(8,128)(2,1)S(1)}, u32[]{:S(2)}, u32[]{:S(2)}) collective-permute-start(bf16[8,128,128]{2,1,0:T(8,128)(2,1)S(1)} %collective-permute-done.refs_0_), channel_id=1, source_target_pairs={{0,1},{1,0},{2,3},{3,2},{4,5},{5,4},{6,7},{7,6},{8,9},{9,8},{10,11... | collective-permute-start | bytes 786440 | tf_op jit(solution)/shard_map/ppermute | solution.py:261
  52.1 15.3 %collective-permute-start.26 = (bf16[8,128,128]{2,1,0:T(8,128)(2,1)S(1)}, bf16[8,128,128]{2,1,0:T(8,128)(2,1)S(1)}, u32[]{:S(2)}, u32[]{:S(2)}) collective-permute-start(bf16[8,128,128]{2,1,0:T(8,128)(2,1)S(1)} %collective-permute-done.12.refs_8_.refs_0_), channel_id=1, source_target_pairs={{0,16},{1,17},{2,18},{3,19},{4,20},{5,21},{6,22},{7,23},{8,24},{9,... | collective-permute-start | bytes 786440 | tf_op jit(solution)/shard_map/ppermute | solution.py:261
  56.4 11.0 %collective-permute-start.21 = (bf16[8,128,128]{2,1,0:T(8,128)(2,1)S(1)}, bf16[8,128,128]{2,1,0:T(8,128)(2,1)S(1)}, u32[]{:S(2)}, u32[]{:S(2)}) collective-permute-start(bf16[8,128,128]{2,1,0:T(8,128)(2,1)S(1)} %get-tuple-element.46), channel_id=1, source_target_pairs={{0,4},{1,5},{2,6},{3,7},{4,0},{5,1},{6,2},{7,3},{8,12},{9,13},{10,... | collective-permute-start | bytes 786440 | tf_op jit(solution)/shard_map/ppermute | solution.py:261
  58.4 13.4 %collective-permute-start.23 = (bf16[8,128,128]{2,1,0:T(8,128)(2,1)S(1)}, bf16[8,128,128]{2,1,0:T(8,128)(2,1)S(1)}, u32[]{:S(2)}, u32[]{:S(2)}) collective-permute-start(bf16[8,128,128]{2,1,0:T(8,128)(2,1)S(1)} %get-tuple-element.48), channel_id=1, source_target_pairs={{0,6},{1,7},{2,4},{3,5},{4,2},{5,3},{6,0},{7,1},{8,14},{9,15},{10,... | collective-permute-start | bytes 786440 | tf_op jit(solution)/shard_map/ppermute | solution.py:261
  60.0 16.3 %collective-permute-start.25 = (bf16[8,128,128]{2,1,0:T(8,128)(2,1)S(1)}, bf16[8,128,128]{2,1,0:T(8,128)(2,1)S(1)}, u32[]{:S(2)}, u32[]{:S(2)}) collective-permute-start(bf16[8,128,128]{2,1,0:T(8,128)(2,1)S(1)} %collective-permute-done.12.refs_8_.refs_0_), channel_id=1, source_target_pairs={{0,8},{1,9},{2,10},{3,11},{4,12},{5,13},{6,14},{7,15},{8,0},{9,1},... | collective-permute-start | bytes 786440 | tf_op jit(solution)/shard_map/ppermute | solution.py:261
  67.4 11.8 %collective-permute-start.28 = (bf16[8,128,128]{2,1,0:T(8,128)(2,1)S(1)}, bf16[8,128,128]{2,1,0:T(8,128)(2,1)S(1)}, u32[]{:S(2)}, u32[]{:S(2)}) collective-permute-start(bf16[8,128,128]{2,1,0:T(8,128)(2,1)S(1)} %collective-permute-done.12.refs_8_.refs_0_), channel_id=1, source_target_pairs={{0,1},{1,0},{2,3},{3,2},{4,5},{5,4},{6,7},{7,6},{8,9},{9,8},{10,11... | collective-permute-start | bytes 786440 | tf_op jit(solution)/shard_map/ppermute | solution.py:261
  67.4 11.6 %collective-permute-start.27 = (bf16[8,128,128]{2,1,0:T(8,128)(2,1)S(1)}, bf16[8,128,128]{2,1,0:T(8,128)(2,1)S(1)}, u32[]{:S(2)}, u32[]{:S(2)}) collective-permute-start(bf16[8,128,128]{2,1,0:T(8,128)(2,1)S(1)} %collective-permute-done.26.refs_2_), channel_id=1, source_target_pairs={{0,8},{1,9},{2,10},{3,11},{4,12},{5,13},{6,14},{7,15},{8,0},{9,1},... | collective-permute-start | bytes 786440 | tf_op jit(solution)/shard_map/ppermute | solution.py:261
  71.9 11.4 %collective-permute-start.32 = (bf16[8,128,128]{2,1,0:T(8,128)(2,1)S(1)}, bf16[8,128,128]{2,1,0:T(8,128)(2,1)S(1)}, u32[]{:S(2)}, u32[]{:S(2)}) collective-permute-start(bf16[8,128,128]{2,1,0:T(8,128)(2,1)S(1)} %add_convert_fusion), channel_id=1, source_target_pairs={{0,0},{1,1},{2,16},{3,17},{4,8},{5,9},{6,24},{7,25},{8,20},{9,21},... | collective-permute-start | bytes 786440 | tf_op jit(solution)/shard_map/ppermute | solution.py:261
  76.3 11.5 %collective-permute-start.24 = (bf16[8,128,128]{2,1,0:T(8,128)(2,1)S(1)}, bf16[8,128,128]{2,1,0:T(8,128)(2,1)S(1)}, u32[]{:S(2)}, u32[]{:S(2)}) collective-permute-start(bf16[8,128,128]{2,1,0:T(8,128)(2,1)S(1)} %add_convert_fusion), channel_id=1, source_target_pairs={{0,0},{1,1},{2,2},{3,3},{4,4},{5,5},{6,6},{7,7},{8,10},{9,11},{10,... | collective-permute-start | bytes 786440 | tf_op jit(solution)/shard_map/ppermute | solution.py:261
  93.4 13.4 %collective-permute-start.36 = (bf16[1040,128]{1,0:T(8,128)(2,1)S(1)}, bf16[1040,128]{1,0:T(8,128)(2,1)S(1)}, u32[]{:S(2)}, u32[]{:S(2)}) collective-permute-start(bf16[1040,128]{1,0:T(8,128)(2,1)S(1)} %get-tuple-element.57), channel_id=1, source_target_pairs={{0,6},{1,7},{2,4},{3,5},{4,2},{5,3},{6,0},{7,1},{8,14},{9,15},{10,... | collective-permute-start | bytes 798728 | tf_op jit(solution)/shard_map/ppermute | solution.py:261
  107.1 12.1 %collective-permute-start.37 = (bf16[1040,128]{1,0:T(8,128)(2,1)S(1)}, bf16[1040,128]{1,0:T(8,128)(2,1)S(1)}, u32[]{:S(2)}, u32[]{:S(2)}) collective-permute-start(bf16[1040,128]{1,0:T(8,128)(2,1)S(1)} %plane_sum.1.own_ref), channel_id=1, source_target_pairs={{0,0},{1,1},{2,20},{3,21},{4,10},{5,11},{6,30},{7,31},{8,16},{9,17... | collective-permute-start | bytes 798728 | tf_op jit(solution)/shard_map/ppermute | solution.py:261
  121.6 11.3 %collective-permute-start.39 = (bf16[8,128,128]{2,1,0:T(8,128)(2,1)S(1)}, bf16[8,128,128]{2,1,0:T(8,128)(2,1)S(1)}, u32[]{:S(2)}, u32[]{:S(2)}) collective-permute-start(bf16[8,128,128]{2,1,0:T(8,128)(2,1)S(1)} %commutator_difference.1), channel_id=1, source_target_pairs={{0,0},{1,4},{2,2},{3,6},{4,1},{5,5},{6,3},{7,7},{8,10},{9,14},{10,... | collective-permute-start | bytes 786440 | tf_op jit(solution)/shard_map/ppermute | solution.py:261
  (21 other events, 111.4 us)

commit v2 on v1

--- a/solution.py
+++ b/solution.py
@@ -201,9 +201,6 @@
         bits = (n_col - 1).bit_length()
         return g ^ sum(((o >> b) & 1) << (bits - 1 - b) for b in range(bits))
 
-    def at_spread(o, h, g):
-        return at(o, h, spread(o, g))
-
     def inside_spread(r, c):
         o, h, p = inside(r, c)
         return o, h, spread(o, p)
@@ -248,9 +245,9 @@
             inner * blocks,
         ).astype(jnp.int32).reshape(-1)
 
-    all_tables += [mirror_table(h_in, group_cols_of(own_rows, g)) for g in (g_in, spread_in)]
+    all_tables.append(mirror_table(h_in, group_cols_of(own_rows, g_in)))
     starts = [sum(table.size for table in all_tables[:t]) for t in range(len(all_tables))]
-    first_at, later_at, mirror_at, last_mirror_at = starts
+    first_at, later_at, mirror_at = starts
     tables = jnp.concatenate(all_tables)
 
     smem = pl.BlockSpec(memory_space=pltpu.SMEM)
@@ -281,9 +278,10 @@
     def listed(pieces, shared):
         return [pieces[m] for m in range(outer)] + [shared[m] for m in range(outer)]
 
-    def mirror(x, target):
-        moved = inside_permute(x, lambda o, h, g: (g, h, o), inside_spread, target)
-        return [moved, share(moved)]
+    def settle(x):
+        mirrored = inside_permute(x, lambda o, h, g: (g, h, o), inside_spread)
+        own = inside_permute(x, lambda o, h, g: (o, h, g), inside_spread)
+        return own, [mirrored, share(mirrored)]
 
     def exchange(outs):
         return [outs[0]] + [
@@ -334,8 +332,8 @@
     step = relayout(flat(step_dir))
     dens_own = relayout(dens)
     inter_far = {m + 1: to_plane(inter_near[m], 1) for m in far_from}
-    dens_behind = after(dens_own, inter_near)
-    dens_near = {m: to_plane(dens_behind, m) for m in far_from}
+    dens_behind = after(dens, inter_near)
+    dens_near = {m: relayout(dens_behind, m) for m in far_from}
     dens_behind, kohn = after((dens_own, kohn), (inter_near, inter_far))
     dens_near[1] = to_plane(dens_behind, 1)
     kohn_own = relayout(kohn)
@@ -379,8 +377,7 @@
     second_outs = outs
     total = total_of(exchange(outs))
 
-    mirrored = mirror(total, at)
-    own = inside_permute(total, lambda o, h, g: (o, h, g), inside_spread)
+    own, mirrored = settle(total)
     kohn_pieces = {0: kohn_own} | after(kohn_pieces, second_outs)
     kohn_beside = share_all(kohn_pieces)
     kohn_last = {m + 1: to_plane(kohn_pieces[m], 1) for m in range(0, outer, 2)}
@@ -414,10 +411,10 @@
         compiler_params=params,
         name="plane_sum",
     )(trace, own, *parts)
-    mirrored = mirror(total, at_spread)
+    own, mirrored = settle(total)
 
     commutator = pl.pallas_call(
-        functools.partial(last_kernel, inner, blocks, last_mirror_at),
+        functools.partial(last_kernel, inner, blocks, mirror_at),
         out_shape=jax.ShapeDtypeStruct(block_shape, bf16),
         in_specs=[smem] + [anywhere] * (1 + inner),
         out_specs=anywhere,
@@ -430,9 +427,9 @@
         ],
         compiler_params=params,
         name="commutator_difference",
-    )(tables, total, *mirrored)
+    )(tables, own, *mirrored)
     commutator = inside_permute(
-        commutator, lambda o, h, g: (o, h, g), inside_spread, lambda o, h, g: (o * inner + h, g)
+        commutator, lambda o, h, g: (o, h, g), inside, lambda o, h, g: (o * inner + h, g)
     )
 
     plane_trace = tree_sum([one_part(piece[blocks * side :]) for piece in mirrored])

time: 136 us -> 140 us (1.029)
  starting transfers between devices: 46.8 us -> 54.7 us
    ppermute x43 -> x44, starting transfers between devices: 46.8 us -> 54.7 us  [permute(): return lax.ppermute(x, ('row', 'col'), row_major_perm(n_row, n_col, target))]
    ppermute x43 -> x44, waiting for transfers between devices: 66.2 us -> 64.9 us  [permute(): return lax.ppermute(x, ('row', 'col'), row_major_perm(n_row, n_col, target))]
  transfers between devices with their start and end apart: 43 -> 44, of which waited for: 17 -> 24; matrix products, arithmetic and copies ran while one was open for 7% -> 6% of each run, Pallas kernels for 3% -> 3%
where the time goes in v2:
time: 140 us; the launch traced here: 139 us
  waiting for transfers between devices  64.9 us (46%)
  starting transfers between devices  54.7 us (39%)
  Pallas kernels  7.78 us (6%)
  local copies, waits for them, and re-layouts  6.24 us (4%)
  other arithmetic  3.07 us (2%)
  between operations  2.78 us (2%)
    ppermute x44, waiting for transfers between devices, permute(): return lax.ppermute(x, ('row', 'col'), row_major_perm(n_row, n_col, target))  64.9 us
    ppermute x44, starting transfers between devices, permute(): return lax.ppermute(x, ('row', 'col'), row_major_perm(n_row, n_col, target))  54.7 us
  transfers between devices with their start and end apart: 44, of which 24 were waited for; matrix products, arithmetic and copies ran while one was open for 6% of the time, Pallas kernels for 3%

profile of v2, /device:TPU:26, one launch (start us, length us, event | category | flops | bytes accessed | tf_op | source)
XLA Modules:
  0.0 139.5 jit_solution(10096468422977493428)
XLA Ops:
  12.0 4.4 %collective-permute-done.2.refs_2_ = bf16[8,128,128]{2,1,0:T(8,128)(2,1)S(1)} collective-permute-done((bf16[8,128,128]{2,1,0:T(8,128)(2,1)}, bf16[8,128,128]{2,1,0:T(8,128)(2,1)S(1)}, u32[]{:S(2)}, u32[]{:S(2)}) %collective-permute-start.2) | collective-permute-done | bytes 262176 | tf_op jit(solution)/shard_map/ppermute | solution.py:258
  20.4 2.6 %collective-permute-start.5 = (bf16[8,128,128]{2,1,0:T(8,128)(2,1)}, bf16[8,128,128]{2,1,0:T(8,128)(2,1)S(1)}, u32[]{:S(2)}, u32[]{:S(2)}) collective-permute-start(bf16[8,128,128]{2,1,0:T(8,128)(2,1)} %bitcast.10), channel_id=1, source_target_pairs={{0,16},{1,20},{2,18},{3,22},{4,17},{5,21},{6,19},{7,23},{8,24},{9,... | collective-permute-start | bytes 786440 | tf_op jit(solution)/shard_map/ppermute | solution.py:258
  23.0 3.0 %collective-permute-done.3.refs_3_ = bf16[8,128,128]{2,1,0:T(8,128)(2,1)S(1)} collective-permute-done((bf16[8,128,128]{2,1,0:T(8,128)(2,1)S(1)}, bf16[8,128,128]{2,1,0:T(8,128)(2,1)S(1)}, u32[]{:S(2)}, u32[]{:S(2)}) %collective-permute-start.3) | collective-permute-done | bytes 262176 | tf_op jit(solution)/shard_map/ppermute | solution.py:258
  31.8 3.9 %collective-permute-done.5.refs_2_ = bf16[8,128,128]{2,1,0:T(8,128)(2,1)S(1)} collective-permute-done((bf16[8,128,128]{2,1,0:T(8,128)(2,1)}, bf16[8,128,128]{2,1,0:T(8,128)(2,1)S(1)}, u32[]{:S(2)}, u32[]{:S(2)}) %collective-permute-start.5) | collective-permute-done | bytes 262176 | tf_op jit(solution)/shard_map/ppermute | solution.py:258
  35.7 2.9 %collective-permute-start.14 = (bf16[8,128,128]{2,1,0:T(8,128)(2,1)S(1)}, bf16[8,128,128]{2,1,0:T(8,128)(2,1)S(1)}, u32[]{:S(2)}, u32[]{:S(2)}) collective-permute-start(bf16[8,128,128]{2,1,0:T(8,128)(2,1)S(1)} %get-tuple-element.36), channel_id=1, source_target_pairs={{0,4},{1,5},{2,6},{3,7},{4,0},{5,1},{6,2},{7,3},{8,12},{9,13},{10,... | collective-permute-start | bytes 786440 | tf_op jit(solution)/shard_map/ppermute | solution.py:258
  41.8 4.4 %collective-permute-done.13.refs_3_ = bf16[8,128,128]{2,1,0:T(8,128)(2,1)S(1)} collective-permute-done((bf16[8,128,128]{2,1,0:T(8,128)(2,1)S(1)}, bf16[8,128,128]{2,1,0:T(8,128)(2,1)S(1)}, u32[]{:S(2)}, u32[]{:S(2)}) %collective-permute-start.13) | collective-permute-done | bytes 262176 | tf_op jit(solution)/shard_map/ppermute | solution.py:258
  47.8 3.8 %collective-permute-done.16.refs_11_ = bf16[8,128,128]{2,1,0:T(8,128)(2,1)S(1)} collective-permute-done((bf16[8,128,128]{2,1,0:T(8,128)(2,1)S(1)}, bf16[8,128,128]{2,1,0:T(8,128)(2,1)S(1)}, u32[]{:S(2)}, u32[]{:S(2)}) %collective-permute-start.16) | collective-permute-done | bytes 262176 | tf_op jit(solution)/shard_map/ppermute | solution.py:258
  54.7 2.3 %change_product.1 = (f32[8,128,128]{2,1,0:T(8,128)S(1)}, bf16[8,128,128]{2,1,0:T(8,128)(2,1)S(1)}, bf16[8,128,128]{2,1,0:T(8,128)(2,1)S(1)}, bf16[8,128,128]{2,1,0:T(8,128)(2,1)S(1)}) custom-call(s32[136]{0:T(256)S(1)} %pad_add_fusion.index_ref, bf16[8,128,128]{2,1,0:T(8,128)(2,1)S(1)} %collective-permute-done.refs_0_, ...), custom_call_target="tpu_custom_call" | custom-call | flops 268435456 | bytes 4194304 | tf_op jit(solution)/shard_map/change_product/pallas_call | solution.py:360
  62.4 5.7 %collective-permute-done.26.refs_2_ = bf16[8,128,128]{2,1,0:T(8,128)(2,1)S(1)} collective-permute-done((bf16[8,128,128]{2,1,0:T(8,128)(2,1)S(1)}, bf16[8,128,128]{2,1,0:T(8,128)(2,1)S(1)}, u32[]{:S(2)}, u32[]{:S(2)}) %collective-permute-start.26) | collective-permute-done | bytes 262176 | tf_op jit(solution)/shard_map/ppermute | solution.py:258
  68.4 4.3 %collective-permute-done.23 = bf16[8,128,128]{2,1,0:T(8,128)(2,1)S(1)} collective-permute-done((bf16[8,128,128]{2,1,0:T(8,128)(2,1)S(1)}, bf16[8,128,128]{2,1,0:T(8,128)(2,1)S(1)}, u32[]{:S(2)}, u32[]{:S(2)}) %collective-permute-start.23) | collective-permute-done | bytes 262176 | tf_op jit(solution)/shard_map/ppermute | solution.py:258
  72.8 4.3 %collective-permute-start.32 = (bf16[8,128,128]{2,1,0:T(8,128)(2,1)S(1)}, bf16[8,128,128]{2,1,0:T(8,128)(2,1)S(1)}, u32[]{:S(2)}, u32[]{:S(2)}) collective-permute-start(bf16[8,128,128]{2,1,0:T(8,128)(2,1)S(1)} %add_convert_fusion), channel_id=1, source_target_pairs={{0,0},{1,1},{2,16},{3,17},{4,8},{5,9},{6,24},{7,25},{8,20},{9,21},... | collective-permute-start | bytes 786440 | tf_op jit(solution)/shard_map/ppermute | solution.py:258
  77.2 3.7 %collective-permute-start.24 = (bf16[8,128,128]{2,1,0:T(8,128)(2,1)S(1)}, bf16[8,128,128]{2,1,0:T(8,128)(2,1)S(1)}, u32[]{:S(2)}, u32[]{:S(2)}) collective-permute-start(bf16[8,128,128]{2,1,0:T(8,128)(2,1)S(1)} %add_convert_fusion), channel_id=1, source_target_pairs={{0,0},{1,1},{2,2},{3,3},{4,4},{5,5},{6,6},{7,7},{8,10},{9,11},{10,... | collective-permute-start | bytes 786440 | tf_op jit(solution)/shard_map/ppermute | solution.py:258
  81.5 2.5 %collective-permute-done.32.refs_8_ = bf16[8,128,128]{2,1,0:T(8,128)(2,1)S(1)} collective-permute-done((bf16[8,128,128]{2,1,0:T(8,128)(2,1)S(1)}, bf16[8,128,128]{2,1,0:T(8,128)(2,1)S(1)}, u32[]{:S(2)}, u32[]{:S(2)}) %collective-permute-start.32) | collective-permute-done | bytes 262176 | tf_op jit(solution)/shard_map/ppermute | solution.py:258
  84.0 4.7 %collective-permute-done.24.own_ref = bf16[8,128,128]{2,1,0:T(8,128)(2,1)S(1)} collective-permute-done((bf16[8,128,128]{2,1,0:T(8,128)(2,1)S(1)}, bf16[8,128,128]{2,1,0:T(8,128)(2,1)S(1)}, u32[]{:S(2)}, u32[]{:S(2)}) %collective-permute-start.24) | collective-permute-done | bytes 262176 | tf_op jit(solution)/shard_map/ppermute | solution.py:258
  88.7 2.3 %commutator_product.1 = (f32[8,128,128]{2,1,0:T(8,128)S(1)}, bf16[1040,128]{1,0:T(8,128)(2,1)S(1)}, bf16[1040,128]{1,0:T(8,128)(2,1)S(1)}, bf16[1040,128]{1,0:T(8,128)(2,1)S(1)}, bf16[16,128]{1,0:T(8,128)(2,1)S(1)}) custom-call(s32[136]{0:T(256)S(1)} %pad_add_fusion.index_ref, bf16[8,128,128]{2,1,0:T(8,128)(2,1)S(1)} %collective-permute-done.24.own_ref, ...), custom_call_target="tpu_custom_call" | custom-call | flops 268435456 | bytes 4194304 | tf_op jit(solution)/shard_map/commutator_product/pallas_call | solution.py:386
  95.9 3.2 %collective-permute-done.34.refs_0_ = bf16[1040,128]{1,0:T(8,128)(2,1)S(1)} collective-permute-done((bf16[1040,128]{1,0:T(8,128)(2,1)S(1)}, bf16[1040,128]{1,0:T(8,128)(2,1)S(1)}, u32[]{:S(2)}, u32[]{:S(2)}) %collective-permute-start.34) | collective-permute-done | bytes 266272 | tf_op jit(solution)/shard_map/ppermute | solution.py:258
  99.2 2.7 %collective-permute-done.35.refs_1_ = bf16[1040,128]{1,0:T(8,128)(2,1)S(1)} collective-permute-done((bf16[1040,128]{1,0:T(8,128)(2,1)S(1)}, bf16[1040,128]{1,0:T(8,128)(2,1)S(1)}, u32[]{:S(2)}, u32[]{:S(2)}) %collective-permute-start.35) | collective-permute-done | bytes 266272 | tf_op jit(solution)/shard_map/ppermute | solution.py:258
  101.8 6.1 %collective-permute-done.36.refs_2_ = bf16[1040,128]{1,0:T(8,128)(2,1)S(1)} collective-permute-done((bf16[1040,128]{1,0:T(8,128)(2,1)S(1)}, bf16[1040,128]{1,0:T(8,128)(2,1)S(1)}, u32[]{:S(2)}, u32[]{:S(2)}) %collective-permute-start.36) | collective-permute-done | bytes 266272 | tf_op jit(solution)/shard_map/ppermute | solution.py:258
  110.2 3.4 %collective-permute-start.37 = (bf16[1040,128]{1,0:T(8,128)(2,1)S(1)}, bf16[1040,128]{1,0:T(8,128)(2,1)S(1)}, u32[]{:S(2)}, u32[]{:S(2)}) collective-permute-start(bf16[1040,128]{1,0:T(8,128)(2,1)S(1)} %plane_sum.1), channel_id=1, source_target_pairs={{0,0},{1,1},{2,2},{3,3},{4,4},{5,5},{6,6},{7,7},{8,10},{9,11},{10,... | collective-permute-start | bytes 798728 | tf_op jit(solution)/shard_map/ppermute | solution.py:258
  113.6 4.0 %collective-permute-done.38.refs_0_ = bf16[1040,128]{1,0:T(8,128)(2,1)S(1)} collective-permute-done((bf16[1040,128]{1,0:T(8,128)(2,1)S(1)}, bf16[1040,128]{1,0:T(8,128)(2,1)S(1)}, u32[]{:S(2)}, u32[]{:S(2)}) %collective-permute-start.38) | collective-permute-done | bytes 266272 | tf_op jit(solution)/shard_map/ppermute | solution.py:258
  117.7 2.8 %collective-permute-done.37.own_ref = bf16[1040,128]{1,0:T(8,128)(2,1)S(1)} collective-permute-done((bf16[1040,128]{1,0:T(8,128)(2,1)S(1)}, bf16[1040,128]{1,0:T(8,128)(2,1)S(1)}, u32[]{:S(2)}, u32[]{:S(2)}) %collective-permute-start.37) | collective-permute-done | bytes 266272 | tf_op jit(solution)/shard_map/ppermute | solution.py:258
  122.0 6.8 %collective-permute-start.41 = (f32[8,128]{1,0:T(8,128)S(1)}, f32[8,128]{1,0:T(8,128)S(1)}, u32[]{:S(2)}, u32[]{:S(2)}) collective-permute-start(f32[8,128]{1,0:T(8,128)S(1)} %fusion.4), channel_id=1, source_target_pairs={{0,4},{1,5},{2,6},{3,7},{4,0},{5,1},{6,2},{7,3},{8,12},{9,13},{10,... | collective-permute-start | bytes 12296 | tf_op jit(solution)/shard_map/ppermute | solution.py:258
  128.9 3.0 %collective-permute-start.42 = (f32[8,128]{1,0:T(8,128)S(1)}, f32[8,128]{1,0:T(8,128)S(1)}, u32[]{:S(2)}, u32[]{:S(2)}) collective-permute-start(f32[8,128]{1,0:T(8,128)S(1)} %fusion.4), channel_id=1, source_target_pairs={{0,2},{1,3},{2,0},{3,1},{4,6},{5,7},{6,4},{7,5},{8,10},{9,11},{10,... | collective-permute-start | bytes 12296 | tf_op jit(solution)/shard_map/ppermute | solution.py:258
  133.5 2.9 %collective-permute-done.43 = f32[8,128]{1,0:T(8,128)S(1)} collective-permute-done((f32[8,128]{1,0:T(8,128)S(1)}, f32[8,128]{1,0:T(8,128)S(1)}, u32[]{:S(2)}, u32[]{:S(2)}) %collective-permute-start.43) | collective-permute-done | bytes 4128 | tf_op jit(solution)/shard_map/ppermute | solution.py:258
  (129 shorter events, 46.8 us)
Async XLA Ops:
  0.6 15.8 %collective-permute-start.2 = (bf16[8,128,128]{2,1,0:T(8,128)(2,1)}, bf16[8,128,128]{2,1,0:T(8,128)(2,1)S(1)}, u32[]{:S(2)}, u32[]{:S(2)}) collective-permute-start(bf16[8,128,128]{2,1,0:T(8,128)(2,1)} %bitcast.32), channel_id=1, source_target_pairs={{0,16},{1,20},{2,18},{3,22},{4,17},{5,21},{6,19},{7,23},{8,24},{9,... | collective-permute-start | bytes 786440 | tf_op jit(solution)/shard_map/ppermute | solution.py:258
  1.0 15.4 %collective-permute-start.1 = (bf16[8,128,128]{2,1,0:T(8,128)(2,1)}, bf16[8,128,128]{2,1,0:T(8,128)(2,1)S(1)}, u32[]{:S(2)}, u32[]{:S(2)}) collective-permute-start(bf16[8,128,128]{2,1,0:T(8,128)(2,1)} %bitcast.33), channel_id=1, source_target_pairs={{0,8},{1,12},{2,10},{3,14},{4,9},{5,13},{6,11},{7,15},{8,0},{9,4},... | collective-permute-start | bytes 786440 | tf_op jit(solution)/shard_map/ppermute | solution.py:258
  1.5 21.5 %collective-permute-start.7 = (bf16[8,128,128]{2,1,0:T(8,128)(2,1)}, bf16[8,128,128]{2,1,0:T(8,128)(2,1)S(1)}, u32[]{:S(2)}, u32[]{:S(2)}) collective-permute-start(bf16[8,128,128]{2,1,0:T(8,128)(2,1)} %bitcast.34), channel_id=1, source_target_pairs={{0,0},{1,4},{2,2},{3,6},{4,1},{5,5},{6,3},{7,7},{8,8},{9,12},{10,1... | collective-permute-start | bytes 786440 | tf_op jit(solution)/shard_map/ppermute | solution.py:258
  3.1 17.3 %collective-permute-start = (bf16[8,128,128]{2,1,0:T(8,128)(2,1)}, bf16[8,128,128]{2,1,0:T(8,128)(2,1)S(1)}, u32[]{:S(2)}, u32[]{:S(2)}) collective-permute-start(bf16[8,128,128]{2,1,0:T(8,128)(2,1)} %bitcast.10), channel_id=1, source_target_pairs={{0,0},{1,4},{2,2},{3,6},{4,1},{5,5},{6,3},{7,7},{8,8},{9,12},{10,1... | collective-permute-start | bytes 786440 | tf_op jit(solution)/shard_map/ppermute | solution.py:258
  4.7 21.3 %collective-permute-start.6 = (bf16[8,128,128]{2,1,0:T(8,128)(2,1)}, bf16[8,128,128]{2,1,0:T(8,128)(2,1)S(1)}, u32[]{:S(2)}, u32[]{:S(2)}) collective-permute-start(bf16[8,128,128]{2,1,0:T(8,128)(2,1)} %bitcast.35), channel_id=1, source_target_pairs={{0,0},{1,4},{2,2},{3,6},{4,1},{5,5},{6,3},{7,7},{8,8},{9,12},{10,1... | collective-permute-start | bytes 786440 | tf_op jit(solution)/shard_map/ppermute | solution.py:258
  16.5 10.2 %collective-permute-start.10 = (bf16[8,128,128]{2,1,0:T(8,128)(2,1)S(1)}, bf16[8,128,128]{2,1,0:T(8,128)(2,1)S(1)}, u32[]{:S(2)}, u32[]{:S(2)}) collective-permute-start(bf16[8,128,128]{2,1,0:T(8,128)(2,1)S(1)} %collective-permute-done.2.refs_2_), channel_id=1, source_target_pairs={{0,1},{1,0},{2,3},{3,2},{4,5},{5,4},{6,7},{7,6},{8,9},{9,8},{10,11... | collective-permute-start | bytes 786440 | tf_op jit(solution)/shard_map/ppermute | solution.py:258
  20.4 15.3 %collective-permute-start.5 = (bf16[8,128,128]{2,1,0:T(8,128)(2,1)}, bf16[8,128,128]{2,1,0:T(8,128)(2,1)S(1)}, u32[]{:S(2)}, u32[]{:S(2)}) collective-permute-start(bf16[8,128,128]{2,1,0:T(8,128)(2,1)} %bitcast.10), channel_id=1, source_target_pairs={{0,16},{1,20},{2,18},{3,22},{4,17},{5,21},{6,19},{7,23},{8,24},{9,... | collective-permute-start | bytes 786440 | tf_op jit(solution)/shard_map/ppermute | solution.py:258
  28.8 12.5 %collective-permute-start.4 = (bf16[8,128,128]{2,1,0:T(8,128)(2,1)S(1)}, bf16[8,128,128]{2,1,0:T(8,128)(2,1)S(1)}, u32[]{:S(2)}, u32[]{:S(2)}) collective-permute-start(bf16[8,128,128]{2,1,0:T(8,128)(2,1)S(1)} %collective-permute-done.refs_0_), channel_id=1, source_target_pairs={{0,8},{1,9},{2,10},{3,11},{4,12},{5,13},{6,14},{7,15},{8,0},{9,1},... | collective-permute-start | bytes 786440 | tf_op jit(solution)/shard_map/ppermute | solution.py:258
  35.7 10.6 %collective-permute-start.13 = (bf16[8,128,128]{2,1,0:T(8,128)(2,1)S(1)}, bf16[8,128,128]{2,1,0:T(8,128)(2,1)S(1)}, u32[]{:S(2)}, u32[]{:S(2)}) collective-permute-start(bf16[8,128,128]{2,1,0:T(8,128)(2,1)S(1)} %collective-permute-done.5.refs_2_), channel_id=1, source_target_pairs={{0,8},{1,9},{2,10},{3,11},{4,12},{5,13},{6,14},{7,15},{8,0},{9,1},... | collective-permute-start | bytes 786440 | tf_op jit(solution)/shard_map/ppermute | solution.py:258
  35.7 10.6 %collective-permute-start.14 = (bf16[8,128,128]{2,1,0:T(8,128)(2,1)S(1)}, bf16[8,128,128]{2,1,0:T(8,128)(2,1)S(1)}, u32[]{:S(2)}, u32[]{:S(2)}) collective-permute-start(bf16[8,128,128]{2,1,0:T(8,128)(2,1)S(1)} %get-tuple-element.36), channel_id=1, source_target_pairs={{0,4},{1,5},{2,6},{3,7},{4,0},{5,1},{6,2},{7,3},{8,12},{9,13},{10,... | collective-permute-start | bytes 786440 | tf_op jit(solution)/shard_map/ppermute | solution.py:258
  39.2 12.5 %collective-permute-start.16 = (bf16[8,128,128]{2,1,0:T(8,128)(2,1)S(1)}, bf16[8,128,128]{2,1,0:T(8,128)(2,1)S(1)}, u32[]{:S(2)}, u32[]{:S(2)}) collective-permute-start(bf16[8,128,128]{2,1,0:T(8,128)(2,1)S(1)} %get-tuple-element.38), channel_id=1, source_target_pairs={{0,6},{1,7},{2,4},{3,5},{4,2},{5,3},{6,0},{7,1},{8,14},{9,15},{10,... | collective-permute-start | bytes 786440 | tf_op jit(solution)/shard_map/ppermute | solution.py:258
  41.2 12.5 %collective-permute-start.17 = (bf16[8,128,128]{2,1,0:T(8,128)(2,1)S(1)}, bf16[8,128,128]{2,1,0:T(8,128)(2,1)S(1)}, u32[]{:S(2)}, u32[]{:S(2)}) collective-permute-start(bf16[8,128,128]{2,1,0:T(8,128)(2,1)S(1)} %collective-permute-done.refs_0_), channel_id=1, source_target_pairs={{0,1},{1,0},{2,3},{3,2},{4,5},{5,4},{6,7},{7,6},{8,9},{9,8},{10,11... | collective-permute-start | bytes 786440 | tf_op jit(solution)/shard_map/ppermute | solution.py:258
  53.3 14.8 %collective-permute-start.26 = (bf16[8,128,128]{2,1,0:T(8,128)(2,1)S(1)}, bf16[8,128,128]{2,1,0:T(8,128)(2,1)S(1)}, u32[]{:S(2)}, u32[]{:S(2)}) collective-permute-start(bf16[8,128,128]{2,1,0:T(8,128)(2,1)S(1)} %collective-permute-done.12.refs_8_.refs_0_), channel_id=1, source_target_pairs={{0,16},{1,17},{2,18},{3,19},{4,20},{5,21},{6,22},{7,23},{8,24},{9,... | collective-permute-start | bytes 786440 | tf_op jit(solution)/shard_map/ppermute | solution.py:258
  56.9 11.2 %collective-permute-start.21 = (bf16[8,128,128]{2,1,0:T(8,128)(2,1)S(1)}, bf16[8,128,128]{2,1,0:T(8,128)(2,1)S(1)}, u32[]{:S(2)}, u32[]{:S(2)}) collective-permute-start(bf16[8,128,128]{2,1,0:T(8,128)(2,1)S(1)} %get-tuple-element.44), channel_id=1, source_target_pairs={{0,4},{1,5},{2,6},{3,7},{4,0},{5,1},{6,2},{7,3},{8,12},{9,13},{10,... | collective-permute-start | bytes 786440 | tf_op jit(solution)/shard_map/ppermute | solution.py:258
  59.7 12.9 %collective-permute-start.23 = (bf16[8,128,128]{2,1,0:T(8,128)(2,1)S(1)}, bf16[8,128,128]{2,1,0:T(8,128)(2,1)S(1)}, u32[]{:S(2)}, u32[]{:S(2)}) collective-permute-start(bf16[8,128,128]{2,1,0:T(8,128)(2,1)S(1)} %get-tuple-element.46), channel_id=1, source_target_pairs={{0,6},{1,7},{2,4},{3,5},{4,2},{5,3},{6,0},{7,1},{8,14},{9,15},{10,... | collective-permute-start | bytes 786440 | tf_op jit(solution)/shard_map/ppermute | solution.py:258
  60.7 16.5 %collective-permute-start.25 = (bf16[8,128,128]{2,1,0:T(8,128)(2,1)S(1)}, bf16[8,128,128]{2,1,0:T(8,128)(2,1)S(1)}, u32[]{:S(2)}, u32[]{:S(2)}) collective-permute-start(bf16[8,128,128]{2,1,0:T(8,128)(2,1)S(1)} %collective-permute-done.12.refs_8_.refs_0_), channel_id=1, source_target_pairs={{0,8},{1,9},{2,10},{3,11},{4,12},{5,13},{6,14},{7,15},{8,0},{9,1},... | collective-permute-start | bytes 786440 | tf_op jit(solution)/shard_map/ppermute | solution.py:258
  68.1 13.0 %collective-permute-start.28 = (bf16[8,128,128]{2,1,0:T(8,128)(2,1)S(1)}, bf16[8,128,128]{2,1,0:T(8,128)(2,1)S(1)}, u32[]{:S(2)}, u32[]{:S(2)}) collective-permute-start(bf16[8,128,128]{2,1,0:T(8,128)(2,1)S(1)} %collective-permute-done.12.refs_8_.refs_0_), channel_id=1, source_target_pairs={{0,1},{1,0},{2,3},{3,2},{4,5},{5,4},{6,7},{7,6},{8,9},{9,8},{10,11... | collective-permute-start | bytes 786440 | tf_op jit(solution)/shard_map/ppermute | solution.py:258
  68.1 12.8 %collective-permute-start.27 = (bf16[8,128,128]{2,1,0:T(8,128)(2,1)S(1)}, bf16[8,128,128]{2,1,0:T(8,128)(2,1)S(1)}, u32[]{:S(2)}, u32[]{:S(2)}) collective-permute-start(bf16[8,128,128]{2,1,0:T(8,128)(2,1)S(1)} %collective-permute-done.26.refs_2_), channel_id=1, source_target_pairs={{0,8},{1,9},{2,10},{3,11},{4,12},{5,13},{6,14},{7,15},{8,0},{9,1},... | collective-permute-start | bytes 786440 | tf_op jit(solution)/shard_map/ppermute | solution.py:258
  72.8 11.2 %collective-permute-start.32 = (bf16[8,128,128]{2,1,0:T(8,128)(2,1)S(1)}, bf16[8,128,128]{2,1,0:T(8,128)(2,1)S(1)}, u32[]{:S(2)}, u32[]{:S(2)}) collective-permute-start(bf16[8,128,128]{2,1,0:T(8,128)(2,1)S(1)} %add_convert_fusion), channel_id=1, source_target_pairs={{0,0},{1,1},{2,16},{3,17},{4,8},{5,9},{6,24},{7,25},{8,20},{9,21},... | collective-permute-start | bytes 786440 | tf_op jit(solution)/shard_map/ppermute | solution.py:258
  77.2 11.5 %collective-permute-start.24 = (bf16[8,128,128]{2,1,0:T(8,128)(2,1)S(1)}, bf16[8,128,128]{2,1,0:T(8,128)(2,1)S(1)}, u32[]{:S(2)}, u32[]{:S(2)}) collective-permute-start(bf16[8,128,128]{2,1,0:T(8,128)(2,1)S(1)} %add_convert_fusion), channel_id=1, source_target_pairs={{0,0},{1,1},{2,2},{3,3},{4,4},{5,5},{6,6},{7,7},{8,10},{9,11},{10,... | collective-permute-start | bytes 786440 | tf_op jit(solution)/shard_map/ppermute | solution.py:258
  94.5 13.4 %collective-permute-start.36 = (bf16[1040,128]{1,0:T(8,128)(2,1)S(1)}, bf16[1040,128]{1,0:T(8,128)(2,1)S(1)}, u32[]{:S(2)}, u32[]{:S(2)}) collective-permute-start(bf16[1040,128]{1,0:T(8,128)(2,1)S(1)} %get-tuple-element.55), channel_id=1, source_target_pairs={{0,6},{1,7},{2,4},{3,5},{4,2},{5,3},{6,0},{7,1},{8,14},{9,15},{10,... | collective-permute-start | bytes 798728 | tf_op jit(solution)/shard_map/ppermute | solution.py:258
  110.2 10.3 %collective-permute-start.37 = (bf16[1040,128]{1,0:T(8,128)(2,1)S(1)}, bf16[1040,128]{1,0:T(8,128)(2,1)S(1)}, u32[]{:S(2)}, u32[]{:S(2)}) collective-permute-start(bf16[1040,128]{1,0:T(8,128)(2,1)S(1)} %plane_sum.1), channel_id=1, source_target_pairs={{0,0},{1,1},{2,2},{3,3},{4,4},{5,5},{6,6},{7,7},{8,10},{9,11},{10,... | collective-permute-start | bytes 798728 | tf_op jit(solution)/shard_map/ppermute | solution.py:258
  121.3 16.3 %collective-permute-start.40 = (bf16[8,128,128]{2,1,0:T(8,128)(2,1)S(1)}, bf16[8,128,128]{2,1,0:T(8,128)(2,1)S(1)}, u32[]{:S(2)}, u32[]{:S(2)}) collective-permute-start(bf16[8,128,128]{2,1,0:T(8,128)(2,1)S(1)} %commutator_difference.1), channel_id=1, source_target_pairs={{0,0},{1,4},{2,2},{3,6},{4,1},{5,5},{6,3},{7,7},{8,8},{9,12},{10,1... | collective-permute-start | bytes 786440 | tf_op jit(solution)/shard_map/ppermute | solution.py:258
  122.0 11.1 %collective-permute-start.41 = (f32[8,128]{1,0:T(8,128)S(1)}, f32[8,128]{1,0:T(8,128)S(1)}, u32[]{:S(2)}, u32[]{:S(2)}) collective-permute-start(f32[8,128]{1,0:T(8,128)S(1)} %fusion.4), channel_id=1, source_target_pairs={{0,4},{1,5},{2,6},{3,7},{4,0},{5,1},{6,2},{7,3},{8,12},{9,13},{10,... | collective-permute-start | bytes 12296 | tf_op jit(solution)/shard_map/ppermute | solution.py:258
  (22 other events, 121.3 us)

commit v3 on v1

--- a/solution.py
+++ b/solution.py
@@ -282,8 +282,7 @@
         return [pieces[m] for m in range(outer)] + [shared[m] for m in range(outer)]
 
     def mirror(x, target):
-        moved = inside_permute(x, lambda o, h, g: (g, h, o), inside_spread, target)
-        return [moved, share(moved)]
+        return inside_permute(x, lambda o, h, g: (g, h, o), inside_spread, target)
 
     def exchange(outs):
         return [outs[0]] + [
@@ -379,7 +378,8 @@
     second_outs = outs
     total = total_of(exchange(outs))
 
-    mirrored = mirror(total, at)
+    mirrored = [mirror(total, at)]
+    mirrored.append(share(mirrored[0]))
     own = inside_permute(total, lambda o, h, g: (o, h, g), inside_spread)
     kohn_pieces = {0: kohn_own} | after(kohn_pieces, second_outs)
     kohn_beside = share_all(kohn_pieces)
@@ -414,7 +414,15 @@
         compiler_params=params,
         name="plane_sum",
     )(trace, own, *parts)
-    mirrored = mirror(total, at_spread)
+    mirrored = [mirror(total, at_spread)]
+
+    trace = one_part(total[blocks * side :])
+    trace = trace + share(trace)
+    step = 1
+    while step < outer:
+        trace = trace + to_plane(trace, step)
+        step *= 2
+    mirrored.append(share(after(mirrored[0], trace)))
 
     commutator = pl.pallas_call(
         functools.partial(last_kernel, inner, blocks, last_mirror_at),
@@ -435,14 +443,6 @@
         commutator, lambda o, h, g: (o, h, g), inside_spread, lambda o, h, g: (o * inner + h, g)
     )
 
-    plane_trace = tree_sum([one_part(piece[blocks * side :]) for piece in mirrored])
-    trace = tree_sum(
-        [plane_trace]
-        + [
-            inside_permute(plane_trace, lambda o, h, g, d=d: (o, h, g ^ d))
-            for d in range(1, n_col)
-        ]
-    )
     trace_value = trace.sum() / (blocks_total * side * side)
     return commutator.reshape(step_dir.shape), trace_value
 

time: 136 us -> 140 us (1.029)
  waiting for transfers between devices: 66.2 us -> 69.4 us
    ppermute x43, waiting for transfers between devices: 66.2 us -> 69.4 us  [permute(): return lax.ppermute(x, ('row', 'col'), row_major_perm(n_row, n_col, target))]
  transfers between devices with their start and end apart: 43 -> 43, of which waited for: 17 -> 16; matrix products, arithmetic and copies ran while one was open for 7% -> 7% of each run, Pallas kernels for 3% -> 3%
where the time goes in v3:
time: 140 us; the launch traced here: 137 us
  waiting for transfers between devices  69.4 us (50%)
  starting transfers between devices  46.4 us (33%)
  Pallas kernels  7.81 us (6%)
  local copies, waits for them, and re-layouts  7.35 us (5%)
  other arithmetic  3.75 us (3%)
  between operations  2.79 us (2%)
    ppermute x43, waiting for transfers between devices, permute(): return lax.ppermute(x, ('row', 'col'), row_major_perm(n_row, n_col, target))  69.4 us
    ppermute x43, starting transfers between devices, permute(): return lax.ppermute(x, ('row', 'col'), row_major_perm(n_row, n_col, target))  46.4 us
  transfers between devices with their start and end apart: 43, of which 16 were waited for; matrix products, arithmetic and copies ran while one was open for 7% of the time, Pallas kernels for 3%

profile of v3, /device:TPU:26, one launch (start us, length us, event | category | flops | bytes accessed | tf_op | source)
XLA Modules:
  0.0 137.4 jit_solution(7588363262938302827)
XLA Ops:
  13.6 2.9 %collective-permute-done.2.refs_2_ = bf16[8,128,128]{2,1,0:T(8,128)(2,1)S(1)} collective-permute-done((bf16[8,128,128]{2,1,0:T(8,128)(2,1)}, bf16[8,128,128]{2,1,0:T(8,128)(2,1)S(1)}, u32[]{:S(2)}, u32[]{:S(2)}) %collective-permute-start.2) | collective-permute-done | bytes 262176 | tf_op jit(solution)/shard_map/ppermute | solution.py:261
  16.5 3.5 %collective-permute-start.10 = (bf16[8,128,128]{2,1,0:T(8,128)(2,1)S(1)}, bf16[8,128,128]{2,1,0:T(8,128)(2,1)S(1)}, u32[]{:S(2)}, u32[]{:S(2)}) collective-permute-start(bf16[8,128,128]{2,1,0:T(8,128)(2,1)S(1)} %collective-permute-done.2.refs_2_), channel_id=1, source_target_pairs={{0,1},{1,0},{2,3},{3,2},{4,5},{5,4},{6,7},{7,6},{8,9},{9,8},{10,11... | collective-permute-start | bytes 786440 | tf_op jit(solution)/shard_map/ppermute | solution.py:261
  21.9 2.6 %collective-permute-start.5 = (bf16[8,128,128]{2,1,0:T(8,128)(2,1)S(1)}, bf16[8,128,128]{2,1,0:T(8,128)(2,1)S(1)}, u32[]{:S(2)}, u32[]{:S(2)}) collective-permute-start(bf16[8,128,128]{2,1,0:T(8,128)(2,1)S(1)} %collective-permute-done.refs_0_), channel_id=1, source_target_pairs={{0,16},{1,17},{2,18},{3,19},{4,20},{5,21},{6,22},{7,23},{8,24},{9,... | collective-permute-start | bytes 786440 | tf_op jit(solution)/shard_map/ppermute | solution.py:261
  29.5 2.2 %scaled_step_product.1 = (f32[8,128,128]{2,1,0:T(8,128)S(1)}, bf16[8,128,128]{2,1,0:T(8,128)(2,1)S(1)}, bf16[8,128,128]{2,1,0:T(8,128)(2,1)S(1)}, bf16[8,128,128]{2,1,0:T(8,128)(2,1)S(1)}) custom-call(s32[144]{0:T(256)S(1)} %pad_add_fusion.index_ref, bf16[8,128,128]{2,1,0:T(8,128)(2,1)S(1)} %collective-permute-done.6.left_ref, ...), custom_call_target="tpu_custom_call" | custom-call | flops 268435456 | bytes 4194304 | tf_op jit(solution)/shard_map/scaled_step_product/pallas_call | solution.py:342
  31.6 5.1 %collective-permute-done.5.refs_2_ = bf16[8,128,128]{2,1,0:T(8,128)(2,1)S(1)} collective-permute-done((bf16[8,128,128]{2,1,0:T(8,128)(2,1)S(1)}, bf16[8,128,128]{2,1,0:T(8,128)(2,1)S(1)}, u32[]{:S(2)}, u32[]{:S(2)}) %collective-permute-start.5) | collective-permute-done | bytes 262176 | tf_op jit(solution)/shard_map/ppermute | solution.py:261
  40.2 2.1 %collective-permute-done.4.refs_1_ = bf16[8,128,128]{2,1,0:T(8,128)(2,1)S(1)} collective-permute-done((bf16[8,128,128]{2,1,0:T(8,128)(2,1)S(1)}, bf16[8,128,128]{2,1,0:T(8,128)(2,1)S(1)}, u32[]{:S(2)}, u32[]{:S(2)}) %collective-permute-start.4) | collective-permute-done | bytes 262176 | tf_op jit(solution)/shard_map/ppermute | solution.py:261
  42.4 5.1 %collective-permute-done.13.refs_3_ = bf16[8,128,128]{2,1,0:T(8,128)(2,1)S(1)} collective-permute-done((bf16[8,128,128]{2,1,0:T(8,128)(2,1)S(1)}, bf16[8,128,128]{2,1,0:T(8,128)(2,1)S(1)}, u32[]{:S(2)}, u32[]{:S(2)}) %collective-permute-start.13) | collective-permute-done | bytes 262176 | tf_op jit(solution)/shard_map/ppermute | solution.py:261
  47.5 4.1 %collective-permute-done.16.refs_11_ = bf16[8,128,128]{2,1,0:T(8,128)(2,1)S(1)} collective-permute-done((bf16[8,128,128]{2,1,0:T(8,128)(2,1)S(1)}, bf16[8,128,128]{2,1,0:T(8,128)(2,1)S(1)}, u32[]{:S(2)}, u32[]{:S(2)}) %collective-permute-start.16) | collective-permute-done | bytes 262176 | tf_op jit(solution)/shard_map/ppermute | solution.py:261
  52.1 2.0 %collective-permute-start.26 = (bf16[8,128,128]{2,1,0:T(8,128)(2,1)S(1)}, bf16[8,128,128]{2,1,0:T(8,128)(2,1)S(1)}, u32[]{:S(2)}, u32[]{:S(2)}) collective-permute-start(bf16[8,128,128]{2,1,0:T(8,128)(2,1)S(1)} %collective-permute-done.12.refs_8_.refs_0_), channel_id=1, source_target_pairs={{0,16},{1,17},{2,18},{3,19},{4,20},{5,21},{6,22},{7,23},{8,24},{9,... | collective-permute-start | bytes 786440 | tf_op jit(solution)/shard_map/ppermute | solution.py:261
  54.2 2.3 %change_product.1 = (f32[8,128,128]{2,1,0:T(8,128)S(1)}, bf16[8,128,128]{2,1,0:T(8,128)(2,1)S(1)}, bf16[8,128,128]{2,1,0:T(8,128)(2,1)S(1)}, bf16[8,128,128]{2,1,0:T(8,128)(2,1)S(1)}) custom-call(s32[144]{0:T(256)S(1)} %pad_add_fusion.index_ref, bf16[8,128,128]{2,1,0:T(8,128)(2,1)S(1)} %collective-permute-done.refs_0_, ...), custom_call_target="tpu_custom_call" | custom-call | flops 268435456 | bytes 4194304 | tf_op jit(solution)/shard_map/change_product/pallas_call | solution.py:361
  61.3 6.1 %collective-permute-done.26.refs_2_ = bf16[8,128,128]{2,1,0:T(8,128)(2,1)S(1)} collective-permute-done((bf16[8,128,128]{2,1,0:T(8,128)(2,1)S(1)}, bf16[8,128,128]{2,1,0:T(8,128)(2,1)S(1)}, u32[]{:S(2)}, u32[]{:S(2)}) %collective-permute-start.26) | collective-permute-done | bytes 262176 | tf_op jit(solution)/shard_map/ppermute | solution.py:261
  67.5 4.3 %collective-permute-done.23 = bf16[8,128,128]{2,1,0:T(8,128)(2,1)S(1)} collective-permute-done((bf16[8,128,128]{2,1,0:T(8,128)(2,1)S(1)}, bf16[8,128,128]{2,1,0:T(8,128)(2,1)S(1)}, u32[]{:S(2)}, u32[]{:S(2)}) %collective-permute-start.23) | collective-permute-done | bytes 262176 | tf_op jit(solution)/shard_map/ppermute | solution.py:261
  71.9 4.3 %collective-permute-start.32 = (bf16[8,128,128]{2,1,0:T(8,128)(2,1)S(1)}, bf16[8,128,128]{2,1,0:T(8,128)(2,1)S(1)}, u32[]{:S(2)}, u32[]{:S(2)}) collective-permute-start(bf16[8,128,128]{2,1,0:T(8,128)(2,1)S(1)} %add_convert_fusion), channel_id=1, source_target_pairs={{0,0},{1,1},{2,16},{3,17},{4,8},{5,9},{6,24},{7,25},{8,20},{9,21},... | collective-permute-start | bytes 786440 | tf_op jit(solution)/shard_map/ppermute | solution.py:261
  76.3 2.7 %collective-permute-start.24 = (bf16[8,128,128]{2,1,0:T(8,128)(2,1)S(1)}, bf16[8,128,128]{2,1,0:T(8,128)(2,1)S(1)}, u32[]{:S(2)}, u32[]{:S(2)}) collective-permute-start(bf16[8,128,128]{2,1,0:T(8,128)(2,1)S(1)} %add_convert_fusion), channel_id=1, source_target_pairs={{0,0},{1,1},{2,2},{3,3},{4,4},{5,5},{6,6},{7,7},{8,10},{9,11},{10,... | collective-permute-start | bytes 786440 | tf_op jit(solution)/shard_map/ppermute | solution.py:261
  79.6 3.6 %collective-permute-done.32.refs_8_ = bf16[8,128,128]{2,1,0:T(8,128)(2,1)S(1)} collective-permute-done((bf16[8,128,128]{2,1,0:T(8,128)(2,1)S(1)}, bf16[8,128,128]{2,1,0:T(8,128)(2,1)S(1)}, u32[]{:S(2)}, u32[]{:S(2)}) %collective-permute-start.32) | collective-permute-done | bytes 262176 | tf_op jit(solution)/shard_map/ppermute | solution.py:261
  83.2 4.5 %collective-permute-done.24.own_ref = bf16[8,128,128]{2,1,0:T(8,128)(2,1)S(1)} collective-permute-done((bf16[8,128,128]{2,1,0:T(8,128)(2,1)S(1)}, bf16[8,128,128]{2,1,0:T(8,128)(2,1)S(1)}, u32[]{:S(2)}, u32[]{:S(2)}) %collective-permute-start.24) | collective-permute-done | bytes 262176 | tf_op jit(solution)/shard_map/ppermute | solution.py:261
  87.8 2.3 %commutator_product.1 = (f32[8,128,128]{2,1,0:T(8,128)S(1)}, bf16[1040,128]{1,0:T(8,128)(2,1)S(1)}, bf16[1040,128]{1,0:T(8,128)(2,1)S(1)}, bf16[1040,128]{1,0:T(8,128)(2,1)S(1)}, bf16[16,128]{1,0:T(8,128)(2,1)S(1)}) custom-call(s32[144]{0:T(256)S(1)} %pad_add_fusion.index_ref, bf16[8,128,128]{2,1,0:T(8,128)(2,1)S(1)} %collective-permute-done.24.own_ref, ...), custom_call_target="tpu_custom_call" | custom-call | flops 268435456 | bytes 4194304 | tf_op jit(solution)/shard_map/commutator_product/pallas_call | solution.py:389
  94.7 3.4 %collective-permute-done.34.refs_0_ = bf16[1040,128]{1,0:T(8,128)(2,1)S(1)} collective-permute-done((bf16[1040,128]{1,0:T(8,128)(2,1)S(1)}, bf16[1040,128]{1,0:T(8,128)(2,1)S(1)}, u32[]{:S(2)}, u32[]{:S(2)}) %collective-permute-start.34) | collective-permute-done | bytes 266272 | tf_op jit(solution)/shard_map/ppermute | solution.py:261
  98.1 2.5 %collective-permute-done.35.refs_1_ = bf16[1040,128]{1,0:T(8,128)(2,1)S(1)} collective-permute-done((bf16[1040,128]{1,0:T(8,128)(2,1)S(1)}, bf16[1040,128]{1,0:T(8,128)(2,1)S(1)}, u32[]{:S(2)}, u32[]{:S(2)}) %collective-permute-start.35) | collective-permute-done | bytes 266272 | tf_op jit(solution)/shard_map/ppermute | solution.py:261
  100.6 6.2 %collective-permute-done.36.refs_2_ = bf16[1040,128]{1,0:T(8,128)(2,1)S(1)} collective-permute-done((bf16[1040,128]{1,0:T(8,128)(2,1)S(1)}, bf16[1040,128]{1,0:T(8,128)(2,1)S(1)}, u32[]{:S(2)}, u32[]{:S(2)}) %collective-permute-start.36) | collective-permute-done | bytes 266272 | tf_op jit(solution)/shard_map/ppermute | solution.py:261
  109.1 3.1 %collective-permute-start.39 = (f32[8,128]{1,0:T(8,128)S(1)}, f32[8,128]{1,0:T(8,128)S(1)}, u32[]{:S(2)}, u32[]{:S(2)}) collective-permute-start(f32[8,128]{1,0:T(8,128)S(1)} %fusion.23), channel_id=1, source_target_pairs={{0,8},{1,9},{2,10},{3,11},{4,12},{5,13},{6,14},{7,15},{8,0},{9,1},... | collective-permute-start | bytes 12296 | tf_op jit(solution)/shard_map/ppermute | solution.py:261
  112.2 6.7 %collective-permute-done.39 = f32[8,128]{1,0:T(8,128)S(1)} collective-permute-done((f32[8,128]{1,0:T(8,128)S(1)}, f32[8,128]{1,0:T(8,128)S(1)}, u32[]{:S(2)}, u32[]{:S(2)}) %collective-permute-start.39) | collective-permute-done | bytes 4128 | tf_op jit(solution)/shard_map/ppermute | solution.py:261
  118.9 4.5 %collective-permute-done.40 = f32[8,128]{1,0:T(8,128)S(1)} collective-permute-done((f32[8,128]{1,0:T(8,128)S(1)}, f32[8,128]{1,0:T(8,128)S(1)}, u32[]{:S(2)}, u32[]{:S(2)}) %collective-permute-start.40) | collective-permute-done | bytes 4128 | tf_op jit(solution)/shard_map/ppermute | solution.py:261
  129.0 6.6 %collective-permute-done.42 = bf16[8,128,128]{2,1,0:T(8,128)(2,1)S(1)} collective-permute-done((bf16[8,128,128]{2,1,0:T(8,128)(2,1)S(1)}, bf16[8,128,128]{2,1,0:T(8,128)(2,1)S(1)}, u32[]{:S(2)}, u32[]{:S(2)}) %collective-permute-start.42) | collective-permute-done | bytes 262176 | tf_op jit(solution)/shard_map/ppermute | solution.py:261
  (137 shorter events, 42.0 us)
Async XLA Ops:
  0.6 15.8 %collective-permute-start.2 = (bf16[8,128,128]{2,1,0:T(8,128)(2,1)}, bf16[8,128,128]{2,1,0:T(8,128)(2,1)S(1)}, u32[]{:S(2)}, u32[]{:S(2)}) collective-permute-start(bf16[8,128,128]{2,1,0:T(8,128)(2,1)} %bitcast.58), channel_id=1, source_target_pairs={{0,16},{1,20},{2,18},{3,22},{4,17},{5,21},{6,19},{7,23},{8,24},{9,... | collective-permute-start | bytes 786440 | tf_op jit(solution)/shard_map/ppermute | solution.py:261
  1.0 15.4 %collective-permute-start.1 = (bf16[8,128,128]{2,1,0:T(8,128)(2,1)}, bf16[8,128,128]{2,1,0:T(8,128)(2,1)S(1)}, u32[]{:S(2)}, u32[]{:S(2)}) collective-permute-start(bf16[8,128,128]{2,1,0:T(8,128)(2,1)} %bitcast.59), channel_id=1, source_target_pairs={{0,8},{1,12},{2,10},{3,14},{4,9},{5,13},{6,11},{7,15},{8,0},{9,4},... | collective-permute-start | bytes 786440 | tf_op jit(solution)/shard_map/ppermute | solution.py:261
  1.5 23.0 %collective-permute-start.7 = (bf16[8,128,128]{2,1,0:T(8,128)(2,1)}, bf16[8,128,128]{2,1,0:T(8,128)(2,1)S(1)}, u32[]{:S(2)}, u32[]{:S(2)}) collective-permute-start(bf16[8,128,128]{2,1,0:T(8,128)(2,1)} %bitcast.60), channel_id=1, source_target_pairs={{0,0},{1,4},{2,2},{3,6},{4,1},{5,5},{6,3},{7,7},{8,8},{9,12},{10,1... | collective-permute-start | bytes 786440 | tf_op jit(solution)/shard_map/ppermute | solution.py:261
  3.1 18.8 %collective-permute-start = (bf16[8,128,128]{2,1,0:T(8,128)(2,1)}, bf16[8,128,128]{2,1,0:T(8,128)(2,1)S(1)}, u32[]{:S(2)}, u32[]{:S(2)}) collective-permute-start(bf16[8,128,128]{2,1,0:T(8,128)(2,1)} %bitcast.57), channel_id=1, source_target_pairs={{0,0},{1,4},{2,2},{3,6},{4,1},{5,5},{6,3},{7,7},{8,8},{9,12},{10,1... | collective-permute-start | bytes 786440 | tf_op jit(solution)/shard_map/ppermute | solution.py:261
  4.7 21.6 %collective-permute-start.6 = (bf16[8,128,128]{2,1,0:T(8,128)(2,1)}, bf16[8,128,128]{2,1,0:T(8,128)(2,1)S(1)}, u32[]{:S(2)}, u32[]{:S(2)}) collective-permute-start(bf16[8,128,128]{2,1,0:T(8,128)(2,1)} %bitcast.61), channel_id=1, source_target_pairs={{0,0},{1,4},{2,2},{3,6},{4,1},{5,5},{6,3},{7,7},{8,8},{9,12},{10,1... | collective-permute-start | bytes 786440 | tf_op jit(solution)/shard_map/ppermute | solution.py:261
  16.5 10.4 %collective-permute-start.10 = (bf16[8,128,128]{2,1,0:T(8,128)(2,1)S(1)}, bf16[8,128,128]{2,1,0:T(8,128)(2,1)S(1)}, u32[]{:S(2)}, u32[]{:S(2)}) collective-permute-start(bf16[8,128,128]{2,1,0:T(8,128)(2,1)S(1)} %collective-permute-done.2.refs_2_), channel_id=1, source_target_pairs={{0,1},{1,0},{2,3},{3,2},{4,5},{5,4},{6,7},{7,6},{8,9},{9,8},{10,11... | collective-permute-start | bytes 786440 | tf_op jit(solution)/shard_map/ppermute | solution.py:261
  21.9 14.8 %collective-permute-start.5 = (bf16[8,128,128]{2,1,0:T(8,128)(2,1)S(1)}, bf16[8,128,128]{2,1,0:T(8,128)(2,1)S(1)}, u32[]{:S(2)}, u32[]{:S(2)}) collective-permute-start(bf16[8,128,128]{2,1,0:T(8,128)(2,1)S(1)} %collective-permute-done.refs_0_), channel_id=1, source_target_pairs={{0,16},{1,17},{2,18},{3,19},{4,20},{5,21},{6,22},{7,23},{8,24},{9,... | collective-permute-start | bytes 786440 | tf_op jit(solution)/shard_map/ppermute | solution.py:261
  28.8 13.6 %collective-permute-start.4 = (bf16[8,128,128]{2,1,0:T(8,128)(2,1)S(1)}, bf16[8,128,128]{2,1,0:T(8,128)(2,1)S(1)}, u32[]{:S(2)}, u32[]{:S(2)}) collective-permute-start(bf16[8,128,128]{2,1,0:T(8,128)(2,1)S(1)} %collective-permute-done.refs_0_), channel_id=1, source_target_pairs={{0,8},{1,9},{2,10},{3,11},{4,12},{5,13},{6,14},{7,15},{8,0},{9,1},... | collective-permute-start | bytes 786440 | tf_op jit(solution)/shard_map/ppermute | solution.py:261
  36.8 10.7 %collective-permute-start.13 = (bf16[8,128,128]{2,1,0:T(8,128)(2,1)S(1)}, bf16[8,128,128]{2,1,0:T(8,128)(2,1)S(1)}, u32[]{:S(2)}, u32[]{:S(2)}) collective-permute-start(bf16[8,128,128]{2,1,0:T(8,128)(2,1)S(1)} %collective-permute-done.5.refs_2_), channel_id=1, source_target_pairs={{0,8},{1,9},{2,10},{3,11},{4,12},{5,13},{6,14},{7,15},{8,0},{9,1},... | collective-permute-start | bytes 786440 | tf_op jit(solution)/shard_map/ppermute | solution.py:261
  36.8 10.7 %collective-permute-start.14 = (bf16[8,128,128]{2,1,0:T(8,128)(2,1)S(1)}, bf16[8,128,128]{2,1,0:T(8,128)(2,1)S(1)}, u32[]{:S(2)}, u32[]{:S(2)}) collective-permute-start(bf16[8,128,128]{2,1,0:T(8,128)(2,1)S(1)} %get-tuple-element.39), channel_id=1, source_target_pairs={{0,4},{1,5},{2,6},{3,7},{4,0},{5,1},{6,2},{7,3},{8,12},{9,13},{10,... | collective-permute-start | bytes 786440 | tf_op jit(solution)/shard_map/ppermute | solution.py:261
  37.7 9.8 %collective-permute-start.15 = (bf16[8,128,128]{2,1,0:T(8,128)(2,1)S(1)}, bf16[8,128,128]{2,1,0:T(8,128)(2,1)S(1)}, u32[]{:S(2)}, u32[]{:S(2)}) collective-permute-start(bf16[8,128,128]{2,1,0:T(8,128)(2,1)S(1)} %get-tuple-element.40), channel_id=1, source_target_pairs={{0,2},{1,3},{2,0},{3,1},{4,6},{5,7},{6,4},{7,5},{8,10},{9,11},{10,... | collective-permute-start | bytes 786440 | tf_op jit(solution)/shard_map/ppermute | solution.py:261
  38.2 13.3 %collective-permute-start.16 = (bf16[8,128,128]{2,1,0:T(8,128)(2,1)S(1)}, bf16[8,128,128]{2,1,0:T(8,128)(2,1)S(1)}, u32[]{:S(2)}, u32[]{:S(2)}) collective-permute-start(bf16[8,128,128]{2,1,0:T(8,128)(2,1)S(1)} %get-tuple-element.41), channel_id=1, source_target_pairs={{0,6},{1,7},{2,4},{3,5},{4,2},{5,3},{6,0},{7,1},{8,14},{9,15},{10,... | collective-permute-start | bytes 786440 | tf_op jit(solution)/shard_map/ppermute | solution.py:261
  42.3 11.8 %collective-permute-start.17 = (bf16[8,128,128]{2,1,0:T(8,128)(2,1)S(1)}, bf16[8,128,128]{2,1,0:T(8,128)(2,1)S(1)}, u32[]{:S(2)}, u32[]{:S(2)}) collective-permute-start(bf16[8,128,128]{2,1,0:T(8,128)(2,1)S(1)} %collective-permute-done.refs_0_), channel_id=1, source_target_pairs={{0,1},{1,0},{2,3},{3,2},{4,5},{5,4},{6,7},{7,6},{8,9},{9,8},{10,11... | collective-permute-start | bytes 786440 | tf_op jit(solution)/shard_map/ppermute | solution.py:261
  52.1 15.3 %collective-permute-start.26 = (bf16[8,128,128]{2,1,0:T(8,128)(2,1)S(1)}, bf16[8,128,128]{2,1,0:T(8,128)(2,1)S(1)}, u32[]{:S(2)}, u32[]{:S(2)}) collective-permute-start(bf16[8,128,128]{2,1,0:T(8,128)(2,1)S(1)} %collective-permute-done.12.refs_8_.refs_0_), channel_id=1, source_target_pairs={{0,16},{1,17},{2,18},{3,19},{4,20},{5,21},{6,22},{7,23},{8,24},{9,... | collective-permute-start | bytes 786440 | tf_op jit(solution)/shard_map/ppermute | solution.py:261
  56.4 11.0 %collective-permute-start.21 = (bf16[8,128,128]{2,1,0:T(8,128)(2,1)S(1)}, bf16[8,128,128]{2,1,0:T(8,128)(2,1)S(1)}, u32[]{:S(2)}, u32[]{:S(2)}) collective-permute-start(bf16[8,128,128]{2,1,0:T(8,128)(2,1)S(1)} %get-tuple-element.47), channel_id=1, source_target_pairs={{0,4},{1,5},{2,6},{3,7},{4,0},{5,1},{6,2},{7,3},{8,12},{9,13},{10,... | collective-permute-start | bytes 786440 | tf_op jit(solution)/shard_map/ppermute | solution.py:261
  58.4 13.4 %collective-permute-start.23 = (bf16[8,128,128]{2,1,0:T(8,128)(2,1)S(1)}, bf16[8,128,128]{2,1,0:T(8,128)(2,1)S(1)}, u32[]{:S(2)}, u32[]{:S(2)}) collective-permute-start(bf16[8,128,128]{2,1,0:T(8,128)(2,1)S(1)} %get-tuple-element.49), channel_id=1, source_target_pairs={{0,6},{1,7},{2,4},{3,5},{4,2},{5,3},{6,0},{7,1},{8,14},{9,15},{10,... | collective-permute-start | bytes 786440 | tf_op jit(solution)/shard_map/ppermute | solution.py:261
  60.0 16.3 %collective-permute-start.25 = (bf16[8,128,128]{2,1,0:T(8,128)(2,1)S(1)}, bf16[8,128,128]{2,1,0:T(8,128)(2,1)S(1)}, u32[]{:S(2)}, u32[]{:S(2)}) collective-permute-start(bf16[8,128,128]{2,1,0:T(8,128)(2,1)S(1)} %collective-permute-done.12.refs_8_.refs_0_), channel_id=1, source_target_pairs={{0,8},{1,9},{2,10},{3,11},{4,12},{5,13},{6,14},{7,15},{8,0},{9,1},... | collective-permute-start | bytes 786440 | tf_op jit(solution)/shard_map/ppermute | solution.py:261
  67.4 11.8 %collective-permute-start.28 = (bf16[8,128,128]{2,1,0:T(8,128)(2,1)S(1)}, bf16[8,128,128]{2,1,0:T(8,128)(2,1)S(1)}, u32[]{:S(2)}, u32[]{:S(2)}) collective-permute-start(bf16[8,128,128]{2,1,0:T(8,128)(2,1)S(1)} %collective-permute-done.12.refs_8_.refs_0_), channel_id=1, source_target_pairs={{0,1},{1,0},{2,3},{3,2},{4,5},{5,4},{6,7},{7,6},{8,9},{9,8},{10,11... | collective-permute-start | bytes 786440 | tf_op jit(solution)/shard_map/ppermute | solution.py:261
  67.4 11.6 %collective-permute-start.27 = (bf16[8,128,128]{2,1,0:T(8,128)(2,1)S(1)}, bf16[8,128,128]{2,1,0:T(8,128)(2,1)S(1)}, u32[]{:S(2)}, u32[]{:S(2)}) collective-permute-start(bf16[8,128,128]{2,1,0:T(8,128)(2,1)S(1)} %collective-permute-done.26.refs_2_), channel_id=1, source_target_pairs={{0,8},{1,9},{2,10},{3,11},{4,12},{5,13},{6,14},{7,15},{8,0},{9,1},... | collective-permute-start | bytes 786440 | tf_op jit(solution)/shard_map/ppermute | solution.py:261
  71.9 11.4 %collective-permute-start.32 = (bf16[8,128,128]{2,1,0:T(8,128)(2,1)S(1)}, bf16[8,128,128]{2,1,0:T(8,128)(2,1)S(1)}, u32[]{:S(2)}, u32[]{:S(2)}) collective-permute-start(bf16[8,128,128]{2,1,0:T(8,128)(2,1)S(1)} %add_convert_fusion), channel_id=1, source_target_pairs={{0,0},{1,1},{2,16},{3,17},{4,8},{5,9},{6,24},{7,25},{8,20},{9,21},... | collective-permute-start | bytes 786440 | tf_op jit(solution)/shard_map/ppermute | solution.py:261
  76.3 11.5 %collective-permute-start.24 = (bf16[8,128,128]{2,1,0:T(8,128)(2,1)S(1)}, bf16[8,128,128]{2,1,0:T(8,128)(2,1)S(1)}, u32[]{:S(2)}, u32[]{:S(2)}) collective-permute-start(bf16[8,128,128]{2,1,0:T(8,128)(2,1)S(1)} %add_convert_fusion), channel_id=1, source_target_pairs={{0,0},{1,1},{2,2},{3,3},{4,4},{5,5},{6,6},{7,7},{8,10},{9,11},{10,... | collective-permute-start | bytes 786440 | tf_op jit(solution)/shard_map/ppermute | solution.py:261
  93.4 13.4 %collective-permute-start.36 = (bf16[1040,128]{1,0:T(8,128)(2,1)S(1)}, bf16[1040,128]{1,0:T(8,128)(2,1)S(1)}, u32[]{:S(2)}, u32[]{:S(2)}) collective-permute-start(bf16[1040,128]{1,0:T(8,128)(2,1)S(1)} %get-tuple-element.58), channel_id=1, source_target_pairs={{0,6},{1,7},{2,4},{3,5},{4,2},{5,3},{6,0},{7,1},{8,14},{9,15},{10,... | collective-permute-start | bytes 798728 | tf_op jit(solution)/shard_map/ppermute | solution.py:261
  107.2 16.9 %collective-permute-start.37 = (bf16[1040,128]{1,0:T(8,128)(2,1)S(1)}, bf16[1040,128]{1,0:T(8,128)(2,1)S(1)}, u32[]{:S(2)}, u32[]{:S(2)}) collective-permute-start(bf16[1040,128]{1,0:T(8,128)(2,1)S(1)} %plane_sum.1.own_ref), channel_id=1, source_target_pairs={{0,0},{1,1},{2,20},{3,21},{4,10},{5,11},{6,30},{7,31},{8,16},{9,17... | collective-permute-start | bytes 798728 | tf_op jit(solution)/shard_map/ppermute | solution.py:261
  109.1 9.8 %collective-permute-start.39 = (f32[8,128]{1,0:T(8,128)S(1)}, f32[8,128]{1,0:T(8,128)S(1)}, u32[]{:S(2)}, u32[]{:S(2)}) collective-permute-start(f32[8,128]{1,0:T(8,128)S(1)} %fusion.23), channel_id=1, source_target_pairs={{0,8},{1,9},{2,10},{3,11},{4,12},{5,13},{6,14},{7,15},{8,0},{9,1},... | collective-permute-start | bytes 12296 | tf_op jit(solution)/shard_map/ppermute | solution.py:261
  (21 other events, 111.4 us)

commit v4 on v1

--- a/solution.py
+++ b/solution.py
@@ -356,7 +356,7 @@
     dens_far = {m + 1: to_plane(after(dens_near[m], outs), 1) for m in far_from}
     kohn_behind = after(kohn_own, (dens_near, outs))
     kohn_pieces = {m: to_plane(kohn_behind, m) for m in far_from}
-    dens_near, dens_far = after((dens_near, dens_far), parts[1:])
+    dens_near = after(dens_near, parts[1:])
     dens_beside |= share_all(dens_near) | share_all(dens_far)
     dens_all = listed({0: dens_own} | dens_near | dens_far, dens_beside)
     outs = pl.pallas_call(

time: 136 us -> 134 us (0.985)
  waiting for transfers between devices: 66.2 us -> 61 us
  starting transfers between devices: 46.8 us -> 50.3 us
    ppermute x43, waiting for transfers between devices: 66.2 us -> 61 us  [permute(): return lax.ppermute(x, ('row', 'col'), row_major_perm(n_row, n_col, target))]
    ppermute x43, starting transfers between devices: 46.8 us -> 50.3 us  [permute(): return lax.ppermute(x, ('row', 'col'), row_major_perm(n_row, n_col, target))]
where the time goes in v4:
time: 134 us; the launch traced here: 133 us
  waiting for transfers between devices  61 us (46%)
  starting transfers between devices  50.3 us (38%)
  Pallas kernels  7.81 us (6%)
  local copies, waits for them, and re-layouts  7.35 us (5%)
  other arithmetic  3.74 us (3%)
  between operations  2.77 us (2%)
    ppermute x43, waiting for transfers between devices, permute(): return lax.ppermute(x, ('row', 'col'), row_major_perm(n_row, n_col, target))  61 us
    ppermute x43, starting transfers between devices, permute(): return lax.ppermute(x, ('row', 'col'), row_major_perm(n_row, n_col, target))  50.3 us
  transfers between devices with their start and end apart: 43, of which 17 were waited for; matrix products, arithmetic and copies ran while one was open for 7% of the time, Pallas kernels for 3%

profile of v4, /device:TPU:26, one launch (start us, length us, event | category | flops | bytes accessed | tf_op | source)
XLA Modules:
  0.0 133.0 jit_solution(12464745837771487063)
XLA Ops:
  13.6 2.9 %collective-permute-done.2.refs_2_ = bf16[8,128,128]{2,1,0:T(8,128)(2,1)S(1)} collective-permute-done((bf16[8,128,128]{2,1,0:T(8,128)(2,1)}, bf16[8,128,128]{2,1,0:T(8,128)(2,1)S(1)}, u32[]{:S(2)}, u32[]{:S(2)}) %collective-permute-start.2) | collective-permute-done | bytes 262176 | tf_op jit(solution)/shard_map/ppermute | solution.py:261
  16.5 3.5 %collective-permute-start.10 = (bf16[8,128,128]{2,1,0:T(8,128)(2,1)S(1)}, bf16[8,128,128]{2,1,0:T(8,128)(2,1)S(1)}, u32[]{:S(2)}, u32[]{:S(2)}) collective-permute-start(bf16[8,128,128]{2,1,0:T(8,128)(2,1)S(1)} %collective-permute-done.2.refs_2_), channel_id=1, source_target_pairs={{0,1},{1,0},{2,3},{3,2},{4,5},{5,4},{6,7},{7,6},{8,9},{9,8},{10,11... | collective-permute-start | bytes 786440 | tf_op jit(solution)/shard_map/ppermute | solution.py:261
  21.9 2.6 %collective-permute-start.5 = (bf16[8,128,128]{2,1,0:T(8,128)(2,1)S(1)}, bf16[8,128,128]{2,1,0:T(8,128)(2,1)S(1)}, u32[]{:S(2)}, u32[]{:S(2)}) collective-permute-start(bf16[8,128,128]{2,1,0:T(8,128)(2,1)S(1)} %collective-permute-done.refs_0_), channel_id=1, source_target_pairs={{0,16},{1,17},{2,18},{3,19},{4,20},{5,21},{6,22},{7,23},{8,24},{9,... | collective-permute-start | bytes 786440 | tf_op jit(solution)/shard_map/ppermute | solution.py:261
  29.5 2.2 %scaled_step_product.1 = (f32[8,128,128]{2,1,0:T(8,128)S(1)}, bf16[8,128,128]{2,1,0:T(8,128)(2,1)S(1)}, bf16[8,128,128]{2,1,0:T(8,128)(2,1)S(1)}, bf16[8,128,128]{2,1,0:T(8,128)(2,1)S(1)}) custom-call(s32[144]{0:T(256)S(1)} %pad_add_fusion.index_ref, bf16[8,128,128]{2,1,0:T(8,128)(2,1)S(1)} %collective-permute-done.6.left_ref, ...), custom_call_target="tpu_custom_call" | custom-call | flops 268435456 | bytes 4194304 | tf_op jit(solution)/shard_map/scaled_step_product/pallas_call | solution.py:343
  31.6 4.4 %collective-permute-start.13 = (bf16[8,128,128]{2,1,0:T(8,128)(2,1)S(1)}, bf16[8,128,128]{2,1,0:T(8,128)(2,1)S(1)}, u32[]{:S(2)}, u32[]{:S(2)}) collective-permute-start(bf16[8,128,128]{2,1,0:T(8,128)(2,1)S(1)} %get-tuple-element.36), channel_id=1, source_target_pairs={{0,4},{1,5},{2,6},{3,7},{4,0},{5,1},{6,2},{7,3},{8,12},{9,13},{10,... | collective-permute-start | bytes 786440 | tf_op jit(solution)/shard_map/ppermute | solution.py:261
  38.3 3.7 %collective-permute-done.4.refs_1_ = bf16[8,128,128]{2,1,0:T(8,128)(2,1)S(1)} collective-permute-done((bf16[8,128,128]{2,1,0:T(8,128)(2,1)S(1)}, bf16[8,128,128]{2,1,0:T(8,128)(2,1)S(1)}, u32[]{:S(2)}, u32[]{:S(2)}) %collective-permute-start.4) | collective-permute-done | bytes 262176 | tf_op jit(solution)/shard_map/ppermute | solution.py:261
  42.5 2.7 %collective-permute-done.14.refs_10_ = bf16[8,128,128]{2,1,0:T(8,128)(2,1)S(1)} collective-permute-done((bf16[8,128,128]{2,1,0:T(8,128)(2,1)S(1)}, bf16[8,128,128]{2,1,0:T(8,128)(2,1)S(1)}, u32[]{:S(2)}, u32[]{:S(2)}) %collective-permute-start.14) | collective-permute-done | bytes 262176 | tf_op jit(solution)/shard_map/ppermute | solution.py:261
  45.2 4.1 %collective-permute-done.15.refs_11_ = bf16[8,128,128]{2,1,0:T(8,128)(2,1)S(1)} collective-permute-done((bf16[8,128,128]{2,1,0:T(8,128)(2,1)S(1)}, bf16[8,128,128]{2,1,0:T(8,128)(2,1)S(1)}, u32[]{:S(2)}, u32[]{:S(2)}) %collective-permute-start.15) | collective-permute-done | bytes 262176 | tf_op jit(solution)/shard_map/ppermute | solution.py:261
  52.5 2.3 %change_product.1 = (f32[8,128,128]{2,1,0:T(8,128)S(1)}, bf16[8,128,128]{2,1,0:T(8,128)(2,1)S(1)}, bf16[8,128,128]{2,1,0:T(8,128)(2,1)S(1)}, bf16[8,128,128]{2,1,0:T(8,128)(2,1)S(1)}) custom-call(s32[144]{0:T(256)S(1)} %pad_add_fusion.index_ref, bf16[8,128,128]{2,1,0:T(8,128)(2,1)S(1)} %collective-permute-done.refs_0_, ...), custom_call_target="tpu_custom_call" | custom-call | flops 268435456 | bytes 4194304 | tf_op jit(solution)/shard_map/change_product/pallas_call | solution.py:362
  59.7 5.8 %collective-permute-done.26.refs_2_ = bf16[8,128,128]{2,1,0:T(8,128)(2,1)S(1)} collective-permute-done((bf16[8,128,128]{2,1,0:T(8,128)(2,1)S(1)}, bf16[8,128,128]{2,1,0:T(8,128)(2,1)S(1)}, u32[]{:S(2)}, u32[]{:S(2)}) %collective-permute-start.26) | collective-permute-done | bytes 262176 | tf_op jit(solution)/shard_map/ppermute | solution.py:261
  65.7 4.3 %collective-permute-done.23 = bf16[8,128,128]{2,1,0:T(8,128)(2,1)S(1)} collective-permute-done((bf16[8,128,128]{2,1,0:T(8,128)(2,1)S(1)}, bf16[8,128,128]{2,1,0:T(8,128)(2,1)S(1)}, u32[]{:S(2)}, u32[]{:S(2)}) %collective-permute-start.23) | collective-permute-done | bytes 262176 | tf_op jit(solution)/shard_map/ppermute | solution.py:261
  70.2 4.2 %collective-permute-start.32 = (bf16[8,128,128]{2,1,0:T(8,128)(2,1)S(1)}, bf16[8,128,128]{2,1,0:T(8,128)(2,1)S(1)}, u32[]{:S(2)}, u32[]{:S(2)}) collective-permute-start(bf16[8,128,128]{2,1,0:T(8,128)(2,1)S(1)} %add_convert_fusion), channel_id=1, source_target_pairs={{0,0},{1,1},{2,16},{3,17},{4,8},{5,9},{6,24},{7,25},{8,20},{9,21},... | collective-permute-start | bytes 786440 | tf_op jit(solution)/shard_map/ppermute | solution.py:261
  74.5 2.3 %collective-permute-start.24 = (bf16[8,128,128]{2,1,0:T(8,128)(2,1)S(1)}, bf16[8,128,128]{2,1,0:T(8,128)(2,1)S(1)}, u32[]{:S(2)}, u32[]{:S(2)}) collective-permute-start(bf16[8,128,128]{2,1,0:T(8,128)(2,1)S(1)} %add_convert_fusion), channel_id=1, source_target_pairs={{0,0},{1,1},{2,2},{3,3},{4,4},{5,5},{6,6},{7,7},{8,10},{9,11},{10,... | collective-permute-start | bytes 786440 | tf_op jit(solution)/shard_map/ppermute | solution.py:261
  77.3 4.9 %collective-permute-done.32.refs_8_ = bf16[8,128,128]{2,1,0:T(8,128)(2,1)S(1)} collective-permute-done((bf16[8,128,128]{2,1,0:T(8,128)(2,1)S(1)}, bf16[8,128,128]{2,1,0:T(8,128)(2,1)S(1)}, u32[]{:S(2)}, u32[]{:S(2)}) %collective-permute-start.32) | collective-permute-done | bytes 262176 | tf_op jit(solution)/shard_map/ppermute | solution.py:261
  82.3 3.6 %collective-permute-done.24.own_ref = bf16[8,128,128]{2,1,0:T(8,128)(2,1)S(1)} collective-permute-done((bf16[8,128,128]{2,1,0:T(8,128)(2,1)S(1)}, bf16[8,128,128]{2,1,0:T(8,128)(2,1)S(1)}, u32[]{:S(2)}, u32[]{:S(2)}) %collective-permute-start.24) | collective-permute-done | bytes 262176 | tf_op jit(solution)/shard_map/ppermute | solution.py:261
  85.9 2.3 %commutator_product.1 = (f32[8,128,128]{2,1,0:T(8,128)S(1)}, bf16[1040,128]{1,0:T(8,128)(2,1)S(1)}, bf16[1040,128]{1,0:T(8,128)(2,1)S(1)}, bf16[1040,128]{1,0:T(8,128)(2,1)S(1)}, bf16[16,128]{1,0:T(8,128)(2,1)S(1)}) custom-call(s32[144]{0:T(256)S(1)} %pad_add_fusion.index_ref, bf16[8,128,128]{2,1,0:T(8,128)(2,1)S(1)} %collective-permute-done.24.own_ref, ...), custom_call_target="tpu_custom_call" | custom-call | flops 268435456 | bytes 4194304 | tf_op jit(solution)/shard_map/commutator_product/pallas_call | solution.py:389
  89.7 2.0 %collective-permute-start.35 = (bf16[1040,128]{1,0:T(8,128)(2,1)S(1)}, bf16[1040,128]{1,0:T(8,128)(2,1)S(1)}, u32[]{:S(2)}, u32[]{:S(2)}) collective-permute-start(bf16[1040,128]{1,0:T(8,128)(2,1)S(1)} %get-tuple-element.54), channel_id=1, source_target_pairs={{0,2},{1,3},{2,0},{3,1},{4,6},{5,7},{6,4},{7,5},{8,10},{9,11},{10,... | collective-permute-start | bytes 798728 | tf_op jit(solution)/shard_map/ppermute | solution.py:261
  93.0 3.2 %collective-permute-done.34.refs_0_ = bf16[1040,128]{1,0:T(8,128)(2,1)S(1)} collective-permute-done((bf16[1040,128]{1,0:T(8,128)(2,1)S(1)}, bf16[1040,128]{1,0:T(8,128)(2,1)S(1)}, u32[]{:S(2)}, u32[]{:S(2)}) %collective-permute-start.34) | collective-permute-done | bytes 266272 | tf_op jit(solution)/shard_map/ppermute | solution.py:261
  96.3 2.6 %collective-permute-done.35.refs_1_ = bf16[1040,128]{1,0:T(8,128)(2,1)S(1)} collective-permute-done((bf16[1040,128]{1,0:T(8,128)(2,1)S(1)}, bf16[1040,128]{1,0:T(8,128)(2,1)S(1)}, u32[]{:S(2)}, u32[]{:S(2)}) %collective-permute-start.35) | collective-permute-done | bytes 266272 | tf_op jit(solution)/shard_map/ppermute | solution.py:261
  98.9 6.2 %collective-permute-done.36.refs_2_ = bf16[1040,128]{1,0:T(8,128)(2,1)S(1)} collective-permute-done((bf16[1040,128]{1,0:T(8,128)(2,1)S(1)}, bf16[1040,128]{1,0:T(8,128)(2,1)S(1)}, u32[]{:S(2)}, u32[]{:S(2)}) %collective-permute-start.36) | collective-permute-done | bytes 266272 | tf_op jit(solution)/shard_map/ppermute | solution.py:261
  105.4 1.9 %collective-permute-start.37 = (bf16[1040,128]{1,0:T(8,128)(2,1)S(1)}, bf16[1040,128]{1,0:T(8,128)(2,1)S(1)}, u32[]{:S(2)}, u32[]{:S(2)}) collective-permute-start(bf16[1040,128]{1,0:T(8,128)(2,1)S(1)} %plane_sum.1.own_ref), channel_id=1, source_target_pairs={{0,0},{1,1},{2,20},{3,21},{4,10},{5,11},{6,30},{7,31},{8,16},{9,17... | collective-permute-start | bytes 798728 | tf_op jit(solution)/shard_map/ppermute | solution.py:261
  107.3 10.2 %collective-permute-done.37.refs_0_ = bf16[1040,128]{1,0:T(8,128)(2,1)S(1)} collective-permute-done((bf16[1040,128]{1,0:T(8,128)(2,1)S(1)}, bf16[1040,128]{1,0:T(8,128)(2,1)S(1)}, u32[]{:S(2)}, u32[]{:S(2)}) %collective-permute-start.37) | collective-permute-done | bytes 266272 | tf_op jit(solution)/shard_map/ppermute | solution.py:261
  121.9 3.5 %collective-permute-start.41 = (f32[8,128]{1,0:T(8,128)S(1)}, f32[8,128]{1,0:T(8,128)S(1)}, u32[]{:S(2)}, u32[]{:S(2)}) collective-permute-start(f32[8,128]{1,0:T(8,128)S(1)} %fusion.4), channel_id=1, source_target_pairs={{0,2},{1,3},{2,0},{3,1},{4,6},{5,7},{6,4},{7,5},{8,10},{9,11},{10,... | collective-permute-start | bytes 12296 | tf_op jit(solution)/shard_map/ppermute | solution.py:261
  125.5 3.9 %collective-permute-done.41 = f32[8,128]{1,0:T(8,128)S(1)} collective-permute-done((f32[8,128]{1,0:T(8,128)S(1)}, f32[8,128]{1,0:T(8,128)S(1)}, u32[]{:S(2)}, u32[]{:S(2)}) %collective-permute-start.41) | collective-permute-done | bytes 4128 | tf_op jit(solution)/shard_map/ppermute | solution.py:261
  (136 shorter events, 41.0 us)
Async XLA Ops:
  0.6 15.8 %collective-permute-start.2 = (bf16[8,128,128]{2,1,0:T(8,128)(2,1)}, bf16[8,128,128]{2,1,0:T(8,128)(2,1)S(1)}, u32[]{:S(2)}, u32[]{:S(2)}) collective-permute-start(bf16[8,128,128]{2,1,0:T(8,128)(2,1)} %bitcast.58), channel_id=1, source_target_pairs={{0,16},{1,20},{2,18},{3,22},{4,17},{5,21},{6,19},{7,23},{8,24},{9,... | collective-permute-start | bytes 786440 | tf_op jit(solution)/shard_map/ppermute | solution.py:261
  1.0 15.4 %collective-permute-start.1 = (bf16[8,128,128]{2,1,0:T(8,128)(2,1)}, bf16[8,128,128]{2,1,0:T(8,128)(2,1)S(1)}, u32[]{:S(2)}, u32[]{:S(2)}) collective-permute-start(bf16[8,128,128]{2,1,0:T(8,128)(2,1)} %bitcast.59), channel_id=1, source_target_pairs={{0,8},{1,12},{2,10},{3,14},{4,9},{5,13},{6,11},{7,15},{8,0},{9,4},... | collective-permute-start | bytes 786440 | tf_op jit(solution)/shard_map/ppermute | solution.py:261
  1.5 23.0 %collective-permute-start.7 = (bf16[8,128,128]{2,1,0:T(8,128)(2,1)}, bf16[8,128,128]{2,1,0:T(8,128)(2,1)S(1)}, u32[]{:S(2)}, u32[]{:S(2)}) collective-permute-start(bf16[8,128,128]{2,1,0:T(8,128)(2,1)} %bitcast.60), channel_id=1, source_target_pairs={{0,0},{1,4},{2,2},{3,6},{4,1},{5,5},{6,3},{7,7},{8,8},{9,12},{10,1... | collective-permute-start | bytes 786440 | tf_op jit(solution)/shard_map/ppermute | solution.py:261
  3.1 18.8 %collective-permute-start = (bf16[8,128,128]{2,1,0:T(8,128)(2,1)}, bf16[8,128,128]{2,1,0:T(8,128)(2,1)S(1)}, u32[]{:S(2)}, u32[]{:S(2)}) collective-permute-start(bf16[8,128,128]{2,1,0:T(8,128)(2,1)} %bitcast.57), channel_id=1, source_target_pairs={{0,0},{1,4},{2,2},{3,6},{4,1},{5,5},{6,3},{7,7},{8,8},{9,12},{10,1... | collective-permute-start | bytes 786440 | tf_op jit(solution)/shard_map/ppermute | solution.py:261
  4.7 21.6 %collective-permute-start.6 = (bf16[8,128,128]{2,1,0:T(8,128)(2,1)}, bf16[8,128,128]{2,1,0:T(8,128)(2,1)S(1)}, u32[]{:S(2)}, u32[]{:S(2)}) collective-permute-start(bf16[8,128,128]{2,1,0:T(8,128)(2,1)} %bitcast.61), channel_id=1, source_target_pairs={{0,0},{1,4},{2,2},{3,6},{4,1},{5,5},{6,3},{7,7},{8,8},{9,12},{10,1... | collective-permute-start | bytes 786440 | tf_op jit(solution)/shard_map/ppermute | solution.py:261
  16.5 10.4 %collective-permute-start.10 = (bf16[8,128,128]{2,1,0:T(8,128)(2,1)S(1)}, bf16[8,128,128]{2,1,0:T(8,128)(2,1)S(1)}, u32[]{:S(2)}, u32[]{:S(2)}) collective-permute-start(bf16[8,128,128]{2,1,0:T(8,128)(2,1)S(1)} %collective-permute-done.2.refs_2_), channel_id=1, source_target_pairs={{0,1},{1,0},{2,3},{3,2},{4,5},{5,4},{6,7},{7,6},{8,9},{9,8},{10,11... | collective-permute-start | bytes 786440 | tf_op jit(solution)/shard_map/ppermute | solution.py:261
  21.9 15.7 %collective-permute-start.5 = (bf16[8,128,128]{2,1,0:T(8,128)(2,1)S(1)}, bf16[8,128,128]{2,1,0:T(8,128)(2,1)S(1)}, u32[]{:S(2)}, u32[]{:S(2)}) collective-permute-start(bf16[8,128,128]{2,1,0:T(8,128)(2,1)S(1)} %collective-permute-done.refs_0_), channel_id=1, source_target_pairs={{0,16},{1,17},{2,18},{3,19},{4,20},{5,21},{6,22},{7,23},{8,24},{9,... | collective-permute-start | bytes 786440 | tf_op jit(solution)/shard_map/ppermute | solution.py:261
  28.8 13.2 %collective-permute-start.4 = (bf16[8,128,128]{2,1,0:T(8,128)(2,1)S(1)}, bf16[8,128,128]{2,1,0:T(8,128)(2,1)S(1)}, u32[]{:S(2)}, u32[]{:S(2)}) collective-permute-start(bf16[8,128,128]{2,1,0:T(8,128)(2,1)S(1)} %collective-permute-done.refs_0_), channel_id=1, source_target_pairs={{0,8},{1,9},{2,10},{3,11},{4,12},{5,13},{6,14},{7,15},{8,0},{9,1},... | collective-permute-start | bytes 786440 | tf_op jit(solution)/shard_map/ppermute | solution.py:261
  31.6 10.9 %collective-permute-start.13 = (bf16[8,128,128]{2,1,0:T(8,128)(2,1)S(1)}, bf16[8,128,128]{2,1,0:T(8,128)(2,1)S(1)}, u32[]{:S(2)}, u32[]{:S(2)}) collective-permute-start(bf16[8,128,128]{2,1,0:T(8,128)(2,1)S(1)} %get-tuple-element.36), channel_id=1, source_target_pairs={{0,4},{1,5},{2,6},{3,7},{4,0},{5,1},{6,2},{7,3},{8,12},{9,13},{10,... | collective-permute-start | bytes 786440 | tf_op jit(solution)/shard_map/ppermute | solution.py:261
  36.6 12.7 %collective-permute-start.15 = (bf16[8,128,128]{2,1,0:T(8,128)(2,1)S(1)}, bf16[8,128,128]{2,1,0:T(8,128)(2,1)S(1)}, u32[]{:S(2)}, u32[]{:S(2)}) collective-permute-start(bf16[8,128,128]{2,1,0:T(8,128)(2,1)S(1)} %get-tuple-element.38), channel_id=1, source_target_pairs={{0,6},{1,7},{2,4},{3,5},{4,2},{5,3},{6,0},{7,1},{8,14},{9,15},{10,... | collective-permute-start | bytes 786440 | tf_op jit(solution)/shard_map/ppermute | solution.py:261
  37.6 12.6 %collective-permute-start.16 = (bf16[8,128,128]{2,1,0:T(8,128)(2,1)S(1)}, bf16[8,128,128]{2,1,0:T(8,128)(2,1)S(1)}, u32[]{:S(2)}, u32[]{:S(2)}) collective-permute-start(bf16[8,128,128]{2,1,0:T(8,128)(2,1)S(1)} %collective-permute-done.5.refs_2_), channel_id=1, source_target_pairs={{0,8},{1,9},{2,10},{3,11},{4,12},{5,13},{6,14},{7,15},{8,0},{9,1},... | collective-permute-start | bytes 786440 | tf_op jit(solution)/shard_map/ppermute | solution.py:261
  42.0 10.5 %collective-permute-start.17 = (bf16[8,128,128]{2,1,0:T(8,128)(2,1)S(1)}, bf16[8,128,128]{2,1,0:T(8,128)(2,1)S(1)}, u32[]{:S(2)}, u32[]{:S(2)}) collective-permute-start(bf16[8,128,128]{2,1,0:T(8,128)(2,1)S(1)} %collective-permute-done.refs_0_), channel_id=1, source_target_pairs={{0,1},{1,0},{2,3},{3,2},{4,5},{5,4},{6,7},{7,6},{8,9},{9,8},{10,11... | collective-permute-start | bytes 786440 | tf_op jit(solution)/shard_map/ppermute | solution.py:261
  50.7 14.8 %collective-permute-start.26 = (bf16[8,128,128]{2,1,0:T(8,128)(2,1)S(1)}, bf16[8,128,128]{2,1,0:T(8,128)(2,1)S(1)}, u32[]{:S(2)}, u32[]{:S(2)}) collective-permute-start(bf16[8,128,128]{2,1,0:T(8,128)(2,1)S(1)} %collective-permute-done.12.refs_8_.refs_0_), channel_id=1, source_target_pairs={{0,16},{1,17},{2,18},{3,19},{4,20},{5,21},{6,22},{7,23},{8,24},{9,... | collective-permute-start | bytes 786440 | tf_op jit(solution)/shard_map/ppermute | solution.py:261
  54.7 10.8 %collective-permute-start.21 = (bf16[8,128,128]{2,1,0:T(8,128)(2,1)S(1)}, bf16[8,128,128]{2,1,0:T(8,128)(2,1)S(1)}, u32[]{:S(2)}, u32[]{:S(2)}) collective-permute-start(bf16[8,128,128]{2,1,0:T(8,128)(2,1)S(1)} %get-tuple-element.44), channel_id=1, source_target_pairs={{0,4},{1,5},{2,6},{3,7},{4,0},{5,1},{6,2},{7,3},{8,12},{9,13},{10,... | collective-permute-start | bytes 786440 | tf_op jit(solution)/shard_map/ppermute | solution.py:261
  56.4 9.3 %collective-permute-start.22 = (bf16[8,128,128]{2,1,0:T(8,128)(2,1)S(1)}, bf16[8,128,128]{2,1,0:T(8,128)(2,1)S(1)}, u32[]{:S(2)}, u32[]{:S(2)}) collective-permute-start(bf16[8,128,128]{2,1,0:T(8,128)(2,1)S(1)} %get-tuple-element.45), channel_id=1, source_target_pairs={{0,2},{1,3},{2,0},{3,1},{4,6},{5,7},{6,4},{7,5},{8,10},{9,11},{10,... | collective-permute-start | bytes 786440 | tf_op jit(solution)/shard_map/ppermute | solution.py:261
  57.0 13.1 %collective-permute-start.23 = (bf16[8,128,128]{2,1,0:T(8,128)(2,1)S(1)}, bf16[8,128,128]{2,1,0:T(8,128)(2,1)S(1)}, u32[]{:S(2)}, u32[]{:S(2)}) collective-permute-start(bf16[8,128,128]{2,1,0:T(8,128)(2,1)S(1)} %get-tuple-element.46), channel_id=1, source_target_pairs={{0,6},{1,7},{2,4},{3,5},{4,2},{5,3},{6,0},{7,1},{8,14},{9,15},{10,... | collective-permute-start | bytes 786440 | tf_op jit(solution)/shard_map/ppermute | solution.py:261
  58.3 16.1 %collective-permute-start.25 = (bf16[8,128,128]{2,1,0:T(8,128)(2,1)S(1)}, bf16[8,128,128]{2,1,0:T(8,128)(2,1)S(1)}, u32[]{:S(2)}, u32[]{:S(2)}) collective-permute-start(bf16[8,128,128]{2,1,0:T(8,128)(2,1)S(1)} %collective-permute-done.12.refs_8_.refs_0_), channel_id=1, source_target_pairs={{0,8},{1,9},{2,10},{3,11},{4,12},{5,13},{6,14},{7,15},{8,0},{9,1},... | collective-permute-start | bytes 786440 | tf_op jit(solution)/shard_map/ppermute | solution.py:261
  65.6 11.5 %collective-permute-start.28 = (bf16[8,128,128]{2,1,0:T(8,128)(2,1)S(1)}, bf16[8,128,128]{2,1,0:T(8,128)(2,1)S(1)}, u32[]{:S(2)}, u32[]{:S(2)}) collective-permute-start(bf16[8,128,128]{2,1,0:T(8,128)(2,1)S(1)} %collective-permute-done.12.refs_8_.refs_0_), channel_id=1, source_target_pairs={{0,1},{1,0},{2,3},{3,2},{4,5},{5,4},{6,7},{7,6},{8,9},{9,8},{10,11... | collective-permute-start | bytes 786440 | tf_op jit(solution)/shard_map/ppermute | solution.py:261
  65.6 11.2 %collective-permute-start.27 = (bf16[8,128,128]{2,1,0:T(8,128)(2,1)S(1)}, bf16[8,128,128]{2,1,0:T(8,128)(2,1)S(1)}, u32[]{:S(2)}, u32[]{:S(2)}) collective-permute-start(bf16[8,128,128]{2,1,0:T(8,128)(2,1)S(1)} %collective-permute-done.26.refs_2_), channel_id=1, source_target_pairs={{0,8},{1,9},{2,10},{3,11},{4,12},{5,13},{6,14},{7,15},{8,0},{9,1},... | collective-permute-start | bytes 786440 | tf_op jit(solution)/shard_map/ppermute | solution.py:261
  70.2 12.1 %collective-permute-start.32 = (bf16[8,128,128]{2,1,0:T(8,128)(2,1)S(1)}, bf16[8,128,128]{2,1,0:T(8,128)(2,1)S(1)}, u32[]{:S(2)}, u32[]{:S(2)}) collective-permute-start(bf16[8,128,128]{2,1,0:T(8,128)(2,1)S(1)} %add_convert_fusion), channel_id=1, source_target_pairs={{0,0},{1,1},{2,16},{3,17},{4,8},{5,9},{6,24},{7,25},{8,20},{9,21},... | collective-permute-start | bytes 786440 | tf_op jit(solution)/shard_map/ppermute | solution.py:261
  74.5 11.5 %collective-permute-start.24 = (bf16[8,128,128]{2,1,0:T(8,128)(2,1)S(1)}, bf16[8,128,128]{2,1,0:T(8,128)(2,1)S(1)}, u32[]{:S(2)}, u32[]{:S(2)}) collective-permute-start(bf16[8,128,128]{2,1,0:T(8,128)(2,1)S(1)} %add_convert_fusion), channel_id=1, source_target_pairs={{0,0},{1,1},{2,2},{3,3},{4,4},{5,5},{6,6},{7,7},{8,10},{9,11},{10,... | collective-permute-start | bytes 786440 | tf_op jit(solution)/shard_map/ppermute | solution.py:261
  91.7 13.4 %collective-permute-start.36 = (bf16[1040,128]{1,0:T(8,128)(2,1)S(1)}, bf16[1040,128]{1,0:T(8,128)(2,1)S(1)}, u32[]{:S(2)}, u32[]{:S(2)}) collective-permute-start(bf16[1040,128]{1,0:T(8,128)(2,1)S(1)} %get-tuple-element.55), channel_id=1, source_target_pairs={{0,6},{1,7},{2,4},{3,5},{4,2},{5,3},{6,0},{7,1},{8,14},{9,15},{10,... | collective-permute-start | bytes 798728 | tf_op jit(solution)/shard_map/ppermute | solution.py:261
  105.4 12.1 %collective-permute-start.37 = (bf16[1040,128]{1,0:T(8,128)(2,1)S(1)}, bf16[1040,128]{1,0:T(8,128)(2,1)S(1)}, u32[]{:S(2)}, u32[]{:S(2)}) collective-permute-start(bf16[1040,128]{1,0:T(8,128)(2,1)S(1)} %plane_sum.1.own_ref), channel_id=1, source_target_pairs={{0,0},{1,1},{2,20},{3,21},{4,10},{5,11},{6,30},{7,31},{8,16},{9,17... | collective-permute-start | bytes 798728 | tf_op jit(solution)/shard_map/ppermute | solution.py:261
  119.9 11.3 %collective-permute-start.39 = (bf16[8,128,128]{2,1,0:T(8,128)(2,1)S(1)}, bf16[8,128,128]{2,1,0:T(8,128)(2,1)S(1)}, u32[]{:S(2)}, u32[]{:S(2)}) collective-permute-start(bf16[8,128,128]{2,1,0:T(8,128)(2,1)S(1)} %commutator_difference.1), channel_id=1, source_target_pairs={{0,0},{1,4},{2,2},{3,6},{4,1},{5,5},{6,3},{7,7},{8,10},{9,14},{10,... | collective-permute-start | bytes 786440 | tf_op jit(solution)/shard_map/ppermute | solution.py:261
  (21 other events, 113.9 us)

commit v5 on v4

--- a/solution.py
+++ b/solution.py
@@ -147,7 +147,7 @@
 
 def sum_kernel(n_out, trace_ref, own_ref, *refs):
     parts, (out, own, others, result, sems, out_sems) = refs[: n_out - 1], refs[n_out - 1 :]
-    pairs = [(part, others.at[d]) for d, part in enumerate(parts)]
+    pairs = [(part, others.at[n_out - 2 - i]) for i, part in enumerate(parts)]
     wait_for(start_copies([(own_ref, own)] + pairs, sems))
     blocks, side = own.shape[:2]
     for b in range(blocks):
@@ -287,9 +287,8 @@
 
     def exchange(outs):
         return [outs[0]] + [
-            inside_permute(out, lambda o, h, g, d=d: (o, h, g ^ d))
-            for d, out in enumerate(outs)
-            if d
+            inside_permute(outs[d], lambda o, h, g, d=d: (o, h, g ^ d))
+            for d in range(len(outs) - 1, 0, -1)
         ]
 
     def total_of(parts):
@@ -341,15 +340,15 @@
     kohn_own = relayout(kohn)
     inter_all = listed(inter_early | inter_far, share_all(inter_early) | share_all(inter_far))
     outs = pl.pallas_call(
-        functools.partial(first_kernel, rows, slots, n_row, 1, first_at),
+        functools.partial(first_kernel, rows, slots, n_row, 0, first_at),
         out_shape=out_shapes,
-        in_specs=[smem] + [anywhere] * (1 + n_row + 1),
+        in_specs=[smem] + [anywhere] * (1 + n_row),
         out_specs=(anywhere,) * n_col,
         scratch_shapes=[held(n_row * blocks + 1), held(blocks), *sums, dma(n_row + 1), dma(n_col)],
         compiler_params=params,
         cost_estimate=cost,
         name="scaled_step_product",
-    )(tables, step, *inter_all, kohn_own)
+    )(tables, step, *inter_all)
     parts = exchange(outs)
 
     dens_beside = {0: share(dens_own)}

time: 134 us -> 132 us (0.985)
  starting transfers between devices: 50.3 us -> 47.5 us
  waiting for transfers between devices: 61 us -> 62.6 us
    ppermute x43, starting transfers between devices: 50.3 us -> 47.5 us  [permute(): return lax.ppermute(x, ('row', 'col'), row_major_perm(n_row, n_col, target))]
    ppermute x43, waiting for transfers between devices: 61 us -> 62.6 us  [permute(): return lax.ppermute(x, ('row', 'col'), row_major_perm(n_row, n_col, target))]
  transfers between devices with their start and end apart: 43 -> 43, of which waited for: 17 -> 22; matrix products, arithmetic and copies ran while one was open for 7% -> 7% of each run, Pallas kernels for 3% -> 3%
where the time goes in v5:
time: 132 us
  waiting for transfers between devices  62.6 us (47%)
  starting transfers between devices  47.5 us (36%)
  Pallas kernels  7.77 us (6%)
  local copies, waits for them, and re-layouts  7.35 us (6%)
  other arithmetic  3.73 us (3%)
  between operations  2.75 us (2%)
    ppermute x43, waiting for transfers between devices, permute(): return lax.ppermute(x, ('row', 'col'), row_major_perm(n_row, n_col, target))  62.6 us
    ppermute x43, starting transfers between devices, permute(): return lax.ppermute(x, ('row', 'col'), row_major_perm(n_row, n_col, target))  47.5 us
  transfers between devices with their start and end apart: 43, of which 22 were waited for; matrix products, arithmetic and copies ran while one was open for 7% of the time, Pallas kernels for 3%

profile of v5, /device:TPU:26, one launch (start us, length us, event | category | flops | bytes accessed | tf_op | source)
XLA Modules:
  0.0 131.7 jit_solution(977014337252294091)
XLA Ops:
  13.6 2.9 %collective-permute-done.2.refs_2_ = bf16[8,128,128]{2,1,0:T(8,128)(2,1)S(1)} collective-permute-done((bf16[8,128,128]{2,1,0:T(8,128)(2,1)}, bf16[8,128,128]{2,1,0:T(8,128)(2,1)S(1)}, u32[]{:S(2)}, u32[]{:S(2)}) %collective-permute-start.2) | collective-permute-done | bytes 262176 | tf_op jit(solution)/shard_map/ppermute | solution.py:261
  19.8 4.4 %collective-permute-start.10 = (bf16[8,128,128]{2,1,0:T(8,128)(2,1)S(1)}, bf16[8,128,128]{2,1,0:T(8,128)(2,1)S(1)}, u32[]{:S(2)}, u32[]{:S(2)}) collective-permute-start(bf16[8,128,128]{2,1,0:T(8,128)(2,1)S(1)} %collective-permute-done.2.refs_2_), channel_id=1, source_target_pairs={{0,1},{1,0},{2,3},{3,2},{4,5},{5,4},{6,7},{7,6},{8,9},{9,8},{10,11... | collective-permute-start | bytes 786440 | tf_op jit(solution)/shard_map/ppermute | solution.py:261
  24.8 2.5 %collective-permute-done.3.refs_3_ = bf16[8,128,128]{2,1,0:T(8,128)(2,1)S(1)} collective-permute-done((bf16[8,128,128]{2,1,0:T(8,128)(2,1)S(1)}, bf16[8,128,128]{2,1,0:T(8,128)(2,1)S(1)}, u32[]{:S(2)}, u32[]{:S(2)}) %collective-permute-start.3) | collective-permute-done | bytes 262176 | tf_op jit(solution)/shard_map/ppermute | solution.py:261
  30.1 2.1 %scaled_step_product.1 = (f32[8,128,128]{2,1,0:T(8,128)S(1)}, bf16[8,128,128]{2,1,0:T(8,128)(2,1)S(1)}, bf16[8,128,128]{2,1,0:T(8,128)(2,1)S(1)}, bf16[8,128,128]{2,1,0:T(8,128)(2,1)S(1)}) custom-call(s32[144]{0:T(256)S(1)} %pad_add_fusion.index_ref, bf16[8,128,128]{2,1,0:T(8,128)(2,1)S(1)} %collective-permute-done.6.left_ref, ...), custom_call_target="tpu_custom_call" | custom-call | flops 268435456 | bytes 4194304 | tf_op jit(solution)/shard_map/scaled_step_product/pallas_call | solution.py:342
  33.7 2.1 %collective-permute-start.14 = (bf16[8,128,128]{2,1,0:T(8,128)(2,1)S(1)}, bf16[8,128,128]{2,1,0:T(8,128)(2,1)S(1)}, u32[]{:S(2)}, u32[]{:S(2)}) collective-permute-start(bf16[8,128,128]{2,1,0:T(8,128)(2,1)S(1)} %get-tuple-element.37), channel_id=1, source_target_pairs={{0,4},{1,5},{2,6},{3,7},{4,0},{5,1},{6,2},{7,3},{8,12},{9,13},{10,... | collective-permute-start | bytes 786440 | tf_op jit(solution)/shard_map/ppermute | solution.py:261
  37.3 2.7 %collective-permute-done.4.refs_1_ = bf16[8,128,128]{2,1,0:T(8,128)(2,1)S(1)} collective-permute-done((bf16[8,128,128]{2,1,0:T(8,128)(2,1)S(1)}, bf16[8,128,128]{2,1,0:T(8,128)(2,1)S(1)}, u32[]{:S(2)}, u32[]{:S(2)}) %collective-permute-start.4) | collective-permute-done | bytes 262176 | tf_op jit(solution)/shard_map/ppermute | solution.py:261
  39.9 2.4 %collective-permute-done.12.refs_9_ = bf16[8,128,128]{2,1,0:T(8,128)(2,1)S(1)} collective-permute-done((bf16[8,128,128]{2,1,0:T(8,128)(2,1)S(1)}, bf16[8,128,128]{2,1,0:T(8,128)(2,1)S(1)}, u32[]{:S(2)}, u32[]{:S(2)}) %collective-permute-start.12) | collective-permute-done | bytes 262176 | tf_op jit(solution)/shard_map/ppermute | solution.py:261
  43.1 2.6 %collective-permute-done.13.refs_10_ = bf16[8,128,128]{2,1,0:T(8,128)(2,1)S(1)} collective-permute-done((bf16[8,128,128]{2,1,0:T(8,128)(2,1)S(1)}, bf16[8,128,128]{2,1,0:T(8,128)(2,1)S(1)}, u32[]{:S(2)}, u32[]{:S(2)}) %collective-permute-start.13) | collective-permute-done | bytes 262176 | tf_op jit(solution)/shard_map/ppermute | solution.py:261
  49.7 2.2 %change_product.1 = (f32[8,128,128]{2,1,0:T(8,128)S(1)}, bf16[8,128,128]{2,1,0:T(8,128)(2,1)S(1)}, bf16[8,128,128]{2,1,0:T(8,128)(2,1)S(1)}, bf16[8,128,128]{2,1,0:T(8,128)(2,1)S(1)}) custom-call(s32[144]{0:T(256)S(1)} %pad_add_fusion.index_ref, bf16[8,128,128]{2,1,0:T(8,128)(2,1)S(1)} %collective-permute-done.refs_0_, ...), custom_call_target="tpu_custom_call" | custom-call | flops 268435456 | bytes 4194304 | tf_op jit(solution)/shard_map/change_product/pallas_call | solution.py:361
  51.9 2.9 %collective-permute-start.20 = (bf16[8,128,128]{2,1,0:T(8,128)(2,1)S(1)}, bf16[8,128,128]{2,1,0:T(8,128)(2,1)S(1)}, u32[]{:S(2)}, u32[]{:S(2)}) collective-permute-start(bf16[8,128,128]{2,1,0:T(8,128)(2,1)S(1)} %get-tuple-element.43), channel_id=1, source_target_pairs={{0,6},{1,7},{2,4},{3,5},{4,2},{5,3},{6,0},{7,1},{8,14},{9,15},{10,... | collective-permute-start | bytes 786440 | tf_op jit(solution)/shard_map/ppermute | solution.py:261
  57.3 6.1 %collective-permute-done.26.refs_2_ = bf16[8,128,128]{2,1,0:T(8,128)(2,1)S(1)} collective-permute-done((bf16[8,128,128]{2,1,0:T(8,128)(2,1)S(1)}, bf16[8,128,128]{2,1,0:T(8,128)(2,1)S(1)}, u32[]{:S(2)}, u32[]{:S(2)}) %collective-permute-start.26) | collective-permute-done | bytes 262176 | tf_op jit(solution)/shard_map/ppermute | solution.py:261
  63.6 2.5 %collective-permute-done.21 = bf16[8,128,128]{2,1,0:T(8,128)(2,1)S(1)} collective-permute-done((bf16[8,128,128]{2,1,0:T(8,128)(2,1)S(1)}, bf16[8,128,128]{2,1,0:T(8,128)(2,1)S(1)}, u32[]{:S(2)}, u32[]{:S(2)}) %collective-permute-start.21) | collective-permute-done | bytes 262176 | tf_op jit(solution)/shard_map/ppermute | solution.py:261
  67.8 2.8 %collective-permute-start.32 = (bf16[8,128,128]{2,1,0:T(8,128)(2,1)S(1)}, bf16[8,128,128]{2,1,0:T(8,128)(2,1)S(1)}, u32[]{:S(2)}, u32[]{:S(2)}) collective-permute-start(bf16[8,128,128]{2,1,0:T(8,128)(2,1)S(1)} %add_convert_fusion), channel_id=1, source_target_pairs={{0,0},{1,1},{2,16},{3,17},{4,8},{5,9},{6,24},{7,25},{8,20},{9,21},... | collective-permute-start | bytes 786440 | tf_op jit(solution)/shard_map/ppermute | solution.py:261
  70.9 2.8 %collective-permute-start.23 = (bf16[8,128,128]{2,1,0:T(8,128)(2,1)S(1)}, bf16[8,128,128]{2,1,0:T(8,128)(2,1)S(1)}, u32[]{:S(2)}, u32[]{:S(2)}) collective-permute-start(bf16[8,128,128]{2,1,0:T(8,128)(2,1)S(1)} %add_convert_fusion), channel_id=1, source_target_pairs={{0,0},{1,1},{2,2},{3,3},{4,4},{5,5},{6,6},{7,7},{8,10},{9,11},{10,... | collective-permute-start | bytes 786440 | tf_op jit(solution)/shard_map/ppermute | solution.py:261
  75.5 4.8 %collective-permute-done.32.refs_8_ = bf16[8,128,128]{2,1,0:T(8,128)(2,1)S(1)} collective-permute-done((bf16[8,128,128]{2,1,0:T(8,128)(2,1)S(1)}, bf16[8,128,128]{2,1,0:T(8,128)(2,1)S(1)}, u32[]{:S(2)}, u32[]{:S(2)}) %collective-permute-start.32) | collective-permute-done | bytes 262176 | tf_op jit(solution)/shard_map/ppermute | solution.py:261
  82.2 2.3 %commutator_product.1 = (f32[8,128,128]{2,1,0:T(8,128)S(1)}, bf16[1040,128]{1,0:T(8,128)(2,1)S(1)}, bf16[1040,128]{1,0:T(8,128)(2,1)S(1)}, bf16[1040,128]{1,0:T(8,128)(2,1)S(1)}, bf16[16,128]{1,0:T(8,128)(2,1)S(1)}) custom-call(s32[144]{0:T(256)S(1)} %pad_add_fusion.index_ref, bf16[8,128,128]{2,1,0:T(8,128)(2,1)S(1)} %collective-permute-done.23.own_ref, ...), custom_call_target="tpu_custom_call" | custom-call | flops 268435456 | bytes 4194304 | tf_op jit(solution)/shard_map/commutator_product/pallas_call | solution.py:388
  85.7 4.4 %collective-permute-start.35 = (bf16[1040,128]{1,0:T(8,128)(2,1)S(1)}, bf16[1040,128]{1,0:T(8,128)(2,1)S(1)}, u32[]{:S(2)}, u32[]{:S(2)}) collective-permute-start(bf16[1040,128]{1,0:T(8,128)(2,1)S(1)} %get-tuple-element.54), channel_id=1, source_target_pairs={{0,2},{1,3},{2,0},{3,1},{4,6},{5,7},{6,4},{7,5},{8,10},{9,11},{10,... | collective-permute-start | bytes 798728 | tf_op jit(solution)/shard_map/ppermute | solution.py:261
  91.5 2.1 %collective-permute-done.34.refs_0_ = bf16[1040,128]{1,0:T(8,128)(2,1)S(1)} collective-permute-done((bf16[1040,128]{1,0:T(8,128)(2,1)S(1)}, bf16[1040,128]{1,0:T(8,128)(2,1)S(1)}, u32[]{:S(2)}, u32[]{:S(2)}) %collective-permute-start.34) | collective-permute-done | bytes 266272 | tf_op jit(solution)/shard_map/ppermute | solution.py:261
  93.6 8.8 %collective-permute-done.35.refs_1_ = bf16[1040,128]{1,0:T(8,128)(2,1)S(1)} collective-permute-done((bf16[1040,128]{1,0:T(8,128)(2,1)S(1)}, bf16[1040,128]{1,0:T(8,128)(2,1)S(1)}, u32[]{:S(2)}, u32[]{:S(2)}) %collective-permute-start.35) | collective-permute-done | bytes 266272 | tf_op jit(solution)/shard_map/ppermute | solution.py:261
  102.7 2.2 %collective-permute-start.37 = (bf16[1040,128]{1,0:T(8,128)(2,1)S(1)}, bf16[1040,128]{1,0:T(8,128)(2,1)S(1)}, u32[]{:S(2)}, u32[]{:S(2)}) collective-permute-start(bf16[1040,128]{1,0:T(8,128)(2,1)S(1)} %plane_sum.1.own_ref), channel_id=1, source_target_pairs={{0,0},{1,1},{2,20},{3,21},{4,10},{5,11},{6,30},{7,31},{8,16},{9,17... | collective-permute-start | bytes 798728 | tf_op jit(solution)/shard_map/ppermute | solution.py:261
  105.0 10.2 %collective-permute-done.37.refs_0_ = bf16[1040,128]{1,0:T(8,128)(2,1)S(1)} collective-permute-done((bf16[1040,128]{1,0:T(8,128)(2,1)S(1)}, bf16[1040,128]{1,0:T(8,128)(2,1)S(1)}, u32[]{:S(2)}, u32[]{:S(2)}) %collective-permute-start.37) | collective-permute-done | bytes 266272 | tf_op jit(solution)/shard_map/ppermute | solution.py:261
  117.5 1.9 %collective-permute-start.39 = (bf16[8,128,128]{2,1,0:T(8,128)(2,1)S(1)}, bf16[8,128,128]{2,1,0:T(8,128)(2,1)S(1)}, u32[]{:S(2)}, u32[]{:S(2)}) collective-permute-start(bf16[8,128,128]{2,1,0:T(8,128)(2,1)S(1)} %commutator_difference.1), channel_id=1, source_target_pairs={{0,0},{1,4},{2,2},{3,6},{4,1},{5,5},{6,3},{7,7},{8,10},{9,14},{10,... | collective-permute-start | bytes 786440 | tf_op jit(solution)/shard_map/ppermute | solution.py:261
  120.5 2.5 %collective-permute-start.41 = (f32[8,128]{1,0:T(8,128)S(1)}, f32[8,128]{1,0:T(8,128)S(1)}, u32[]{:S(2)}, u32[]{:S(2)}) collective-permute-start(f32[8,128]{1,0:T(8,128)S(1)} %fusion.4), channel_id=1, source_target_pairs={{0,2},{1,3},{2,0},{3,1},{4,6},{5,7},{6,4},{7,5},{8,10},{9,11},{10,... | collective-permute-start | bytes 12296 | tf_op jit(solution)/shard_map/ppermute | solution.py:261
  123.2 5.2 %collective-permute-done.41 = f32[8,128]{1,0:T(8,128)S(1)} collective-permute-done((f32[8,128]{1,0:T(8,128)S(1)}, f32[8,128]{1,0:T(8,128)S(1)}, u32[]{:S(2)}, u32[]{:S(2)}) %collective-permute-start.41) | collective-permute-done | bytes 4128 | tf_op jit(solution)/shard_map/ppermute | solution.py:261
  (136 shorter events, 43.4 us)
Async XLA Ops:
  0.6 15.8 %collective-permute-start.2 = (bf16[8,128,128]{2,1,0:T(8,128)(2,1)}, bf16[8,128,128]{2,1,0:T(8,128)(2,1)S(1)}, u32[]{:S(2)}, u32[]{:S(2)}) collective-permute-start(bf16[8,128,128]{2,1,0:T(8,128)(2,1)} %bitcast.58), channel_id=1, source_target_pairs={{0,16},{1,20},{2,18},{3,22},{4,17},{5,21},{6,19},{7,23},{8,24},{9,... | collective-permute-start | bytes 786440 | tf_op jit(solution)/shard_map/ppermute | solution.py:261
  1.0 17.4 %collective-permute-start.1 = (bf16[8,128,128]{2,1,0:T(8,128)(2,1)}, bf16[8,128,128]{2,1,0:T(8,128)(2,1)S(1)}, u32[]{:S(2)}, u32[]{:S(2)}) collective-permute-start(bf16[8,128,128]{2,1,0:T(8,128)(2,1)} %bitcast.59), channel_id=1, source_target_pairs={{0,8},{1,12},{2,10},{3,14},{4,9},{5,13},{6,11},{7,15},{8,0},{9,4},... | collective-permute-start | bytes 786440 | tf_op jit(solution)/shard_map/ppermute | solution.py:261
  1.5 22.8 %collective-permute-start.7 = (bf16[8,128,128]{2,1,0:T(8,128)(2,1)}, bf16[8,128,128]{2,1,0:T(8,128)(2,1)S(1)}, u32[]{:S(2)}, u32[]{:S(2)}) collective-permute-start(bf16[8,128,128]{2,1,0:T(8,128)(2,1)} %bitcast.60), channel_id=1, source_target_pairs={{0,0},{1,4},{2,2},{3,6},{4,1},{5,5},{6,3},{7,7},{8,8},{9,12},{10,1... | collective-permute-start | bytes 786440 | tf_op jit(solution)/shard_map/ppermute | solution.py:261
  3.1 21.2 %collective-permute-start.6 = (bf16[8,128,128]{2,1,0:T(8,128)(2,1)}, bf16[8,128,128]{2,1,0:T(8,128)(2,1)S(1)}, u32[]{:S(2)}, u32[]{:S(2)}) collective-permute-start(bf16[8,128,128]{2,1,0:T(8,128)(2,1)} %bitcast.61), channel_id=1, source_target_pairs={{0,0},{1,4},{2,2},{3,6},{4,1},{5,5},{6,3},{7,7},{8,8},{9,12},{10,1... | collective-permute-start | bytes 786440 | tf_op jit(solution)/shard_map/ppermute | solution.py:261
  4.7 13.8 %collective-permute-start = (bf16[8,128,128]{2,1,0:T(8,128)(2,1)}, bf16[8,128,128]{2,1,0:T(8,128)(2,1)S(1)}, u32[]{:S(2)}, u32[]{:S(2)}) collective-permute-start(bf16[8,128,128]{2,1,0:T(8,128)(2,1)} %bitcast.57), channel_id=1, source_target_pairs={{0,0},{1,4},{2,2},{3,6},{4,1},{5,5},{6,3},{7,7},{8,8},{9,12},{10,1... | collective-permute-start | bytes 786440 | tf_op jit(solution)/shard_map/ppermute | solution.py:261
  16.5 10.8 %collective-permute-start.3 = (bf16[8,128,128]{2,1,0:T(8,128)(2,1)S(1)}, bf16[8,128,128]{2,1,0:T(8,128)(2,1)S(1)}, u32[]{:S(2)}, u32[]{:S(2)}) collective-permute-start(bf16[8,128,128]{2,1,0:T(8,128)(2,1)S(1)} %collective-permute-done.2.refs_2_), channel_id=1, source_target_pairs={{0,8},{1,9},{2,10},{3,11},{4,12},{5,13},{6,14},{7,15},{8,0},{9,1},... | collective-permute-start | bytes 786440 | tf_op jit(solution)/shard_map/ppermute | solution.py:261
  18.4 17.4 %collective-permute-start.5 = (bf16[8,128,128]{2,1,0:T(8,128)(2,1)S(1)}, bf16[8,128,128]{2,1,0:T(8,128)(2,1)S(1)}, u32[]{:S(2)}, u32[]{:S(2)}) collective-permute-start(bf16[8,128,128]{2,1,0:T(8,128)(2,1)S(1)} %collective-permute-done.refs_0_), channel_id=1, source_target_pairs={{0,16},{1,17},{2,18},{3,19},{4,20},{5,21},{6,22},{7,23},{8,24},{9,... | collective-permute-start | bytes 786440 | tf_op jit(solution)/shard_map/ppermute | solution.py:261
  29.5 10.5 %collective-permute-start.4 = (bf16[8,128,128]{2,1,0:T(8,128)(2,1)S(1)}, bf16[8,128,128]{2,1,0:T(8,128)(2,1)S(1)}, u32[]{:S(2)}, u32[]{:S(2)}) collective-permute-start(bf16[8,128,128]{2,1,0:T(8,128)(2,1)S(1)} %collective-permute-done.refs_0_), channel_id=1, source_target_pairs={{0,8},{1,9},{2,10},{3,11},{4,12},{5,13},{6,14},{7,15},{8,0},{9,1},... | collective-permute-start | bytes 786440 | tf_op jit(solution)/shard_map/ppermute | solution.py:261
  32.3 13.4 %collective-permute-start.13 = (bf16[8,128,128]{2,1,0:T(8,128)(2,1)S(1)}, bf16[8,128,128]{2,1,0:T(8,128)(2,1)S(1)}, u32[]{:S(2)}, u32[]{:S(2)}) collective-permute-start(bf16[8,128,128]{2,1,0:T(8,128)(2,1)S(1)} %get-tuple-element.36), channel_id=1, source_target_pairs={{0,2},{1,3},{2,0},{3,1},{4,6},{5,7},{6,4},{7,5},{8,10},{9,11},{10,... | collective-permute-start | bytes 786440 | tf_op jit(solution)/shard_map/ppermute | solution.py:261
  33.7 13.7 %collective-permute-start.14 = (bf16[8,128,128]{2,1,0:T(8,128)(2,1)S(1)}, bf16[8,128,128]{2,1,0:T(8,128)(2,1)S(1)}, u32[]{:S(2)}, u32[]{:S(2)}) collective-permute-start(bf16[8,128,128]{2,1,0:T(8,128)(2,1)S(1)} %get-tuple-element.37), channel_id=1, source_target_pairs={{0,4},{1,5},{2,6},{3,7},{4,0},{5,1},{6,2},{7,3},{8,12},{9,13},{10,... | collective-permute-start | bytes 786440 | tf_op jit(solution)/shard_map/ppermute | solution.py:261
  35.8 11.6 %collective-permute-start.15 = (bf16[8,128,128]{2,1,0:T(8,128)(2,1)S(1)}, bf16[8,128,128]{2,1,0:T(8,128)(2,1)S(1)}, u32[]{:S(2)}, u32[]{:S(2)}) collective-permute-start(bf16[8,128,128]{2,1,0:T(8,128)(2,1)S(1)} %collective-permute-done.5.refs_2_), channel_id=1, source_target_pairs={{0,8},{1,9},{2,10},{3,11},{4,12},{5,13},{6,14},{7,15},{8,0},{9,1},... | collective-permute-start | bytes 786440 | tf_op jit(solution)/shard_map/ppermute | solution.py:261
  48.0 15.5 %collective-permute-start.26 = (bf16[8,128,128]{2,1,0:T(8,128)(2,1)S(1)}, bf16[8,128,128]{2,1,0:T(8,128)(2,1)S(1)}, u32[]{:S(2)}, u32[]{:S(2)}) collective-permute-start(bf16[8,128,128]{2,1,0:T(8,128)(2,1)S(1)} %collective-permute-done.24.refs_0_), channel_id=1, source_target_pairs={{0,16},{1,17},{2,18},{3,19},{4,20},{5,21},{6,22},{7,23},{8,24},{9,... | collective-permute-start | bytes 786440 | tf_op jit(solution)/shard_map/ppermute | solution.py:261
  51.9 11.6 %collective-permute-start.20 = (bf16[8,128,128]{2,1,0:T(8,128)(2,1)S(1)}, bf16[8,128,128]{2,1,0:T(8,128)(2,1)S(1)}, u32[]{:S(2)}, u32[]{:S(2)}) collective-permute-start(bf16[8,128,128]{2,1,0:T(8,128)(2,1)S(1)} %get-tuple-element.43), channel_id=1, source_target_pairs={{0,6},{1,7},{2,4},{3,5},{4,2},{5,3},{6,0},{7,1},{8,14},{9,15},{10,... | collective-permute-start | bytes 786440 | tf_op jit(solution)/shard_map/ppermute | solution.py:261
  54.8 11.2 %collective-permute-start.21 = (bf16[8,128,128]{2,1,0:T(8,128)(2,1)S(1)}, bf16[8,128,128]{2,1,0:T(8,128)(2,1)S(1)}, u32[]{:S(2)}, u32[]{:S(2)}) collective-permute-start(bf16[8,128,128]{2,1,0:T(8,128)(2,1)S(1)} %get-tuple-element.44), channel_id=1, source_target_pairs={{0,2},{1,3},{2,0},{3,1},{4,6},{5,7},{6,4},{7,5},{8,10},{9,11},{10,... | collective-permute-start | bytes 786440 | tf_op jit(solution)/shard_map/ppermute | solution.py:261
  56.3 11.4 %collective-permute-start.22 = (bf16[8,128,128]{2,1,0:T(8,128)(2,1)S(1)}, bf16[8,128,128]{2,1,0:T(8,128)(2,1)S(1)}, u32[]{:S(2)}, u32[]{:S(2)}) collective-permute-start(bf16[8,128,128]{2,1,0:T(8,128)(2,1)S(1)} %get-tuple-element.45), channel_id=1, source_target_pairs={{0,4},{1,5},{2,6},{3,7},{4,0},{5,1},{6,2},{7,3},{8,12},{9,13},{10,... | collective-permute-start | bytes 786440 | tf_op jit(solution)/shard_map/ppermute | solution.py:261
  56.3 14.6 %collective-permute-start.25 = (bf16[8,128,128]{2,1,0:T(8,128)(2,1)S(1)}, bf16[8,128,128]{2,1,0:T(8,128)(2,1)S(1)}, u32[]{:S(2)}, u32[]{:S(2)}) collective-permute-start(bf16[8,128,128]{2,1,0:T(8,128)(2,1)S(1)} %collective-permute-done.24.refs_0_), channel_id=1, source_target_pairs={{0,8},{1,9},{2,10},{3,11},{4,12},{5,13},{6,14},{7,15},{8,0},{9,1},... | collective-permute-start | bytes 786440 | tf_op jit(solution)/shard_map/ppermute | solution.py:261
  63.4 11.6 %collective-permute-start.28 = (bf16[8,128,128]{2,1,0:T(8,128)(2,1)S(1)}, bf16[8,128,128]{2,1,0:T(8,128)(2,1)S(1)}, u32[]{:S(2)}, u32[]{:S(2)}) collective-permute-start(bf16[8,128,128]{2,1,0:T(8,128)(2,1)S(1)} %collective-permute-done.24.refs_0_), channel_id=1, source_target_pairs={{0,1},{1,0},{2,3},{3,2},{4,5},{5,4},{6,7},{7,6},{8,9},{9,8},{10,11... | collective-permute-start | bytes 786440 | tf_op jit(solution)/shard_map/ppermute | solution.py:261
  63.6 11.4 %collective-permute-start.27 = (bf16[8,128,128]{2,1,0:T(8,128)(2,1)S(1)}, bf16[8,128,128]{2,1,0:T(8,128)(2,1)S(1)}, u32[]{:S(2)}, u32[]{:S(2)}) collective-permute-start(bf16[8,128,128]{2,1,0:T(8,128)(2,1)S(1)} %collective-permute-done.26.refs_2_), channel_id=1, source_target_pairs={{0,8},{1,9},{2,10},{3,11},{4,12},{5,13},{6,14},{7,15},{8,0},{9,1},... | collective-permute-start | bytes 786440 | tf_op jit(solution)/shard_map/ppermute | solution.py:261
  67.8 12.5 %collective-permute-start.32 = (bf16[8,128,128]{2,1,0:T(8,128)(2,1)S(1)}, bf16[8,128,128]{2,1,0:T(8,128)(2,1)S(1)}, u32[]{:S(2)}, u32[]{:S(2)}) collective-permute-start(bf16[8,128,128]{2,1,0:T(8,128)(2,1)S(1)} %add_convert_fusion), channel_id=1, source_target_pairs={{0,0},{1,1},{2,16},{3,17},{4,8},{5,9},{6,24},{7,25},{8,20},{9,21},... | collective-permute-start | bytes 786440 | tf_op jit(solution)/shard_map/ppermute | solution.py:261
  70.9 11.2 %collective-permute-start.23 = (bf16[8,128,128]{2,1,0:T(8,128)(2,1)S(1)}, bf16[8,128,128]{2,1,0:T(8,128)(2,1)S(1)}, u32[]{:S(2)}, u32[]{:S(2)}) collective-permute-start(bf16[8,128,128]{2,1,0:T(8,128)(2,1)S(1)} %add_convert_fusion), channel_id=1, source_target_pairs={{0,0},{1,1},{2,2},{3,3},{4,4},{5,5},{6,6},{7,7},{8,10},{9,11},{10,... | collective-permute-start | bytes 786440 | tf_op jit(solution)/shard_map/ppermute | solution.py:261
  85.7 16.7 %collective-permute-start.35 = (bf16[1040,128]{1,0:T(8,128)(2,1)S(1)}, bf16[1040,128]{1,0:T(8,128)(2,1)S(1)}, u32[]{:S(2)}, u32[]{:S(2)}) collective-permute-start(bf16[1040,128]{1,0:T(8,128)(2,1)S(1)} %get-tuple-element.54), channel_id=1, source_target_pairs={{0,2},{1,3},{2,0},{3,1},{4,6},{5,7},{6,4},{7,5},{8,10},{9,11},{10,... | collective-permute-start | bytes 798728 | tf_op jit(solution)/shard_map/ppermute | solution.py:261
  90.1 12.3 %collective-permute-start.36 = (bf16[1040,128]{1,0:T(8,128)(2,1)S(1)}, bf16[1040,128]{1,0:T(8,128)(2,1)S(1)}, u32[]{:S(2)}, u32[]{:S(2)}) collective-permute-start(bf16[1040,128]{1,0:T(8,128)(2,1)S(1)} %get-tuple-element.55), channel_id=1, source_target_pairs={{0,4},{1,5},{2,6},{3,7},{4,0},{5,1},{6,2},{7,3},{8,12},{9,13},{10,... | collective-permute-start | bytes 798728 | tf_op jit(solution)/shard_map/ppermute | solution.py:261
  102.7 12.4 %collective-permute-start.37 = (bf16[1040,128]{1,0:T(8,128)(2,1)S(1)}, bf16[1040,128]{1,0:T(8,128)(2,1)S(1)}, u32[]{:S(2)}, u32[]{:S(2)}) collective-permute-start(bf16[1040,128]{1,0:T(8,128)(2,1)S(1)} %plane_sum.1.own_ref), channel_id=1, source_target_pairs={{0,0},{1,1},{2,20},{3,21},{4,10},{5,11},{6,30},{7,31},{8,16},{9,17... | collective-permute-start | bytes 798728 | tf_op jit(solution)/shard_map/ppermute | solution.py:261
  117.5 12.4 %collective-permute-start.39 = (bf16[8,128,128]{2,1,0:T(8,128)(2,1)S(1)}, bf16[8,128,128]{2,1,0:T(8,128)(2,1)S(1)}, u32[]{:S(2)}, u32[]{:S(2)}) collective-permute-start(bf16[8,128,128]{2,1,0:T(8,128)(2,1)S(1)} %commutator_difference.1), channel_id=1, source_target_pairs={{0,0},{1,4},{2,2},{3,6},{4,1},{5,5},{6,3},{7,7},{8,10},{9,14},{10,... | collective-permute-start | bytes 786440 | tf_op jit(solution)/shard_map/ppermute | solution.py:261
  (21 other events, 116.8 us)

commit v6 on v5

--- a/solution.py
+++ b/solution.py
@@ -281,9 +281,9 @@
     def listed(pieces, shared):
         return [pieces[m] for m in range(outer)] + [shared[m] for m in range(outer)]
 
-    def mirror(x, target):
+    def mirror(x, target, done=()):
         moved = inside_permute(x, lambda o, h, g: (g, h, o), inside_spread, target)
-        return [moved, share(moved)]
+        return [moved, share(after(moved, done))]
 
     def exchange(outs):
         return [outs[0]] + [
@@ -354,7 +354,7 @@
     dens_beside = {0: share(dens_own)}
     dens_far = {m + 1: to_plane(after(dens_near[m], outs), 1) for m in far_from}
     kohn_behind = after(kohn_own, (dens_near, outs))
-    kohn_pieces = {m: to_plane(kohn_behind, m) for m in far_from}
+    kohn_pieces = {m: to_plane(kohn_behind, m) for m in near}
     dens_near = after(dens_near, parts[1:])
     dens_beside |= share_all(dens_near) | share_all(dens_far)
     dens_all = listed({0: dens_own} | dens_near | dens_far, dens_beside)
@@ -378,11 +378,11 @@
     second_outs = outs
     total = total_of(exchange(outs))
 
-    mirrored = mirror(total, at)
     own = inside_permute(total, lambda o, h, g: (o, h, g), inside_spread)
+    mirrored = mirror(total, at, own)
     kohn_pieces = {0: kohn_own} | after(kohn_pieces, second_outs)
     kohn_beside = share_all(kohn_pieces)
-    kohn_last = {m + 1: to_plane(kohn_pieces[m], 1) for m in range(0, outer, 2)}
+    kohn_last = {m + 1: to_plane(kohn_pieces[m], 1) for m in far_from}
     kohn_last = after(kohn_last, total)
     kohn_all = listed(kohn_pieces | kohn_last, kohn_beside | share_all(kohn_last))
     *outs, trace = pl.pallas_call(

time: 132 us -> 134 us (1.015)
  starting transfers between devices: 47.5 us -> 49.4 us
    ppermute x43, starting transfers between devices: 47.5 us -> 49.4 us  [permute(): return lax.ppermute(x, ('row', 'col'), row_major_perm(n_row, n_col, target))]
where the time goes in v6:
time: 134 us; the launch traced here: 133 us
  waiting for transfers between devices  61.8 us (46%)
  starting transfers between devices  49.4 us (37%)
  Pallas kernels  7.78 us (6%)
  local copies, waits for them, and re-layouts  7.35 us (5%)
  other arithmetic  3.74 us (3%)
  between operations  2.76 us (2%)
    ppermute x43, waiting for transfers between devices, permute(): return lax.ppermute(x, ('row', 'col'), row_major_perm(n_row, n_col, target))  61.8 us
    ppermute x43, starting transfers between devices, permute(): return lax.ppermute(x, ('row', 'col'), row_major_perm(n_row, n_col, target))  49.4 us
  transfers between devices with their start and end apart: 43, of which 22 were waited for; matrix products, arithmetic and copies ran while one was open for 7% of the time, Pallas kernels for 3%

profile of v6, /device:TPU:26, one launch (start us, length us, event | category | flops | bytes accessed | tf_op | source)
XLA Modules:
  0.0 132.8 jit_solution(14905841068125268456)
XLA Ops:
  13.6 2.9 %collective-permute-done.2.refs_2_ = bf16[8,128,128]{2,1,0:T(8,128)(2,1)S(1)} collective-permute-done((bf16[8,128,128]{2,1,0:T(8,128)(2,1)}, bf16[8,128,128]{2,1,0:T(8,128)(2,1)S(1)}, u32[]{:S(2)}, u32[]{:S(2)}) %collective-permute-start.2) | collective-permute-done | bytes 262176 | tf_op jit(solution)/shard_map/ppermute | solution.py:261
  19.8 4.4 %collective-permute-start.10 = (bf16[8,128,128]{2,1,0:T(8,128)(2,1)S(1)}, bf16[8,128,128]{2,1,0:T(8,128)(2,1)S(1)}, u32[]{:S(2)}, u32[]{:S(2)}) collective-permute-start(bf16[8,128,128]{2,1,0:T(8,128)(2,1)S(1)} %collective-permute-done.2.refs_2_), channel_id=1, source_target_pairs={{0,1},{1,0},{2,3},{3,2},{4,5},{5,4},{6,7},{7,6},{8,9},{9,8},{10,11... | collective-permute-start | bytes 786440 | tf_op jit(solution)/shard_map/ppermute | solution.py:261
  24.8 2.5 %collective-permute-done.3.refs_3_ = bf16[8,128,128]{2,1,0:T(8,128)(2,1)S(1)} collective-permute-done((bf16[8,128,128]{2,1,0:T(8,128)(2,1)S(1)}, bf16[8,128,128]{2,1,0:T(8,128)(2,1)S(1)}, u32[]{:S(2)}, u32[]{:S(2)}) %collective-permute-start.3) | collective-permute-done | bytes 262176 | tf_op jit(solution)/shard_map/ppermute | solution.py:261
  30.1 2.1 %scaled_step_product.1 = (f32[8,128,128]{2,1,0:T(8,128)S(1)}, bf16[8,128,128]{2,1,0:T(8,128)(2,1)S(1)}, bf16[8,128,128]{2,1,0:T(8,128)(2,1)S(1)}, bf16[8,128,128]{2,1,0:T(8,128)(2,1)S(1)}) custom-call(s32[144]{0:T(256)S(1)} %pad_add_fusion.index_ref, bf16[8,128,128]{2,1,0:T(8,128)(2,1)S(1)} %collective-permute-done.6.left_ref, ...), custom_call_target="tpu_custom_call" | custom-call | flops 268435456 | bytes 4194304 | tf_op jit(solution)/shard_map/scaled_step_product/pallas_call | solution.py:342
  37.3 2.7 %collective-permute-done.4.refs_1_ = bf16[8,128,128]{2,1,0:T(8,128)(2,1)S(1)} collective-permute-done((bf16[8,128,128]{2,1,0:T(8,128)(2,1)S(1)}, bf16[8,128,128]{2,1,0:T(8,128)(2,1)S(1)}, u32[]{:S(2)}, u32[]{:S(2)}) %collective-permute-start.4) | collective-permute-done | bytes 262176 | tf_op jit(solution)/shard_map/ppermute | solution.py:261
  39.9 2.4 %collective-permute-done.12.refs_9_ = bf16[8,128,128]{2,1,0:T(8,128)(2,1)S(1)} collective-permute-done((bf16[8,128,128]{2,1,0:T(8,128)(2,1)S(1)}, bf16[8,128,128]{2,1,0:T(8,128)(2,1)S(1)}, u32[]{:S(2)}, u32[]{:S(2)}) %collective-permute-start.12) | collective-permute-done | bytes 262176 | tf_op jit(solution)/shard_map/ppermute | solution.py:261
  43.1 2.6 %collective-permute-done.13.refs_10_ = bf16[8,128,128]{2,1,0:T(8,128)(2,1)S(1)} collective-permute-done((bf16[8,128,128]{2,1,0:T(8,128)(2,1)S(1)}, bf16[8,128,128]{2,1,0:T(8,128)(2,1)S(1)}, u32[]{:S(2)}, u32[]{:S(2)}) %collective-permute-start.13) | collective-permute-done | bytes 262176 | tf_op jit(solution)/shard_map/ppermute | solution.py:261
  50.0 2.3 %change_product.1 = (f32[8,128,128]{2,1,0:T(8,128)S(1)}, bf16[8,128,128]{2,1,0:T(8,128)(2,1)S(1)}, bf16[8,128,128]{2,1,0:T(8,128)(2,1)S(1)}, bf16[8,128,128]{2,1,0:T(8,128)(2,1)S(1)}) custom-call(s32[144]{0:T(256)S(1)} %pad_add_fusion.index_ref, bf16[8,128,128]{2,1,0:T(8,128)(2,1)S(1)} %collective-permute-done.refs_0_, ...), custom_call_target="tpu_custom_call" | custom-call | flops 268435456 | bytes 4194304 | tf_op jit(solution)/shard_map/change_product/pallas_call | solution.py:361
  52.2 3.5 %collective-permute-start.20 = (bf16[8,128,128]{2,1,0:T(8,128)(2,1)S(1)}, bf16[8,128,128]{2,1,0:T(8,128)(2,1)S(1)}, u32[]{:S(2)}, u32[]{:S(2)}) collective-permute-start(bf16[8,128,128]{2,1,0:T(8,128)(2,1)S(1)} %get-tuple-element.44), channel_id=1, source_target_pairs={{0,6},{1,7},{2,4},{3,5},{4,2},{5,3},{6,0},{7,1},{8,14},{9,15},{10,... | collective-permute-start | bytes 786440 | tf_op jit(solution)/shard_map/ppermute | solution.py:261
  57.3 3.0 %collective-permute-done.25.refs_1_ = bf16[8,128,128]{2,1,0:T(8,128)(2,1)S(1)} collective-permute-done((bf16[8,128,128]{2,1,0:T(8,128)(2,1)S(1)}, bf16[8,128,128]{2,1,0:T(8,128)(2,1)S(1)}, u32[]{:S(2)}, u32[]{:S(2)}) %collective-permute-start.25) | collective-permute-done | bytes 262176 | tf_op jit(solution)/shard_map/ppermute | solution.py:261
  60.3 3.4 %collective-permute-done.26.refs_2_ = bf16[8,128,128]{2,1,0:T(8,128)(2,1)S(1)} collective-permute-done((bf16[8,128,128]{2,1,0:T(8,128)(2,1)S(1)}, bf16[8,128,128]{2,1,0:T(8,128)(2,1)S(1)}, u32[]{:S(2)}, u32[]{:S(2)}) %collective-permute-start.26) | collective-permute-done | bytes 262176 | tf_op jit(solution)/shard_map/ppermute | solution.py:261
  63.7 2.9 %collective-permute-done.21 = bf16[8,128,128]{2,1,0:T(8,128)(2,1)S(1)} collective-permute-done((bf16[8,128,128]{2,1,0:T(8,128)(2,1)S(1)}, bf16[8,128,128]{2,1,0:T(8,128)(2,1)S(1)}, u32[]{:S(2)}, u32[]{:S(2)}) %collective-permute-start.21) | collective-permute-done | bytes 262176 | tf_op jit(solution)/shard_map/ppermute | solution.py:261
  68.7 2.5 %collective-permute-start.23 = (bf16[8,128,128]{2,1,0:T(8,128)(2,1)S(1)}, bf16[8,128,128]{2,1,0:T(8,128)(2,1)S(1)}, u32[]{:S(2)}, u32[]{:S(2)}) collective-permute-start(bf16[8,128,128]{2,1,0:T(8,128)(2,1)S(1)} %add_convert_fusion), channel_id=1, source_target_pairs={{0,0},{1,1},{2,2},{3,3},{4,4},{5,5},{6,6},{7,7},{8,10},{9,11},{10,... | collective-permute-start | bytes 786440 | tf_op jit(solution)/shard_map/ppermute | solution.py:261
  71.2 3.3 %collective-permute-start.32 = (bf16[8,128,128]{2,1,0:T(8,128)(2,1)S(1)}, bf16[8,128,128]{2,1,0:T(8,128)(2,1)S(1)}, u32[]{:S(2)}, u32[]{:S(2)}) collective-permute-start(bf16[8,128,128]{2,1,0:T(8,128)(2,1)S(1)} %add_convert_fusion), channel_id=1, source_target_pairs={{0,0},{1,1},{2,16},{3,17},{4,8},{5,9},{6,24},{7,25},{8,20},{9,21},... | collective-permute-start | bytes 786440 | tf_op jit(solution)/shard_map/ppermute | solution.py:261
  75.2 4.5 %collective-permute-done.23.own_ref = bf16[8,128,128]{2,1,0:T(8,128)(2,1)S(1)} collective-permute-done((bf16[8,128,128]{2,1,0:T(8,128)(2,1)S(1)}, bf16[8,128,128]{2,1,0:T(8,128)(2,1)S(1)}, u32[]{:S(2)}, u32[]{:S(2)}) %collective-permute-start.23) | collective-permute-done | bytes 262176 | tf_op jit(solution)/shard_map/ppermute | solution.py:261
  82.2 2.3 %commutator_product.1 = (f32[8,128,128]{2,1,0:T(8,128)S(1)}, bf16[1040,128]{1,0:T(8,128)(2,1)S(1)}, bf16[1040,128]{1,0:T(8,128)(2,1)S(1)}, bf16[1040,128]{1,0:T(8,128)(2,1)S(1)}, bf16[16,128]{1,0:T(8,128)(2,1)S(1)}) custom-call(s32[144]{0:T(256)S(1)} %pad_add_fusion.index_ref, bf16[8,128,128]{2,1,0:T(8,128)(2,1)S(1)} %collective-permute-done.23.own_ref, ...), custom_call_target="tpu_custom_call" | custom-call | flops 268435456 | bytes 4194304 | tf_op jit(solution)/shard_map/commutator_product/pallas_call | solution.py:388
  84.5 3.6 %collective-permute-start.34 = (bf16[1040,128]{1,0:T(8,128)(2,1)S(1)}, bf16[1040,128]{1,0:T(8,128)(2,1)S(1)}, u32[]{:S(2)}, u32[]{:S(2)}) collective-permute-start(bf16[1040,128]{1,0:T(8,128)(2,1)S(1)} %get-tuple-element.55), channel_id=1, source_target_pairs={{0,6},{1,7},{2,4},{3,5},{4,2},{5,3},{6,0},{7,1},{8,14},{9,15},{10,... | collective-permute-start | bytes 798728 | tf_op jit(solution)/shard_map/ppermute | solution.py:261
  88.1 3.2 %collective-permute-start.35 = (bf16[1040,128]{1,0:T(8,128)(2,1)S(1)}, bf16[1040,128]{1,0:T(8,128)(2,1)S(1)}, u32[]{:S(2)}, u32[]{:S(2)}) collective-permute-start(bf16[1040,128]{1,0:T(8,128)(2,1)S(1)} %get-tuple-element.56), channel_id=1, source_target_pairs={{0,2},{1,3},{2,0},{3,1},{4,6},{5,7},{6,4},{7,5},{8,10},{9,11},{10,... | collective-permute-start | bytes 798728 | tf_op jit(solution)/shard_map/ppermute | solution.py:261
  91.5 3.8 %collective-permute-done.34.refs_0_ = bf16[1040,128]{1,0:T(8,128)(2,1)S(1)} collective-permute-done((bf16[1040,128]{1,0:T(8,128)(2,1)S(1)}, bf16[1040,128]{1,0:T(8,128)(2,1)S(1)}, u32[]{:S(2)}, u32[]{:S(2)}) %collective-permute-start.34) | collective-permute-done | bytes 266272 | tf_op jit(solution)/shard_map/ppermute | solution.py:261
  95.3 8.2 %collective-permute-done.35.refs_1_ = bf16[1040,128]{1,0:T(8,128)(2,1)S(1)} collective-permute-done((bf16[1040,128]{1,0:T(8,128)(2,1)S(1)}, bf16[1040,128]{1,0:T(8,128)(2,1)S(1)}, u32[]{:S(2)}, u32[]{:S(2)}) %collective-permute-start.35) | collective-permute-done | bytes 266272 | tf_op jit(solution)/shard_map/ppermute | solution.py:261
  103.8 3.4 %collective-permute-start.37 = (bf16[1040,128]{1,0:T(8,128)(2,1)S(1)}, bf16[1040,128]{1,0:T(8,128)(2,1)S(1)}, u32[]{:S(2)}, u32[]{:S(2)}) collective-permute-start(bf16[1040,128]{1,0:T(8,128)(2,1)S(1)} %plane_sum.1.own_ref), channel_id=1, source_target_pairs={{0,0},{1,1},{2,20},{3,21},{4,10},{5,11},{6,30},{7,31},{8,16},{9,17... | collective-permute-start | bytes 798728 | tf_op jit(solution)/shard_map/ppermute | solution.py:261
  107.2 8.8 %collective-permute-done.37.refs_0_ = bf16[1040,128]{1,0:T(8,128)(2,1)S(1)} collective-permute-done((bf16[1040,128]{1,0:T(8,128)(2,1)S(1)}, bf16[1040,128]{1,0:T(8,128)(2,1)S(1)}, u32[]{:S(2)}, u32[]{:S(2)}) %collective-permute-start.37) | collective-permute-done | bytes 266272 | tf_op jit(solution)/shard_map/ppermute | solution.py:261
  121.6 2.2 %collective-permute-start.41 = (f32[8,128]{1,0:T(8,128)S(1)}, f32[8,128]{1,0:T(8,128)S(1)}, u32[]{:S(2)}, u32[]{:S(2)}) collective-permute-start(f32[8,128]{1,0:T(8,128)S(1)} %fusion.4), channel_id=1, source_target_pairs={{0,2},{1,3},{2,0},{3,1},{4,6},{5,7},{6,4},{7,5},{8,10},{9,11},{10,... | collective-permute-start | bytes 12296 | tf_op jit(solution)/shard_map/ppermute | solution.py:261
  124.0 5.2 %collective-permute-done.41 = f32[8,128]{1,0:T(8,128)S(1)} collective-permute-done((f32[8,128]{1,0:T(8,128)S(1)}, f32[8,128]{1,0:T(8,128)S(1)}, u32[]{:S(2)}, u32[]{:S(2)}) %collective-permute-start.41) | collective-permute-done | bytes 4128 | tf_op jit(solution)/shard_map/ppermute | solution.py:261
  (136 shorter events, 44.2 us)
Async XLA Ops:
  0.6 15.8 %collective-permute-start.2 = (bf16[8,128,128]{2,1,0:T(8,128)(2,1)}, bf16[8,128,128]{2,1,0:T(8,128)(2,1)S(1)}, u32[]{:S(2)}, u32[]{:S(2)}) collective-permute-start(bf16[8,128,128]{2,1,0:T(8,128)(2,1)} %bitcast.58), channel_id=1, source_target_pairs={{0,16},{1,20},{2,18},{3,22},{4,17},{5,21},{6,19},{7,23},{8,24},{9,... | collective-permute-start | bytes 786440 | tf_op jit(solution)/shard_map/ppermute | solution.py:261
  1.0 17.4 %collective-permute-start.1 = (bf16[8,128,128]{2,1,0:T(8,128)(2,1)}, bf16[8,128,128]{2,1,0:T(8,128)(2,1)S(1)}, u32[]{:S(2)}, u32[]{:S(2)}) collective-permute-start(bf16[8,128,128]{2,1,0:T(8,128)(2,1)} %bitcast.59), channel_id=1, source_target_pairs={{0,8},{1,12},{2,10},{3,14},{4,9},{5,13},{6,11},{7,15},{8,0},{9,4},... | collective-permute-start | bytes 786440 | tf_op jit(solution)/shard_map/ppermute | solution.py:261
  1.5 22.8 %collective-permute-start.7 = (bf16[8,128,128]{2,1,0:T(8,128)(2,1)}, bf16[8,128,128]{2,1,0:T(8,128)(2,1)S(1)}, u32[]{:S(2)}, u32[]{:S(2)}) collective-permute-start(bf16[8,128,128]{2,1,0:T(8,128)(2,1)} %bitcast.60), channel_id=1, source_target_pairs={{0,0},{1,4},{2,2},{3,6},{4,1},{5,5},{6,3},{7,7},{8,8},{9,12},{10,1... | collective-permute-start | bytes 786440 | tf_op jit(solution)/shard_map/ppermute | solution.py:261
  3.1 21.2 %collective-permute-start.6 = (bf16[8,128,128]{2,1,0:T(8,128)(2,1)}, bf16[8,128,128]{2,1,0:T(8,128)(2,1)S(1)}, u32[]{:S(2)}, u32[]{:S(2)}) collective-permute-start(bf16[8,128,128]{2,1,0:T(8,128)(2,1)} %bitcast.61), channel_id=1, source_target_pairs={{0,0},{1,4},{2,2},{3,6},{4,1},{5,5},{6,3},{7,7},{8,8},{9,12},{10,1... | collective-permute-start | bytes 786440 | tf_op jit(solution)/shard_map/ppermute | solution.py:261
  4.7 13.8 %collective-permute-start = (bf16[8,128,128]{2,1,0:T(8,128)(2,1)}, bf16[8,128,128]{2,1,0:T(8,128)(2,1)S(1)}, u32[]{:S(2)}, u32[]{:S(2)}) collective-permute-start(bf16[8,128,128]{2,1,0:T(8,128)(2,1)} %bitcast.57), channel_id=1, source_target_pairs={{0,0},{1,4},{2,2},{3,6},{4,1},{5,5},{6,3},{7,7},{8,8},{9,12},{10,1... | collective-permute-start | bytes 786440 | tf_op jit(solution)/shard_map/ppermute | solution.py:261
  16.5 10.8 %collective-permute-start.3 = (bf16[8,128,128]{2,1,0:T(8,128)(2,1)S(1)}, bf16[8,128,128]{2,1,0:T(8,128)(2,1)S(1)}, u32[]{:S(2)}, u32[]{:S(2)}) collective-permute-start(bf16[8,128,128]{2,1,0:T(8,128)(2,1)S(1)} %collective-permute-done.2.refs_2_), channel_id=1, source_target_pairs={{0,8},{1,9},{2,10},{3,11},{4,12},{5,13},{6,14},{7,15},{8,0},{9,1},... | collective-permute-start | bytes 786440 | tf_op jit(solution)/shard_map/ppermute | solution.py:261
  18.4 17.4 %collective-permute-start.5 = (bf16[8,128,128]{2,1,0:T(8,128)(2,1)S(1)}, bf16[8,128,128]{2,1,0:T(8,128)(2,1)S(1)}, u32[]{:S(2)}, u32[]{:S(2)}) collective-permute-start(bf16[8,128,128]{2,1,0:T(8,128)(2,1)S(1)} %collective-permute-done.refs_0_), channel_id=1, source_target_pairs={{0,16},{1,17},{2,18},{3,19},{4,20},{5,21},{6,22},{7,23},{8,24},{9,... | collective-permute-start | bytes 786440 | tf_op jit(solution)/shard_map/ppermute | solution.py:261
  29.5 10.5 %collective-permute-start.4 = (bf16[8,128,128]{2,1,0:T(8,128)(2,1)S(1)}, bf16[8,128,128]{2,1,0:T(8,128)(2,1)S(1)}, u32[]{:S(2)}, u32[]{:S(2)}) collective-permute-start(bf16[8,128,128]{2,1,0:T(8,128)(2,1)S(1)} %collective-permute-done.refs_0_), channel_id=1, source_target_pairs={{0,8},{1,9},{2,10},{3,11},{4,12},{5,13},{6,14},{7,15},{8,0},{9,1},... | collective-permute-start | bytes 786440 | tf_op jit(solution)/shard_map/ppermute | solution.py:261
  32.2 10.2 %collective-permute-start.12 = (bf16[8,128,128]{2,1,0:T(8,128)(2,1)S(1)}, bf16[8,128,128]{2,1,0:T(8,128)(2,1)S(1)}, u32[]{:S(2)}, u32[]{:S(2)}) collective-permute-start(bf16[8,128,128]{2,1,0:T(8,128)(2,1)S(1)} %get-tuple-element.36), channel_id=1, source_target_pairs={{0,6},{1,7},{2,4},{3,5},{4,2},{5,3},{6,0},{7,1},{8,14},{9,15},{10,... | collective-permute-start | bytes 786440 | tf_op jit(solution)/shard_map/ppermute | solution.py:261
  32.3 13.4 %collective-permute-start.13 = (bf16[8,128,128]{2,1,0:T(8,128)(2,1)S(1)}, bf16[8,128,128]{2,1,0:T(8,128)(2,1)S(1)}, u32[]{:S(2)}, u32[]{:S(2)}) collective-permute-start(bf16[8,128,128]{2,1,0:T(8,128)(2,1)S(1)} %get-tuple-element.37), channel_id=1, source_target_pairs={{0,2},{1,3},{2,0},{3,1},{4,6},{5,7},{6,4},{7,5},{8,10},{9,11},{10,... | collective-permute-start | bytes 786440 | tf_op jit(solution)/shard_map/ppermute | solution.py:261
  33.7 13.7 %collective-permute-start.14 = (bf16[8,128,128]{2,1,0:T(8,128)(2,1)S(1)}, bf16[8,128,128]{2,1,0:T(8,128)(2,1)S(1)}, u32[]{:S(2)}, u32[]{:S(2)}) collective-permute-start(bf16[8,128,128]{2,1,0:T(8,128)(2,1)S(1)} %get-tuple-element.38), channel_id=1, source_target_pairs={{0,4},{1,5},{2,6},{3,7},{4,0},{5,1},{6,2},{7,3},{8,12},{9,13},{10,... | collective-permute-start | bytes 786440 | tf_op jit(solution)/shard_map/ppermute | solution.py:261
  35.8 11.6 %collective-permute-start.15 = (bf16[8,128,128]{2,1,0:T(8,128)(2,1)S(1)}, bf16[8,128,128]{2,1,0:T(8,128)(2,1)S(1)}, u32[]{:S(2)}, u32[]{:S(2)}) collective-permute-start(bf16[8,128,128]{2,1,0:T(8,128)(2,1)S(1)} %collective-permute-done.5.refs_2_), channel_id=1, source_target_pairs={{0,8},{1,9},{2,10},{3,11},{4,12},{5,13},{6,14},{7,15},{8,0},{9,1},... | collective-permute-start | bytes 786440 | tf_op jit(solution)/shard_map/ppermute | solution.py:261
  48.0 12.3 %collective-permute-start.25 = (bf16[8,128,128]{2,1,0:T(8,128)(2,1)S(1)}, bf16[8,128,128]{2,1,0:T(8,128)(2,1)S(1)}, u32[]{:S(2)}, u32[]{:S(2)}) collective-permute-start(bf16[8,128,128]{2,1,0:T(8,128)(2,1)S(1)} %collective-permute-done.24.refs_0_), channel_id=1, source_target_pairs={{0,8},{1,9},{2,10},{3,11},{4,12},{5,13},{6,14},{7,15},{8,0},{9,1},... | collective-permute-start | bytes 786440 | tf_op jit(solution)/shard_map/ppermute | solution.py:261
  48.8 14.9 %collective-permute-start.26 = (bf16[8,128,128]{2,1,0:T(8,128)(2,1)S(1)}, bf16[8,128,128]{2,1,0:T(8,128)(2,1)S(1)}, u32[]{:S(2)}, u32[]{:S(2)}) collective-permute-start(bf16[8,128,128]{2,1,0:T(8,128)(2,1)S(1)} %collective-permute-done.24.refs_0_), channel_id=1, source_target_pairs={{0,16},{1,17},{2,18},{3,19},{4,20},{5,21},{6,22},{7,23},{8,24},{9,... | collective-permute-start | bytes 786440 | tf_op jit(solution)/shard_map/ppermute | solution.py:261
  52.2 11.5 %collective-permute-start.20 = (bf16[8,128,128]{2,1,0:T(8,128)(2,1)S(1)}, bf16[8,128,128]{2,1,0:T(8,128)(2,1)S(1)}, u32[]{:S(2)}, u32[]{:S(2)}) collective-permute-start(bf16[8,128,128]{2,1,0:T(8,128)(2,1)S(1)} %get-tuple-element.44), channel_id=1, source_target_pairs={{0,6},{1,7},{2,4},{3,5},{4,2},{5,3},{6,0},{7,1},{8,14},{9,15},{10,... | collective-permute-start | bytes 786440 | tf_op jit(solution)/shard_map/ppermute | solution.py:261
  55.7 10.8 %collective-permute-start.21 = (bf16[8,128,128]{2,1,0:T(8,128)(2,1)S(1)}, bf16[8,128,128]{2,1,0:T(8,128)(2,1)S(1)}, u32[]{:S(2)}, u32[]{:S(2)}) collective-permute-start(bf16[8,128,128]{2,1,0:T(8,128)(2,1)S(1)} %get-tuple-element.45), channel_id=1, source_target_pairs={{0,2},{1,3},{2,0},{3,1},{4,6},{5,7},{6,4},{7,5},{8,10},{9,11},{10,... | collective-permute-start | bytes 786440 | tf_op jit(solution)/shard_map/ppermute | solution.py:261
  57.3 11.3 %collective-permute-start.22 = (bf16[8,128,128]{2,1,0:T(8,128)(2,1)S(1)}, bf16[8,128,128]{2,1,0:T(8,128)(2,1)S(1)}, u32[]{:S(2)}, u32[]{:S(2)}) collective-permute-start(bf16[8,128,128]{2,1,0:T(8,128)(2,1)S(1)} %get-tuple-element.46), channel_id=1, source_target_pairs={{0,4},{1,5},{2,6},{3,7},{4,0},{5,1},{6,2},{7,3},{8,12},{9,13},{10,... | collective-permute-start | bytes 786440 | tf_op jit(solution)/shard_map/ppermute | solution.py:261
  63.7 11.4 %collective-permute-start.27 = (bf16[8,128,128]{2,1,0:T(8,128)(2,1)S(1)}, bf16[8,128,128]{2,1,0:T(8,128)(2,1)S(1)}, u32[]{:S(2)}, u32[]{:S(2)}) collective-permute-start(bf16[8,128,128]{2,1,0:T(8,128)(2,1)S(1)} %collective-permute-done.26.refs_2_), channel_id=1, source_target_pairs={{0,8},{1,9},{2,10},{3,11},{4,12},{5,13},{6,14},{7,15},{8,0},{9,1},... | collective-permute-start | bytes 786440 | tf_op jit(solution)/shard_map/ppermute | solution.py:261
  68.7 11.0 %collective-permute-start.23 = (bf16[8,128,128]{2,1,0:T(8,128)(2,1)S(1)}, bf16[8,128,128]{2,1,0:T(8,128)(2,1)S(1)}, u32[]{:S(2)}, u32[]{:S(2)}) collective-permute-start(bf16[8,128,128]{2,1,0:T(8,128)(2,1)S(1)} %add_convert_fusion), channel_id=1, source_target_pairs={{0,0},{1,1},{2,2},{3,3},{4,4},{5,5},{6,6},{7,7},{8,10},{9,11},{10,... | collective-permute-start | bytes 786440 | tf_op jit(solution)/shard_map/ppermute | solution.py:261
  84.5 10.8 %collective-permute-start.34 = (bf16[1040,128]{1,0:T(8,128)(2,1)S(1)}, bf16[1040,128]{1,0:T(8,128)(2,1)S(1)}, u32[]{:S(2)}, u32[]{:S(2)}) collective-permute-start(bf16[1040,128]{1,0:T(8,128)(2,1)S(1)} %get-tuple-element.55), channel_id=1, source_target_pairs={{0,6},{1,7},{2,4},{3,5},{4,2},{5,3},{6,0},{7,1},{8,14},{9,15},{10,... | collective-permute-start | bytes 798728 | tf_op jit(solution)/shard_map/ppermute | solution.py:261
  88.1 15.4 %collective-permute-start.35 = (bf16[1040,128]{1,0:T(8,128)(2,1)S(1)}, bf16[1040,128]{1,0:T(8,128)(2,1)S(1)}, u32[]{:S(2)}, u32[]{:S(2)}) collective-permute-start(bf16[1040,128]{1,0:T(8,128)(2,1)S(1)} %get-tuple-element.56), channel_id=1, source_target_pairs={{0,2},{1,3},{2,0},{3,1},{4,6},{5,7},{6,4},{7,5},{8,10},{9,11},{10,... | collective-permute-start | bytes 798728 | tf_op jit(solution)/shard_map/ppermute | solution.py:261
  91.3 12.2 %collective-permute-start.36 = (bf16[1040,128]{1,0:T(8,128)(2,1)S(1)}, bf16[1040,128]{1,0:T(8,128)(2,1)S(1)}, u32[]{:S(2)}, u32[]{:S(2)}) collective-permute-start(bf16[1040,128]{1,0:T(8,128)(2,1)S(1)} %get-tuple-element.57), channel_id=1, source_target_pairs={{0,4},{1,5},{2,6},{3,7},{4,0},{5,1},{6,2},{7,3},{8,12},{9,13},{10,... | collective-permute-start | bytes 798728 | tf_op jit(solution)/shard_map/ppermute | solution.py:261
  103.8 12.2 %collective-permute-start.37 = (bf16[1040,128]{1,0:T(8,128)(2,1)S(1)}, bf16[1040,128]{1,0:T(8,128)(2,1)S(1)}, u32[]{:S(2)}, u32[]{:S(2)}) collective-permute-start(bf16[1040,128]{1,0:T(8,128)(2,1)S(1)} %plane_sum.1.own_ref), channel_id=1, source_target_pairs={{0,0},{1,1},{2,20},{3,21},{4,10},{5,11},{6,30},{7,31},{8,16},{9,17... | collective-permute-start | bytes 798728 | tf_op jit(solution)/shard_map/ppermute | solution.py:261
  118.4 12.6 %collective-permute-start.39 = (bf16[8,128,128]{2,1,0:T(8,128)(2,1)S(1)}, bf16[8,128,128]{2,1,0:T(8,128)(2,1)S(1)}, u32[]{:S(2)}, u32[]{:S(2)}) collective-permute-start(bf16[8,128,128]{2,1,0:T(8,128)(2,1)S(1)} %commutator_difference.1), channel_id=1, source_target_pairs={{0,0},{1,4},{2,2},{3,6},{4,1},{5,5},{6,3},{7,7},{8,10},{9,14},{10,... | collective-permute-start | bytes 786440 | tf_op jit(solution)/shard_map/ppermute | solution.py:261
  (21 other events, 107.2 us)
